TPU v7x, 1024 devices: a whole 4x8x16 slice. The times are simulated.
1024 devices in a mesh: outer: 32 (over x, y_hi, core), inner: 32 (over y_lo, z).
Axes of the slice: x: 4, y: 8 (y_hi: 4, y_lo: 2; y = y_hi * 2 + y_lo), z: 16, core: 2. Of those that a mesh axis runs over, the one named last changes fastest.
Arguments:
- image_embed: bfloat16 [16384, 1152], P(('outer', 'inner')), may hold values from -1 to 1, as said below
- text_embed: bfloat16 [16384, 1152], P(('outer', 'inner')), may hold values from -1 to 1, as said below
- labels: int32 [16384], P(('outer', 'inner')), may hold values from 0 to 8191
- log_temp: float32 [1], replicated, may hold values from 0.5 to 1.5
- bias: float32 [1], replicated, may hold values from -2 to 0
Outputs:
- grad_image: float32 [16384, 1152], P(('outer', 'inner'))
- grad_text: float32 [16384, 1152], P(('outer', 'inner'))
- row_loss: float32 [16384], P(('outer', 'inner'))
Inputs may be any that keep to these rules, and one draw needn't show every extreme that they name: `image_embed`: embedding rows of varied length. `text_embed`: embedding rows of varied length.
All inputs are finite; a program needn't handle non-finite values.
Results may differ from a plain program's by a relative error of at most 0.0036.
Values may be sent and summed in bfloat16 or wider, within the bound.
No kernel may reach another device: no remote copies, remote signals or barrier semaphores. Data moves between devices by JAX's collectives and lax.ppermute only.
A program may use at most 32 MiB of HBM per device.

v0:
```python
import jax
import jax.numpy as jnp
from jax import lax
from jax.sharding import PartitionSpec as P


def normalize(embed):
    values = embed.astype(jnp.float32)
    radius = jnp.sqrt(jnp.sum(values * values, axis=1, keepdims=True) + 1e-06)
    return (values / radius, radius)


def unproject(unit, radius, grad):
    return (grad - unit * jnp.sum(unit * grad, axis=1, keepdims=True)) / radius


def contract(left, right, left_dim, right_dim):
    return lax.dot_general(
        left, right, (((left_dim,), (right_dim,)), ((), ())), preferred_element_type=jnp.float32
    )


def block_terms(group_image, image_labels, group_text, text_labels, scale_now, offset):
    scores = scale_now * contract(group_image, group_text, 1, 1) + offset
    positive = image_labels[:, None] == text_labels[None, :]
    loss_part = jnp.sum(jax.nn.softplus(jnp.where(positive, -scores, scores)), axis=1)
    coeffs = (jax.nn.sigmoid(scores) - positive.astype(jnp.float32)).astype(jnp.bfloat16)
    return (coeffs, loss_part)


def on_device(image_embed, text_embed, labels, log_temp, bias):
    image_unit, image_radius = normalize(image_embed)
    text_unit, text_radius = normalize(text_embed)
    image_low = image_unit.astype(jnp.bfloat16)
    text_low = text_unit.astype(jnp.bfloat16)
    scale_now = jnp.exp(log_temp[0])
    offset = bias[0]
    rows_here = image_embed.shape[0]
    total = rows_here * lax.axis_size("outer") * lax.axis_size("inner")
    group_image, image_labels = (
        lax.all_gather(image_low, "inner", axis=0, tiled=True),
        lax.all_gather(labels, "inner", axis=0, tiled=True),
    )
    group_text, text_labels = (
        lax.all_gather(text_low, "outer", axis=0, tiled=True),
        lax.all_gather(labels, "outer", axis=0, tiled=True),
    )
    coeffs, loss_part = block_terms(
        group_image, image_labels, group_text, text_labels, scale_now, offset
    )
    part = coeffs
    image_sum = lax.psum_scatter(
        scale_now * contract(part, group_text, 1, 0), "inner", scatter_dimension=0, tiled=True
    )
    loss_sum = lax.psum_scatter(loss_part, "inner", scatter_dimension=0, tiled=True)
    part = coeffs
    text_sum = lax.psum_scatter(
        scale_now * contract(part, group_image, 0, 0), "outer", scatter_dimension=0, tiled=True
    )
    grad_image = unproject(image_unit, image_radius, image_sum)
    grad_text = unproject(text_unit, text_radius, text_sum)
    return (grad_image, grad_text, loss_sum / total)


def solution(mesh):
    placed = (
        P(("outer", "inner"), None),
        P(("outer", "inner"), None),
        P(("outer", "inner")),
        P(),
        P(),
    )
    return jax.shard_map(
        on_device,
        mesh=mesh,
        in_specs=placed,
        out_specs=(P(("outer", "inner"), None), P(("outer", "inner"), None), P(("outer", "inner"))),
        check_vma=False,
    )
```

profile of v0, /device:TPU:2, one launch (start us, length us, event | category | flops | bytes accessed | tf_op | source)
XLA Modules:
  0.0 497.4 jit_solution(12623114950810239558)
XLA Ops:
  7.2 0.0 all-gather.5.cloned.1.call-start
  7.2 0.9 fusion.7
  8.1 1.5 fusion.9
  9.6 0.0 all-gather.5.cloned.1.call-update
  9.6 0.0 all-gather.3.cloned.1.call-start
  9.7 0.9 fusion.6
  10.6 1.5 fusion.8
  12.0 0.0 all-gather.3.cloned.1.call-update
  12.1 0.0 reduce-scatter.5.cloned.1.call-start
  13.4 1.3 dynamic-slice.1
  15.4 1.4 fusion.12
  17.4 0.9 dynamic-update-slice
  18.2 0.8 dynamic-update-slice.1
  19.1 36.3 %all-reduce = s32[512]{0:T(512)S(1)} all-reduce(s32[512]{0:T(512)S(1)} %dynamic-update-slice), channel_id=1, replica_groups=mesh['outer'=32,'inner'=32] {'inner'}, use_global_device_ids=true, to_apply=%add | all-reduce | flops 512 | bytes 4096
  55.4 17.8 %all-reduce.1 = s32[512]{0:T(512)S(1)} all-reduce(s32[512]{0:T(512)S(1)} %dynamic-update-slice.1), channel_id=1, replica_groups=mesh['outer'=32,'inner'=32] {'outer'}, use_global_device_ids=true, to_apply=%add.1 | all-reduce | flops 512 | bytes 4096
  73.2 14.6 %all-gather.5.cloned.1.call-done = bf16[512,1152]{1,0:T(8,128)(2,1)} async-done(((bf16[16,1152]{1,0:T(8,128)(2,1)}), bf16[512,1152]{1,0:T(8,128)(2,1)}) %all-gather.5.cloned.1.call-update) | async-done | bytes 1179664 | tf_op jit(solution)/shard_map/all_gather | solution.py:45
  87.8 138.5 %all-gather.3.cloned.1.call-done = bf16[512,1152]{1,0:T(8,128)(2,1)} async-done(((bf16[16,1152]{1,0:T(8,128)(2,1)}), bf16[512,1152]{1,0:T(8,128)(2,1)}) %all-gather.3.cloned.1.call-update) | async-done | bytes 1179664 | tf_op jit(solution)/shard_map/all_gather | solution.py:41
  226.3 3.2 fusion.5
  229.6 2.5 convolution_multiply_fusion
  232.0 0.0 reduce-scatter.5.cloned.1.call-update
  232.1 0.0 reduce-scatter.3.cloned.1.call-start
  232.1 1.2 copy-done.2
  233.3 2.4 convolution_multiply_fusion.1
  235.7 0.0 reduce-scatter.3.cloned.1.call-update
  236.3 62.7 %all-reduce.2 = f32[512]{0:T(512)S(1)} all-reduce(f32[512]{0:T(512)S(1)} %get-tuple-element.5), channel_id=4, replica_groups=mesh['outer'=32,'inner'=32] {'inner'}, use_global_device_ids=true, to_apply=%region_7.8.clone | all-reduce | flops 512 | bytes 4096
  299.0 0.6 dynamic-slice_multiply_fusion
  299.6 41.7 %reduce-scatter.5.cloned.1.call-done = f32[16,1152]{1,0:T(8,128)} async-done(((f32[512,1152]{1,0:T(8,128)}), f32[16,1152]{1,0:T(8,128)}) %reduce-scatter.5.cloned.1.call-update) | async-done | bytes 73744 | tf_op jit(solution)/shard_map/reduce_scatter | solution.py:57
  341.3 1.1 multiply_reduce_fusion
  342.4 1.6 subtract_divide_fusion
  344.0 144.2 %reduce-scatter.3.cloned.1.call-done = f32[16,1152]{1,0:T(8,128)} async-done(((f32[512,1152]{1,0:T(8,128)}), f32[16,1152]{1,0:T(8,128)}) %reduce-scatter.3.cloned.1.call-update) | async-done | bytes 73744 | tf_op jit(solution)/shard_map/reduce_scatter | solution.py:52
  488.2 1.1 multiply_reduce_fusion.1
  489.3 1.6 subtract_divide_fusion.1
  (11 shorter events, 0.0 us)
Async XLA Ops:
  7.2 80.7 %all-gather.5.cloned.1.call-start = ((), (), s32[]{:S(2)}) async-start(), calls=%async_computation.3 | async-start | bytes 1216512 | tf_op jit(solution)/shard_map/all_gather | solution.py:45
  9.6 216.7 %all-gather.3.cloned.1.call-start = ((), (), s32[]{:S(2)}) async-start(), calls=%async_computation.2 | async-start | bytes 1216512 | tf_op jit(solution)/shard_map/all_gather | solution.py:41
  12.1 329.2 %reduce-scatter.5.cloned.1.call-start = ((), (), s32[]{:S(2)}) async-start(), calls=%async_computation.5 | async-start | bytes 2433024 | tf_op jit(solution)/shard_map/reduce_scatter | solution.py:57
  226.3 3.2 copy-start.3
  232.0 1.3 copy-start.2
  232.1 256.1 %reduce-scatter.3.cloned.1.call-start = ((), (), s32[]{:S(2)}) async-start(), calls=%async_computation.4 | async-start | bytes 2433024 | tf_op jit(solution)/shard_map/reduce_scatter | solution.py:52
  235.7 105.6 %copy-start = (bf16[16,1152]{1,0:T(8,128)(2,1)S(1)}, bf16[16,1152]{1,0:T(8,128)(2,1)}, u32[]{:S(2)}) copy-start(bf16[16,1152]{1,0:T(8,128)(2,1)} %param.6) | copy-start | bytes 110596
  235.7 252.5 %copy-start.1 = (bf16[16,1152]{1,0:T(8,128)(2,1)S(1)}, bf16[16,1152]{1,0:T(8,128)(2,1)}, u32[]{:S(2)}) copy-start(bf16[16,1152]{1,0:T(8,128)(2,1)} %param.5) | copy-start | bytes 110596
Sparse Core Ops, SparseCore 0:
  12.9 74.8 all-gather.4
  91.1 135.2 all-gather.2
  232.2 109.0 reduce-scatter.4
  344.9 143.2 reduce-scatter.2
where the time goes:
time: 498 us; the launch traced here: 497 us
  waiting for transfers between devices  339 us (68%)
  blocking collectives  117 us (23%)
  between operations  17 us (3%)
  other arithmetic  10.7 us (2%)
  matrix products  8.08 us (2%)
  local copies, waits for them, and re-layouts  5.58 us (1%)
    reduce_scatter x1, waiting for transfers between devices, on_device(): lax.psum_scatter(scale_now * contract(part, group_text, 1, 0), 'inner', s...  144 us
    all_gather x1, waiting for transfers between devices, on_device(): lax.all_gather(image_low, 'inner', axis=0, tiled=True)  139 us
    unnamed x3, blocking collectives  117 us
    reduce_scatter x1, waiting for transfers between devices, on_device(): lax.psum_scatter(scale_now * contract(part, group_image, 0, 0), 'outer',...  41.7 us
    all_gather x1, waiting for transfers between devices, on_device(): lax.all_gather(text_low, 'outer', axis=0, tiled=True)  14.6 us
  transfers between devices with their start and end apart: 4, of which 4 were waited for; matrix products, arithmetic and copies ran while one was open for 2% of the time, Pallas kernels for 0%

commit v1 on v0

v1 whole, which is shorter than its diff:
```python
import jax
import jax.numpy as jnp
from jax import lax
from jax.sharding import Mesh, PartitionSpec as P

AXES = ("x", "y_hi", "core", "y_lo", "z")
PLANE = ("x", "y_hi", "y_lo")
WIDTH = 1152


def normalize(embed):
    values = embed.astype(jnp.float32)
    radius = jnp.sqrt(jnp.sum(values * values, axis=1, keepdims=True) + 1e-06)
    return (values / radius, radius)


def unproject(unit, radius, grad):
    return (grad - unit * jnp.sum(unit * grad, axis=1, keepdims=True)) / radius


def contract(left, right, left_dim, right_dim):
    return lax.dot_general(
        left, right, (((left_dim,), (right_dim,)), ((), ())), preferred_element_type=jnp.float32
    )


def label_columns(labels):
    high, low = labels // 128, labels % 128
    columns = jnp.stack([high, low], axis=1).astype(jnp.bfloat16)
    return jnp.pad(columns, ((0, 0), (0, 126)))


def label_of(columns):
    part = columns[:, WIDTH : WIDTH + 2].astype(jnp.int32)
    return part[:, 0] * 128 + part[:, 1]


def spread(block, axes):
    copies = lax.axis_size(axes)
    out = jnp.broadcast_to(block[None], (copies,) + block.shape)
    return lax.all_to_all(out, axes, 0, 0, tiled=True).reshape(-1, block.shape[1])


def swap_cores(part):
    return lax.ppermute(part, "core", [(0, 1), (1, 0)])


def on_device(image_embed, text_embed, labels, log_temp, bias):
    image_unit, image_radius = normalize(image_embed)
    text_unit, text_radius = normalize(text_embed)
    marks = label_columns(labels)
    image_low = jnp.concatenate([image_unit.astype(jnp.bfloat16), marks], axis=1)
    text_low = jnp.concatenate([text_unit.astype(jnp.bfloat16), marks], axis=1)
    scale_now = jnp.exp(log_temp[0])
    offset = bias[0]
    rows_here = image_embed.shape[0]
    total = rows_here * lax.axis_size(AXES)

    mine = spread(image_low, "z")
    group_text = spread(text_low, PLANE)
    group_image = jnp.concatenate([mine, swap_cores(mine)], axis=0)

    scores = scale_now * contract(group_image[:, :WIDTH], group_text[:, :WIDTH], 1, 1) + offset
    positive = label_of(group_image)[:, None] == label_of(group_text)[None, :]
    loss_part = jnp.sum(jax.nn.softplus(jnp.where(positive, -scores, scores)), axis=1)
    coeffs = (jax.nn.sigmoid(scores) - positive.astype(jnp.float32)).astype(jnp.bfloat16)

    image_part = contract(coeffs, group_text[:, :WIDTH], 1, 0)
    text_part = contract(coeffs, group_image[:, :WIDTH], 0, 0).astype(jnp.bfloat16)
    loss_high = loss_part.astype(jnp.bfloat16)
    loss_low = (loss_part - loss_high.astype(jnp.float32)).astype(jnp.bfloat16)
    loss_cols = jnp.pad(jnp.stack([loss_high, loss_low], axis=1), ((0, 0), (0, 126))).astype(jnp.float32)
    image_part = jnp.concatenate([image_part, loss_cols], axis=1)

    half = image_part.shape[0] // 2
    other = swap_cores(image_part[half:].astype(jnp.bfloat16))
    other = other.astype(jnp.float32)
    got_loss = jnp.sum(other[:, WIDTH : WIDTH + 2], axis=1) + loss_part[:half]
    both = (image_part[:half, :WIDTH] + other[:, :WIDTH]).astype(jnp.bfloat16)
    loss_high = got_loss.astype(jnp.bfloat16)
    loss_low = (got_loss - loss_high.astype(jnp.float32)).astype(jnp.bfloat16)
    loss_cols = jnp.pad(jnp.stack([loss_high, loss_low], axis=1), ((0, 0), (0, 126)))
    both = jnp.concatenate([both, loss_cols], axis=1)
    text_terms = lax.all_to_all(text_part.reshape(-1, rows_here, WIDTH), PLANE, 0, 0, tiled=True)
    image_terms = lax.all_to_all(both.reshape(-1, rows_here, WIDTH + 128), "z", 0, 0, tiled=True)

    text_sum = scale_now * jnp.sum(text_terms.astype(jnp.float32), axis=0)
    image_sum = jnp.sum(image_terms.astype(jnp.float32), axis=0)
    row_loss = jnp.sum(image_sum[:, WIDTH : WIDTH + 2], axis=1) / total
    grad_image = unproject(image_unit, image_radius, scale_now * image_sum[:, :WIDTH])
    grad_text = unproject(text_unit, text_radius, text_sum)
    return (grad_image, grad_text, row_loss)


def solution(mesh):
    parts = Mesh(mesh.devices.reshape(4, 4, 2, 2, 16), AXES)
    placed = (P(AXES, None), P(AXES, None), P(AXES), P(), P())
    return jax.shard_map(
        on_device,
        mesh=parts,
        in_specs=placed,
        out_specs=(P(AXES, None), P(AXES, None), P(AXES)),
        check_vma=False,
    )
```

time: 498 us -> 185 us (0.37)
  the two profiles are of different devices: /device:TPU:2 before, /device:TPU:8 now
where the time goes in v1:
time: 185 us; the launch traced here: 184 us
  waiting for transfers between devices  80.6 us (44%)
  blocking collectives  55.1 us (30%)
  starting transfers between devices  29.5 us (16%)
  other arithmetic  9.17 us (5%)
  matrix products  5.98 us (3%)
  between operations  2.18 us (1%)
    all_to_all x1, blocking collectives, spread(): lax.all_to_all(out, axes, 0, 0, tiled=True).reshape(-1, block.shape[1])  55.1 us
    all_to_all x1, waiting for transfers between devices, on_device(): lax.all_to_all(both.reshape(-1, rows_here, WIDTH + 128), 'z', 0, 0, tiled...  29.8 us
    all_to_all x1, waiting for transfers between devices, spread(): lax.all_to_all(out, axes, 0, 0, tiled=True).reshape(-1, block.shape[1])  28.2 us
    all_to_all x1, waiting for transfers between devices, on_device(): lax.all_to_all(text_part.reshape(-1, rows_here, WIDTH), PLANE, 0, 0, tile...  20.6 us
    all_to_all x1, starting transfers between devices, on_device(): lax.all_to_all(both.reshape(-1, rows_here, WIDTH + 128), 'z', 0, 0, tiled...  10.4 us
    all_to_all x1, starting transfers between devices, spread(): lax.all_to_all(out, axes, 0, 0, tiled=True).reshape(-1, block.shape[1])  10.2 us
    dot_general x3, matrix products, contract(): lax.dot_general(left, right, (((left_dim,), (right_dim,)), ((), ())), pre...  5.98 us
    all_to_all x1, starting transfers between devices, on_device(): lax.all_to_all(text_part.reshape(-1, rows_here, WIDTH), PLANE, 0, 0, tile...  5.13 us
  transfers between devices with their start and end apart: 5, of which 4 were waited for; matrix products, arithmetic and copies ran while one was open for 2% of the time, Pallas kernels for 0%

profile of v1, /device:TPU:8, one launch (start us, length us, event | category | flops | bytes accessed | tf_op | source)
XLA Modules:
  0.0 184.2 jit_solution(7590154437723094520)
XLA Ops:
  0.6 0.9 fusion.19
  1.5 0.9 fusion.20
  2.4 0.7 convert_bitcast_fusion
  3.2 0.9 fusion.26
  4.2 55.1 %all_to_all.20 = bf16[16,16,1280]{2,1,0:T(8,128)(2,1)S(1)} all-to-all(bf16[16,16,1280]{2,1,0:T(8,128)(2,1)S(1)} %broadcast_in_dim.4), channel_id=1, replica_groups=mesh['x'=4,'y_hi'=4,'core'=2,'y_lo'=2,'z'=16] {'z'}, dimensions={0} | all-to-all | bytes 1310720 | tf_op jit(solution)/shard_map/all_to_all | solution.py:41
  59.3 1.1 broadcast_in_dim.5
  60.4 10.2 %all-to-all-start.1 = ((bf16[32,16,1280]{2,1,0:T(8,128)(2,1)}), bf16[32,16,1280]{2,1,0:T(8,128)(2,1)S(1)}, u32[]{:S(2)}, u32[]{:S(2)}) async-start(bf16[32,16,1280]{2,1,0:T(8,128)(2,1)} %broadcast_in_dim.5), calls=%async_computation.1 | async-start | bytes 2621440 | tf_op jit(solution)/shard_map/all_to_all | solution.py:41
  70.6 1.9 %collective-permute-start = (bf16[256,1280]{1,0:T(8,128)(2,1)S(1)}, bf16[256,1280]{1,0:T(8,128)(2,1)S(1)}, u32[]{:S(2)}, u32[]{:S(2)}) collective-permute-start(bf16[256,1280]{1,0:T(8,128)(2,1)S(1)} %bitcast.12), channel_id=1, source_target_pairs={{0,32},{32,0},{1,33},{33,1},{2,34},{34,2},{3,35},{35,3},{4,36},{36... | collective-permute-start | bytes 1966088 | tf_op jit(solution)/shard_map/ppermute | solution.py:45
  73.8 28.2 %all-to-all-done.1 = bf16[32,16,1280]{2,1,0:T(8,128)(2,1)S(1)} async-done(((bf16[32,16,1280]{2,1,0:T(8,128)(2,1)}), bf16[32,16,1280]{2,1,0:T(8,128)(2,1)S(1)}, u32[]{:S(2)}, u32[]{:S(2)}) %all-to-all-start.1) | async-done | bytes 1310752 | tf_op jit(solution)/shard_map/all_to_all | solution.py:41
  102.1 0.2 fusion.15
  102.4 0.2 fusion.16
  102.6 1.5 fusion.9
  104.2 2.4 %fusion.33 = (bf16[512,1152]{1,0:T(8,128)(2,1)S(1)}, f32[512,1152]{1,0:T(8,128)}) fusion(bf16[512,1280]{1,0:T(8,128)(2,1)S(1)} %bitcast.18, f32[512,512]{0,1:T(8,128)S(1)} %get-tuple-element.12, s32[512]{0:T(512)S(1)} %fusion.16, s32[512]{0:T(512)S(1)} %fusion.15), kind=kOutput, calls=%fused_computation.73 | convolution fusion | flops 606404608 | bytes 5771264 | tf_op jit(solution)/shard_map/dot_general | solution.py:22
  106.6 2.1 %convolution_convert_fusion = bf16[512,1152]{1,0:T(8,128)(2,1)} fusion(bf16[256,1280]{1,0:T(8,128)(2,1)S(1)} %bitcast.15, bf16[256,1280]{1,0:T(8,128)(2,1)S(1)} %copy-done.1, f32[512,512]{0,1:T(8,128)S(1)} %get-tuple-element.12, s32[512]{0:T(512)S(1)} %fusion.16, s32[512]{0:T(512)S(1)} %fusion.15), kind=kOutput, calls=%fused_computation.1 | convolution fusion | flops 608763904 | bytes 3543040 | tf_op jit(solution)/shard_map/dot_general | solution.py:22
  108.6 5.1 %all-to-all-start.3 = ((bf16[32,16,1152]{2,1,0:T(8,128)(2,1)}), bf16[32,16,1152]{2,1,0:T(8,128)(2,1)S(1)}, u32[]{:S(2)}, u32[]{:S(2)}) async-start(bf16[32,16,1152]{2,1,0:T(8,128)(2,1)} %bitcast.8), calls=%async_computation.3 | async-start | bytes 2359296 | tf_op jit(solution)/shard_map/all_to_all | solution.py:84
  113.8 0.2 copy.26
  114.0 1.9 %collective-permute-start.1 = (bf16[256,1280]{1,0:T(8,128)(2,1)S(1)}, bf16[256,1280]{1,0:T(8,128)(2,1)S(1)}, u32[]{:S(2)}, u32[]{:S(2)}) collective-permute-start(bf16[256,1280]{1,0:T(8,128)(2,1)S(1)} %fusion.13), channel_id=1, source_target_pairs={{0,32},{32,0},{1,33},{33,1},{2,34},{34,2},{3,35},{35,3},{4,36},{36... | collective-permute-start | bytes 1966088 | tf_op jit(solution)/shard_map/ppermute | solution.py:45
  116.0 2.1 %collective-permute-done.1 = bf16[256,1280]{1,0:T(8,128)(2,1)S(1)} collective-permute-done((bf16[256,1280]{1,0:T(8,128)(2,1)S(1)}, bf16[256,1280]{1,0:T(8,128)(2,1)S(1)}, u32[]{:S(2)}, u32[]{:S(2)}) %collective-permute-start.1) | collective-permute-done | bytes 655392 | tf_op jit(solution)/shard_map/ppermute | solution.py:45
  118.1 0.1 slice_reduce_fusion
  118.3 0.1 copy.27
  118.4 1.4 fusion.4
  119.8 0.9 fusion.14
  120.7 20.6 %all-to-all-done.3 = bf16[32,16,1152]{2,1,0:T(8,128)(2,1)S(1)} async-done(((bf16[32,16,1152]{2,1,0:T(8,128)(2,1)}), bf16[32,16,1152]{2,1,0:T(8,128)(2,1)S(1)}, u32[]{:S(2)}, u32[]{:S(2)}) %all-to-all-start.3) | async-done | bytes 1179680 | tf_op jit(solution)/shard_map/all_to_all | solution.py:84
  141.3 10.4 %all-to-all-start.2 = ((bf16[16,16,1280]{2,1,0:T(8,128)(2,1)}), bf16[16,16,1280]{2,1,0:T(8,128)(2,1)S(1)}, u32[]{:S(2)}, u32[]{:S(2)}) async-start(bf16[16,16,1280]{2,1,0:T(8,128)(2,1)} %bitcast.7), calls=%async_computation.2 | async-start | bytes 1310720 | tf_op jit(solution)/shard_map/all_to_all | solution.py:85
  151.6 0.2 convert_reduce_fusion
  151.8 0.2 multiply_reduce_fusion
  152.0 0.7 subtract_divide_fusion
  152.8 29.8 %all-to-all-done.2 = bf16[16,16,1280]{2,1,0:T(8,128)(2,1)S(1)} async-done(((bf16[16,16,1280]{2,1,0:T(8,128)(2,1)}), bf16[16,16,1280]{2,1,0:T(8,128)(2,1)S(1)}, u32[]{:S(2)}, u32[]{:S(2)}) %all-to-all-start.2) | async-done | bytes 655392 | tf_op jit(solution)/shard_map/all_to_all | solution.py:85
  182.6 0.1 slice_reduce_fusion.1
  182.7 0.2 multiply_reduce_fusion.1
  182.9 0.5 broadcast_multiply_fusion
  183.4 0.7 subtract_divide_fusion.1
  (27 shorter events, 0.5 us)
Async XLA Ops:
  60.4 41.6 %all-to-all-start.1 = ((bf16[32,16,1280]{2,1,0:T(8,128)(2,1)}), bf16[32,16,1280]{2,1,0:T(8,128)(2,1)S(1)}, u32[]{:S(2)}, u32[]{:S(2)}) async-start(bf16[32,16,1280]{2,1,0:T(8,128)(2,1)} %broadcast_in_dim.5), calls=%async_computation.1 | async-start | bytes 2621440 | tf_op jit(solution)/shard_map/all_to_all | solution.py:41
  70.6 31.7 %collective-permute-start = (bf16[256,1280]{1,0:T(8,128)(2,1)S(1)}, bf16[256,1280]{1,0:T(8,128)(2,1)S(1)}, u32[]{:S(2)}, u32[]{:S(2)}) collective-permute-start(bf16[256,1280]{1,0:T(8,128)(2,1)S(1)} %bitcast.12), channel_id=1, source_target_pairs={{0,32},{32,0},{1,33},{33,1},{2,34},{34,2},{3,35},{35,3},{4,36},{36... | collective-permute-start | bytes 1966088 | tf_op jit(solution)/shard_map/ppermute | solution.py:45
  102.3 1.8 copy-start
  104.1 2.4 %copy-start.1 = (bf16[256,1280]{1,0:T(8,128)(2,1)S(1)}, bf16[256,1280]{1,0:T(8,128)(2,1)}, u32[]{:S(2)}) copy-start(bf16[256,1280]{1,0:T(8,128)(2,1)} %copy-done) | copy-start | bytes 1966084
  108.6 32.7 %all-to-all-start.3 = ((bf16[32,16,1152]{2,1,0:T(8,128)(2,1)}), bf16[32,16,1152]{2,1,0:T(8,128)(2,1)S(1)}, u32[]{:S(2)}, u32[]{:S(2)}) async-start(bf16[32,16,1152]{2,1,0:T(8,128)(2,1)} %bitcast.8), calls=%async_computation.3 | async-start | bytes 2359296 | tf_op jit(solution)/shard_map/all_to_all | solution.py:84
  114.0 4.0 %collective-permute-start.1 = (bf16[256,1280]{1,0:T(8,128)(2,1)S(1)}, bf16[256,1280]{1,0:T(8,128)(2,1)S(1)}, u32[]{:S(2)}, u32[]{:S(2)}) collective-permute-start(bf16[256,1280]{1,0:T(8,128)(2,1)S(1)} %fusion.13), channel_id=1, source_target_pairs={{0,32},{32,0},{1,33},{33,1},{2,34},{34,2},{3,35},{35,3},{4,36},{36... | collective-permute-start | bytes 1966088 | tf_op jit(solution)/shard_map/ppermute | solution.py:45
  120.7 31.1 %copy-start.2 = (bf16[16,1152]{1,0:T(8,128)(2,1)S(1)}, bf16[16,1152]{1,0:T(8,128)(2,1)}, u32[]{:S(2)}) copy-start(bf16[16,1152]{1,0:T(8,128)(2,1)} %param.6) | copy-start | bytes 110596
  141.3 41.2 %all-to-all-start.2 = ((bf16[16,16,1280]{2,1,0:T(8,128)(2,1)}), bf16[16,16,1280]{2,1,0:T(8,128)(2,1)S(1)}, u32[]{:S(2)}, u32[]{:S(2)}) async-start(bf16[16,16,1280]{2,1,0:T(8,128)(2,1)} %bitcast.7), calls=%async_computation.2 | async-start | bytes 1310720 | tf_op jit(solution)/shard_map/all_to_all | solution.py:85
  151.6 31.1 %copy-start.3 = (bf16[16,1152]{1,0:T(8,128)(2,1)S(1)}, bf16[16,1152]{1,0:T(8,128)(2,1)}, u32[]{:S(2)}) copy-start(bf16[16,1152]{1,0:T(8,128)(2,1)} %param.5) | copy-start | bytes 110596

commit v2 on v1

v2 whole, which is shorter than its diff:
```python
import functools

import jax
import jax.numpy as jnp
from jax import lax
from jax.experimental import pallas as pl
from jax.experimental.pallas import tpu as pltpu
from jax.sharding import Mesh, PartitionSpec as P

AXES = ("x", "y_hi", "core", "y_lo", "z_hi", "z_lo")
PLANE = ("x", "y_hi", "y_lo")
COLUMN = ("z_hi", "z_lo")
WIDTH = 1152
WIDE = WIDTH + 128
ROWS = 16
LABEL_BASE = 128
F32, BF16 = jnp.float32, jnp.bfloat16

VMEM = pl.BlockSpec(memory_space=pltpu.VMEM)
SMEM = pl.BlockSpec(memory_space=pltpu.SMEM)


def call(kernel, out_shape, in_specs, flops=0, bytes_accessed=0):
    many = isinstance(out_shape, (list, tuple))
    return pl.pallas_call(
        kernel,
        out_shape=out_shape,
        in_specs=in_specs,
        out_specs=[VMEM] * len(out_shape) if many else VMEM,
        compiler_params=pltpu.CompilerParams(vmem_limit_bytes=20 * 1024 * 1024),
        cost_estimate=pl.CostEstimate(
            flops=flops, bytes_accessed=bytes_accessed, transcendentals=0
        ),
    )


def unit_of(embed):
    values = embed.astype(F32)
    radius = jnp.sqrt(jnp.sum(values * values, axis=1, keepdims=True) + 1e-06)
    return values / radius, radius


def prepare(labels_ref, image_ref, text_ref, image_out, text_out):
    shape = (ROWS, 128)
    row = lax.broadcasted_iota(jnp.int32, shape, 0)
    lane = lax.broadcasted_iota(jnp.int32, shape, 1)
    label = jnp.zeros(shape, jnp.int32)
    for r in range(ROWS):
        label = jnp.where(row == r, labels_ref[r], label)
    high, low = label >> 7, label & (LABEL_BASE - 1)
    norm = high * high + low * low
    norm_high, norm_low = norm >> 7, norm & (LABEL_BASE - 1)

    def features(values):
        out = jnp.zeros(shape, jnp.int32)
        for k, value in enumerate(values):
            out = jnp.where(lane == k, value, out)
        return out.astype(F32).astype(BF16)

    image_out[:, :WIDTH] = unit_of(image_ref[...])[0].astype(BF16)
    image_out[:, WIDTH:] = features((-2 * high, -2 * low, norm_high, norm_low, LABEL_BASE, 1))
    text_low = unit_of(text_ref[...])[0].astype(BF16)
    marks = features((high, low, LABEL_BASE, 1, norm_high, norm_low))
    for k in range(text_out.shape[0]):
        text_out[k, :, :WIDTH] = text_low
        text_out[k, :, WIDTH:] = marks


def dot(left, right, left_dim, right_dim):
    return lax.dot_general(
        left, right, (((left_dim,), (right_dim,)), ((), ())), preferred_element_type=F32
    )


def loss_pair(loss):
    lane = lax.broadcasted_iota(jnp.int32, (loss.shape[0], 128), 1)
    high = loss.astype(BF16).astype(F32)
    return jnp.where(lane == 0, high, jnp.where(lane == 1, loss - high, 0.0)).astype(BF16)


def tile(log_temp_ref, bias_ref, mine_ref, other_ref, text_ref, keep_out, give_out, text_out):
    scale = jnp.exp(jnp.full((1, 1), log_temp_ref[0], F32))
    bias = bias_ref[0]
    text = text_ref[:, :WIDTH]
    marks = text_ref[:, WIDTH:]
    total = None
    for half, image_ref in enumerate((mine_ref, other_ref)):
        image = image_ref[:, :WIDTH]
        scores = scale * dot(image, text, 1, 1) + bias
        positive = dot(image_ref[:, WIDTH:], marks, 1, 1) == 0.0
        small = jnp.exp(-jnp.abs(scores))
        losses = jnp.maximum(jnp.where(positive, -scores, scores), 0.0) + jnp.log1p(small)
        loss = jnp.sum(losses, axis=1, keepdims=True)
        sigmoid = jnp.where(scores >= 0.0, 1.0, small) / (1.0 + small)
        coeffs = (sigmoid - jnp.where(positive, 1.0, 0.0)).astype(BF16)
        part = dot(coeffs, text, 1, 0)
        if half == 0:
            lane = lax.broadcasted_iota(jnp.int32, (loss.shape[0], 128), 1)
            keep_out[:, :WIDTH] = part
            keep_out[:, WIDTH:] = jnp.where(lane == 0, loss, 0.0)
        else:
            give_out[:, :WIDTH] = part.astype(BF16)
            give_out[:, WIDTH:] = loss_pair(loss)
        back = dot(coeffs, image, 0, 0)
        total = back if total is None else total + back
    text_out[...] = total.astype(BF16)


def merged(keep_ref, got_ref, rows):
    body = keep_ref[rows, :WIDTH] + got_ref[rows, :WIDTH].astype(F32)
    loss = jnp.sum(
        keep_ref[rows, WIDTH:] + got_ref[rows, WIDTH:].astype(F32), axis=1, keepdims=True
    )
    return body, loss


def fold(side_ref, keep_ref, got_ref, keep_out, *give_outs):
    side = side_ref[0]
    size = len(give_outs) + 1
    lane = lax.broadcasted_iota(jnp.int32, (ROWS, 128), 1)
    for group in range(keep_out.shape[0] // ROWS):
        out = pl.ds(group * ROWS, ROWS)
        for shift in range(size):
            place = lax.rem(side + shift, size)
            body, loss = merged(keep_ref, got_ref, pl.ds((size * group + place) * ROWS, ROWS))
            if shift == 0:
                keep_out[out, :WIDTH] = body
                keep_out[out, WIDTH:] = jnp.where(lane == 0, loss, 0.0)
            else:
                give_outs[shift - 1][out, :WIDTH] = body.astype(BF16)
                give_outs[shift - 1][out, WIDTH:] = loss_pair(loss)


def last_fold(keep_ref, *refs):
    got_refs, out_ref = refs[:-2], refs[-1]
    for block in range(out_ref.shape[0]):
        rows = pl.ds(block * ROWS, ROWS)
        terms = keep_ref[rows, :]
        for got_ref in got_refs:
            terms += got_ref[rows, :].astype(F32)
        out_ref[block, :, :WIDTH] = terms[:, :WIDTH].astype(BF16)
        out_ref[block, :, WIDTH:] = loss_pair(jnp.sum(terms[:, WIDTH:], axis=1, keepdims=True))


def unproject(log_temp_ref, embed_ref, terms):
    scale = jnp.exp(jnp.full((1, 1), log_temp_ref[0], F32))
    unit, radius = unit_of(embed_ref[...])
    grad = scale * terms
    return (grad - unit * jnp.sum(unit * grad, axis=1, keepdims=True)) / radius


def finish_text(log_temp_ref, embed_ref, terms_ref, grad_out):
    terms = terms_ref[0].astype(F32)
    for k in range(1, terms_ref.shape[0]):
        terms += terms_ref[k].astype(F32)
    grad_out[...] = unproject(log_temp_ref, embed_ref, terms)


def finish_image(total, log_temp_ref, embed_ref, terms_ref, grad_out, loss_out):
    terms = terms_ref[0].astype(F32)
    for k in range(1, terms_ref.shape[0]):
        terms += terms_ref[k].astype(F32)
    grad_out[...] = unproject(log_temp_ref, embed_ref, terms[:, :WIDTH])
    loss = jnp.sum(terms[:, WIDTH:], axis=1, keepdims=True) / total
    row = lax.broadcasted_iota(jnp.int32, (ROWS, 128), 0)
    lane = lax.broadcasted_iota(jnp.int32, (ROWS, 128), 1)
    loss_out[...] = jnp.sum(jnp.where(row == lane, loss, 0.0), axis=0, keepdims=True)[:, :ROWS]


def swap_cores(part):
    return lax.ppermute(part, "core", [(0, 1), (1, 0)])


def on_device(image_embed, text_embed, labels, log_temp, bias):
    total = ROWS * lax.axis_size(AXES)
    plane, column = lax.axis_size(PLANE), lax.axis_size(COLUMN)
    shape = jax.ShapeDtypeStruct

    image_wide, text_wide = call(
        prepare,
        [shape((ROWS, WIDE), BF16), shape((plane, ROWS, WIDE), BF16)],
        [SMEM, VMEM, VMEM],
        bytes_accessed=plane * ROWS * WIDE * 2,
    )(labels, image_embed, text_embed)

    group_text = lax.all_to_all(text_wide, PLANE, 0, 0, tiled=True).reshape(-1, WIDE)
    mine = lax.all_gather(image_wide, COLUMN, axis=0, tiled=True)
    other = swap_cores(mine)

    half, texts = column * ROWS, plane * ROWS
    keep, give, text_part = call(
        tile,
        [shape((half, WIDE), F32), shape((half, WIDE), BF16), shape((texts, WIDTH), BF16)],
        [SMEM, SMEM, VMEM, VMEM, VMEM],
        flops=12 * half * texts * WIDTH,
        bytes_accessed=8 * texts * WIDE,
    )(log_temp, bias, mine, other, group_text)

    text_terms = lax.all_to_all(text_part.reshape(plane, ROWS, WIDTH), PLANE, 0, 0, tiled=True)

    got = swap_cores(give)
    side = lax.axis_index("z_lo").astype(jnp.int32).reshape(1)
    size, blocks = lax.axis_size("z_lo"), lax.axis_size("z_hi")
    rows = blocks * ROWS
    keep, *gives = call(
        fold,
        [shape((rows, WIDE), F32)] + [shape((rows, WIDE), BF16)] * (size - 1),
        [SMEM, VMEM, VMEM],
        bytes_accessed=32 * rows * WIDE,
    )(side, keep, got)
    gots = [
        lax.ppermute(give, "z_lo", [(i, (i + shift) % size) for i in range(size)])
        for shift, give in enumerate(gives, 1)
    ]
    image_terms = call(
        last_fold,
        shape((blocks, ROWS, WIDE), BF16),
        [VMEM] * size + [pl.BlockSpec(memory_space=pl.ANY)],
        bytes_accessed=12 * rows * WIDE,
    )(keep, *gots, text_terms)
    image_terms = lax.all_to_all(image_terms, "z_hi", 0, 0, tiled=True)

    grad_text = call(
        finish_text, shape((ROWS, WIDTH), F32), [SMEM, VMEM, VMEM], bytes_accessed=2 * texts * WIDTH
    )(log_temp, text_embed, text_terms)
    grad_image, loss = call(
        functools.partial(finish_image, total),
        [shape((ROWS, WIDTH), F32), shape((1, ROWS), F32)],
        [SMEM, VMEM, VMEM],
        bytes_accessed=2 * blocks * ROWS * WIDE,
    )(log_temp, image_embed, image_terms)
    return (grad_image, grad_text, loss.reshape(ROWS))


def solution(mesh):
    parts = Mesh(mesh.devices.reshape(4, 4, 2, 2, 4, 4), AXES)
    placed = (P(AXES, None), P(AXES, None), P(AXES), P(), P())
    return jax.shard_map(
        on_device,
        mesh=parts,
        in_specs=placed,
        out_specs=(P(AXES, None), P(AXES, None), P(AXES)),
        check_vma=False,
    )
```

time: 185 us -> 134 us (0.72)
  waiting for transfers between devices: 80.6 us -> 34.1 us
  blocking collectives: 55.1 us -> 39.5 us
  starting transfers between devices: 29.5 us -> 44 us
  other arithmetic: 9.17 us -> 0 us
  Pallas kernels: 0 us -> 7.37 us
  matrix products: 5.98 us -> 0 us
  local copies, waits for them, and re-layouts: 1.64 us -> 6.45 us
    all_to_all x3, waiting for transfers between devices: 78.6 us -> 23 us  [the longest x1 13.8 us: on_device(): image_terms = lax.all_to_all(image_terms, 'z_hi', 0, 0, tiled=True)]
    all_to_all x1 -> x0, blocking collectives: 55.1 us -> none  [spread(): lax.all_to_all(out, axes, 0, 0, tiled=True).reshape(-1, block.shape[1])]
    all_gather x0 -> x1, blocking collectives: none -> 39.5 us  [on_device(): mine = lax.all_gather(image_wide, COLUMN, axis=0, tiled=True)]
    ppermute x0 -> x3, starting transfers between devices: none -> 9.69 us  [on_device(): lax.ppermute(give, 'z_lo', [(i, (i + shift) % size) for i in range(size)])]
    ppermute x0 -> x3, waiting for transfers between devices: none -> 8.03 us  [on_device(): lax.ppermute(give, 'z_lo', [(i, (i + shift) % size) for i in range(size)])]
    pallas_call x0 -> x6, Pallas kernels: none -> 7.37 us  [the longest x1 2.9 us: on_device(): call(tile, [shape((half, WIDE), F32), shape((half, WIDE), BF16), shape((t...]
    unnamed x9 -> x18, local copies, waits for them, and re-layouts: 0.12 us -> 6.45 us
    dot_general x3 -> x0, matrix products: 5.98 us -> none  [contract(): lax.dot_general(left, right, (((left_dim,), (right_dim,)), ((), ())), pre...]
  transfers between devices with their start and end apart: 5 -> 8, of which waited for: 4 -> 7; matrix products, arithmetic and copies ran while one was open for 2% -> 0% of each run, Pallas kernels for 0% -> 1%
where the time goes in v2:
time: 134 us; the launch traced here: 133 us
  starting transfers between devices  44 us (33%)
  blocking collectives  39.5 us (29%)
  waiting for transfers between devices  34.1 us (25%)
  Pallas kernels  7.37 us (6%)
  local copies, waits for them, and re-layouts  6.45 us (5%)
  between operations  2.03 us (2%)
    all_gather x1, blocking collectives, on_device(): mine = lax.all_gather(image_wide, COLUMN, axis=0, tiled=True)  39.5 us
    all_to_all x1, starting transfers between devices, on_device(): lax.all_to_all(text_wide, PLANE, 0, 0, tiled=True).reshape(-1, WIDE)  16.7 us
    all_to_all x1, waiting for transfers between devices, on_device(): image_terms = lax.all_to_all(image_terms, 'z_hi', 0, 0, tiled=True)  13.8 us
    all_to_all x1, starting transfers between devices, on_device(): lax.all_to_all(text_part.reshape(plane, ROWS, WIDTH), PLANE, 0, 0, tiled=...  9.78 us
    ppermute x3, starting transfers between devices, on_device(): lax.ppermute(give, 'z_lo', [(i, (i + shift) % size) for i in range(size)])  9.69 us
    all_to_all x1, waiting for transfers between devices, on_device(): lax.all_to_all(text_part.reshape(plane, ROWS, WIDTH), PLANE, 0, 0, tiled=...  9.2 us
    ppermute x3, waiting for transfers between devices, on_device(): lax.ppermute(give, 'z_lo', [(i, (i + shift) % size) for i in range(size)])  8.03 us
    unnamed x18, local copies, waits for them, and re-layouts  6.45 us
  transfers between devices with their start and end apart: 8, of which 7 were waited for; matrix products, arithmetic and copies ran while one was open for 0% of the time, Pallas kernels for 1%

profile of v2, /device:TPU:8, one launch (start us, length us, event | category | flops | bytes accessed | tf_op | source)
XLA Modules:
  0.0 133.4 jit_solution(11920220121943815224)
XLA Ops:
  0.6 0.0 copy-start.3
  0.6 0.8 copy-done.3
  1.4 0.8 copy-done.5
  2.2 0.7 copy-done.7
  2.8 1.8 %shard_map.76 = (bf16[16,1280]{1,0:T(8,128)(2,1)S(1)}, bf16[32,16,1280]{2,1,0:T(8,128)(2,1)}) custom-call(s32[16]{0:T(128)S(1)} %copy-done.7, bf16[16,1152]{1,0:T(8,128)(2,1)S(1)} %copy-done.5, bf16[16,1152]{1,0:T(8,128)(2,1)S(1)} %copy-done.3), custom_call_target="tpu_custom_call" | custom-call | bytes 1310720 | tf_op jit(solution)/shard_map/pallas_call | solution.py:179
  4.6 16.7 %all-to-all-start = ((bf16[32,16,1280]{2,1,0:T(8,128)(2,1)}), bf16[32,16,1280]{2,1,0:T(8,128)(2,1)S(1)}, u32[]{:S(2)}, u32[]{:S(2)}) async-start(bf16[32,16,1280]{2,1,0:T(8,128)(2,1)} %get-tuple-element.15), calls=%async_computation | async-start | bytes 2621440 | tf_op jit(solution)/shard_map/all_to_all | solution.py:186
  21.3 39.5 %all_gather.3.mine_ref = bf16[256,1280]{1,0:T(8,128)(2,1)S(1)} all-gather(bf16[16,1280]{1,0:T(8,128)(2,1)S(1)} %get-tuple-element.14), channel_id=1, replica_groups=mesh['x'=4,'y_hi'=4,'core'=2,'y_lo'=2,'z_hi'=4,'z_lo'=4] {'z_hi','z_lo'}, dimensions={0}, use_global_device_ids=true | all-gather | bytes 696320 | tf_op jit(solution)/shard_map/all_gather | solution.py:187
  60.8 1.9 %collective-permute-start = (bf16[256,1280]{1,0:T(8,128)(2,1)S(1)}, bf16[256,1280]{1,0:T(8,128)(2,1)S(1)}, u32[]{:S(2)}, u32[]{:S(2)}) collective-permute-start(bf16[256,1280]{1,0:T(8,128)(2,1)S(1)} %all_gather.3.mine_ref), channel_id=1, source_target_pairs={{0,32},{32,0},{1,33},{33,1},{2,34},{34,2},{3,35},{35,3},{4,36},{36... | collective-permute-start | bytes 1966088 | tf_op jit(solution)/shard_map/ppermute | solution.py:171
  64.0 0.8 collective-permute-done.other_ref
  64.8 0.0 all-to-all-done
  64.8 1.1 copy-done
  65.9 1.3 copy-done.1
  67.2 2.9 %shard_map.77 = (f32[256,1280]{1,0:T(8,128)S(1)}, bf16[256,1280]{1,0:T(8,128)(2,1)S(1)}, bf16[512,1152]{1,0:T(8,128)(2,1)S(1)}) custom-call(f32[1]{0:T(128)S(6)} %copy.8.log_temp_ref, f32[1]{0:T(128)S(6)} %copy.9.bias_ref, bf16[256,1280]{1,0:T(8,128)(2,1)S(1)} %all_gather.3.mine_ref, bf16[256,1280]{1,0:T(8,128)(2,1)S(1)} %collective-permute-done.other_ref, ...), custom_call_target="tpu_custom_call" | custom-call | flops 1811939328 | bytes 5242880 | tf_op jit(solution)/shard_map/pallas_call | solution.py:191
  70.1 0.0 copy-start.2
  70.1 1.0 copy-done.2
  71.1 0.8 copy-done.8
  72.0 9.8 %all-to-all-start.1 = ((bf16[32,16,1152]{2,1,0:T(8,128)(2,1)}), bf16[32,16,1152]{2,1,0:T(8,128)(2,1)S(1)}, u32[]{:S(2)}, u32[]{:S(2)}) async-start(bf16[32,16,1152]{2,1,0:T(8,128)(2,1)} %bitcast.5), calls=%async_computation.1 | async-start | bytes 2359296 | tf_op jit(solution)/shard_map/all_to_all | solution.py:199
  81.8 1.9 %collective-permute-start.1 = (bf16[256,1280]{1,0:T(8,128)(2,1)}, bf16[256,1280]{1,0:T(8,128)(2,1)S(1)}, u32[]{:S(2)}, u32[]{:S(2)}) collective-permute-start(bf16[256,1280]{1,0:T(8,128)(2,1)} %copy-done.8), channel_id=1, source_target_pairs={{0,32},{32,0},{1,33},{33,1},{2,34},{34,2},{3,35},{35,3},{4,36},{36... | collective-permute-start | bytes 1966088 | tf_op jit(solution)/shard_map/ppermute | solution.py:171
  83.7 2.3 %collective-permute-done.1.got_ref = bf16[256,1280]{1,0:T(8,128)(2,1)S(1)} collective-permute-done((bf16[256,1280]{1,0:T(8,128)(2,1)}, bf16[256,1280]{1,0:T(8,128)(2,1)S(1)}, u32[]{:S(2)}, u32[]{:S(2)}) %collective-permute-start.1) | collective-permute-done | bytes 655392 | tf_op jit(solution)/shard_map/ppermute | solution.py:171
  86.0 0.2 shard_map.78
  86.2 2.1 %collective-permute-start.2 = (bf16[64,1280]{1,0:T(8,128)(2,1)S(1)}, bf16[64,1280]{1,0:T(8,128)(2,1)S(1)}, u32[]{:S(2)}, u32[]{:S(2)}) collective-permute-start(bf16[64,1280]{1,0:T(8,128)(2,1)S(1)} %get-tuple-element.19), channel_id=1, source_target_pairs={{0,1},{1,2},{2,3},{3,0},{4,5},{5,6},{6,7},{7,4},{8,9},{9,10},{10,1... | collective-permute-start | bytes 491528 | tf_op jit(solution)/shard_map/ppermute | solution.py:212
  88.2 2.2 %collective-permute-start.3 = (bf16[64,1280]{1,0:T(8,128)(2,1)S(1)}, bf16[64,1280]{1,0:T(8,128)(2,1)S(1)}, u32[]{:S(2)}, u32[]{:S(2)}) collective-permute-start(bf16[64,1280]{1,0:T(8,128)(2,1)S(1)} %get-tuple-element.20), channel_id=1, source_target_pairs={{0,2},{1,3},{2,0},{3,1},{4,6},{5,7},{6,4},{7,5},{8,10},{9,11},{10,... | collective-permute-start | bytes 491528 | tf_op jit(solution)/shard_map/ppermute | solution.py:212
  90.4 5.5 %collective-permute-start.4 = (bf16[64,1280]{1,0:T(8,128)(2,1)S(1)}, bf16[64,1280]{1,0:T(8,128)(2,1)S(1)}, u32[]{:S(2)}, u32[]{:S(2)}) collective-permute-start(bf16[64,1280]{1,0:T(8,128)(2,1)S(1)} %get-tuple-element.21), channel_id=1, source_target_pairs={{0,3},{1,0},{2,1},{3,2},{4,7},{5,4},{6,5},{7,6},{8,11},{9,8},{10,9... | collective-permute-start | bytes 491528 | tf_op jit(solution)/shard_map/ppermute | solution.py:212
  95.9 1.3 collective-permute-done.2.refs_0_
  97.1 6.2 %collective-permute-done.3.refs_1_ = bf16[64,1280]{1,0:T(8,128)(2,1)S(1)} collective-permute-done((bf16[64,1280]{1,0:T(8,128)(2,1)S(1)}, bf16[64,1280]{1,0:T(8,128)(2,1)S(1)}, u32[]{:S(2)}, u32[]{:S(2)}) %collective-permute-start.3) | collective-permute-done | bytes 163872 | tf_op jit(solution)/shard_map/ppermute | solution.py:212
  103.4 0.5 collective-permute-done.4.refs_2_
  103.9 9.2 %all-to-all-done.1.refs_3_.terms_ref = bf16[32,16,1152]{2,1,0:T(8,128)(2,1)S(1)} async-done(((bf16[32,16,1152]{2,1,0:T(8,128)(2,1)}), bf16[32,16,1152]{2,1,0:T(8,128)(2,1)S(1)}, u32[]{:S(2)}, u32[]{:S(2)}) %all-to-all-start.1) | async-done | bytes 1179680 | tf_op jit(solution)/shard_map/all_to_all | solution.py:199
  113.1 0.8 shard_map.79
  113.9 4.0 %all-to-all-start.2 = ((bf16[4,16,1280]{2,1,0:T(8,128)(2,1)}), bf16[4,16,1280]{2,1,0:T(8,128)(2,1)S(1)}, u32[]{:S(2)}, u32[]{:S(2)}) async-start(bf16[4,16,1280]{2,1,0:T(8,128)(2,1)} %shard_map.79), calls=%async_computation.2 | async-start | bytes 327680 | tf_op jit(solution)/shard_map/all_to_all | solution.py:221
  117.9 0.9 shard_map.81
  118.8 13.8 %all-to-all-done.2.terms_ref = bf16[4,16,1280]{2,1,0:T(8,128)(2,1)S(1)} async-done(((bf16[4,16,1280]{2,1,0:T(8,128)(2,1)}), bf16[4,16,1280]{2,1,0:T(8,128)(2,1)S(1)}, u32[]{:S(2)}, u32[]{:S(2)}) %all-to-all-start.2) | async-done | bytes 163872 | tf_op jit(solution)/shard_map/all_to_all | solution.py:221
  132.6 0.8 shard_map.80
  (9 shorter events, 0.0 us)
Async XLA Ops:
  0.6 0.8 copy-start.3
  1.4 0.8 copy-start.5
  2.2 0.7 copy-start.7
  4.6 60.2 %all-to-all-start = ((bf16[32,16,1280]{2,1,0:T(8,128)(2,1)}), bf16[32,16,1280]{2,1,0:T(8,128)(2,1)S(1)}, u32[]{:S(2)}, u32[]{:S(2)}) async-start(bf16[32,16,1280]{2,1,0:T(8,128)(2,1)} %get-tuple-element.15), calls=%async_computation | async-start | bytes 2621440 | tf_op jit(solution)/shard_map/all_to_all | solution.py:186
  60.8 4.0 %collective-permute-start = (bf16[256,1280]{1,0:T(8,128)(2,1)S(1)}, bf16[256,1280]{1,0:T(8,128)(2,1)S(1)}, u32[]{:S(2)}, u32[]{:S(2)}) collective-permute-start(bf16[256,1280]{1,0:T(8,128)(2,1)S(1)} %all_gather.3.mine_ref), channel_id=1, source_target_pairs={{0,32},{32,0},{1,33},{33,1},{2,34},{34,2},{3,35},{35,3},{4,36},{36... | collective-permute-start | bytes 1966088 | tf_op jit(solution)/shard_map/ppermute | solution.py:171
  64.8 1.1 copy-start
  65.9 1.3 copy-start.1
  70.1 1.0 copy-start.2
  71.1 0.8 copy-start.8
  72.0 41.1 %all-to-all-start.1 = ((bf16[32,16,1152]{2,1,0:T(8,128)(2,1)}), bf16[32,16,1152]{2,1,0:T(8,128)(2,1)S(1)}, u32[]{:S(2)}, u32[]{:S(2)}) async-start(bf16[32,16,1152]{2,1,0:T(8,128)(2,1)} %bitcast.5), calls=%async_computation.1 | async-start | bytes 2359296 | tf_op jit(solution)/shard_map/all_to_all | solution.py:199
  81.8 4.2 %collective-permute-start.1 = (bf16[256,1280]{1,0:T(8,128)(2,1)}, bf16[256,1280]{1,0:T(8,128)(2,1)S(1)}, u32[]{:S(2)}, u32[]{:S(2)}) collective-permute-start(bf16[256,1280]{1,0:T(8,128)(2,1)} %copy-done.8), channel_id=1, source_target_pairs={{0,32},{32,0},{1,33},{33,1},{2,34},{34,2},{3,35},{35,3},{4,36},{36... | collective-permute-start | bytes 1966088 | tf_op jit(solution)/shard_map/ppermute | solution.py:171
  86.2 31.7 %copy-start.4 = (bf16[16,1152]{1,0:T(8,128)(2,1)S(1)}, bf16[16,1152]{1,0:T(8,128)(2,1)}, u32[]{:S(2)}) copy-start(bf16[16,1152]{1,0:T(8,128)(2,1)} %embed_ref.3) | copy-start | bytes 110596
  86.2 11.0 %collective-permute-start.2 = (bf16[64,1280]{1,0:T(8,128)(2,1)S(1)}, bf16[64,1280]{1,0:T(8,128)(2,1)S(1)}, u32[]{:S(2)}, u32[]{:S(2)}) collective-permute-start(bf16[64,1280]{1,0:T(8,128)(2,1)S(1)} %get-tuple-element.19), channel_id=1, source_target_pairs={{0,1},{1,2},{2,3},{3,0},{4,5},{5,6},{6,7},{7,4},{8,9},{9,10},{10,1... | collective-permute-start | bytes 491528 | tf_op jit(solution)/shard_map/ppermute | solution.py:212
  88.2 15.1 %collective-permute-start.3 = (bf16[64,1280]{1,0:T(8,128)(2,1)S(1)}, bf16[64,1280]{1,0:T(8,128)(2,1)S(1)}, u32[]{:S(2)}, u32[]{:S(2)}) collective-permute-start(bf16[64,1280]{1,0:T(8,128)(2,1)S(1)} %get-tuple-element.20), channel_id=1, source_target_pairs={{0,2},{1,3},{2,0},{3,1},{4,6},{5,7},{6,4},{7,5},{8,10},{9,11},{10,... | collective-permute-start | bytes 491528 | tf_op jit(solution)/shard_map/ppermute | solution.py:212
  90.4 13.5 %collective-permute-start.4 = (bf16[64,1280]{1,0:T(8,128)(2,1)S(1)}, bf16[64,1280]{1,0:T(8,128)(2,1)S(1)}, u32[]{:S(2)}, u32[]{:S(2)}) collective-permute-start(bf16[64,1280]{1,0:T(8,128)(2,1)S(1)} %get-tuple-element.21), channel_id=1, source_target_pairs={{0,3},{1,0},{2,1},{3,2},{4,7},{5,4},{6,5},{7,6},{8,11},{9,8},{10,9... | collective-permute-start | bytes 491528 | tf_op jit(solution)/shard_map/ppermute | solution.py:212
  113.9 18.7 %copy-start.6 = (bf16[16,1152]{1,0:T(8,128)(2,1)S(1)}, bf16[16,1152]{1,0:T(8,128)(2,1)}, u32[]{:S(2)}) copy-start(bf16[16,1152]{1,0:T(8,128)(2,1)} %embed_ref.2) | copy-start | bytes 110596
  113.9 18.7 %all-to-all-start.2 = ((bf16[4,16,1280]{2,1,0:T(8,128)(2,1)}), bf16[4,16,1280]{2,1,0:T(8,128)(2,1)S(1)}, u32[]{:S(2)}, u32[]{:S(2)}) async-start(bf16[4,16,1280]{2,1,0:T(8,128)(2,1)} %shard_map.79), calls=%async_computation.2 | async-start | bytes 327680 | tf_op jit(solution)/shard_map/all_to_all | solution.py:221

commit v3 on v2

v3 whole, which is shorter than its diff:
```python
import functools

import jax
import jax.numpy as jnp
from jax import lax
from jax.experimental import pallas as pl
from jax.experimental.pallas import tpu as pltpu
from jax.sharding import Mesh, PartitionSpec as P

AXES = ("x", "y_hi", "core", "y_lo", "z_hi", "z_lo")
PLANE = ("x", "y_hi", "y_lo")
COLUMN = ("z_hi", "z_lo")
WIDTH = 1152
WIDE = WIDTH + 128
ROWS = 16
LABEL_BASE = 128
F32, BF16 = jnp.float32, jnp.bfloat16

VMEM = pl.BlockSpec(memory_space=pltpu.VMEM)
SMEM = pl.BlockSpec(memory_space=pltpu.SMEM)
HBM = pl.BlockSpec(memory_space=pltpu.HBM)


def call(kernel, outs, in_specs, scratch=(), flops=0, bytes_accessed=0, vmem=16):
    return pl.pallas_call(
        kernel,
        out_shape=[
            pltpu.HBM(shape.shape, shape.dtype) if spec is HBM else shape for spec, shape in outs
        ],
        in_specs=in_specs,
        out_specs=[spec for spec, _ in outs],
        scratch_shapes=list(scratch),
        compiler_params=pltpu.CompilerParams(vmem_limit_bytes=vmem * 1024 * 1024),
        cost_estimate=pl.CostEstimate(
            flops=flops, bytes_accessed=bytes_accessed, transcendentals=0
        ),
    )


def start(*copies):
    for copy in copies:
        copy.start()
    return copies


def wait(*copies):
    for copy in copies:
        copy.wait()


def unit_of(embed):
    values = embed.astype(F32)
    radius = jnp.sqrt(jnp.sum(values * values, axis=1, keepdims=True) + 1e-06)
    return values / radius, radius


def prepare(
    labels_ref, image_ref, text_ref, image_out, text_out, labels_now, image_now, text_now, text_wide, in_sem, out_sem
):
    labels_copy, image_copy, text_copy = start(
        pltpu.make_async_copy(labels_ref, labels_now, in_sem.at[0]),
        pltpu.make_async_copy(image_ref, image_now, in_sem.at[1]),
        pltpu.make_async_copy(text_ref, text_now, in_sem.at[2]),
    )
    wait(labels_copy)
    shape = (ROWS, 128)
    row = lax.broadcasted_iota(jnp.int32, shape, 0)
    lane = lax.broadcasted_iota(jnp.int32, shape, 1)
    label = jnp.zeros(shape, jnp.int32)
    for r in range(ROWS):
        label = jnp.where(row == r, labels_now[r], label)
    high, low = label >> 7, label & (LABEL_BASE - 1)
    norm = high * high + low * low
    norm_high, norm_low = norm >> 7, norm & (LABEL_BASE - 1)

    def features(values):
        out = jnp.zeros(shape, jnp.int32)
        for k, value in enumerate(values):
            out = jnp.where(lane == k, value, out)
        return out.astype(F32).astype(BF16)

    wait(text_copy)
    text_wide[:, :WIDTH] = unit_of(text_now[...])[0].astype(BF16)
    text_wide[:, WIDTH:] = features((high, low, LABEL_BASE, 1, norm_high, norm_low))
    copies = start(
        *[
            pltpu.make_async_copy(text_wide, text_out.at[k], out_sem.at[k])
            for k in range(text_out.shape[0])
        ]
    )
    wait(image_copy)
    image_out[:, :WIDTH] = unit_of(image_now[...])[0].astype(BF16)
    image_out[:, WIDTH:] = features((-2 * high, -2 * low, norm_high, norm_low, LABEL_BASE, 1))
    wait(*copies)


def dot(left, right, left_dim, right_dim):
    return lax.dot_general(
        left, right, (((left_dim,), (right_dim,)), ((), ())), preferred_element_type=F32
    )


def loss_pair(loss):
    lane = lax.broadcasted_iota(jnp.int32, (loss.shape[0], 128), 1)
    high = loss.astype(BF16).astype(F32)
    return jnp.where(lane == 0, high, jnp.where(lane == 1, loss - high, 0.0)).astype(BF16)


def half_tile(log_temp_ref, bias_ref, wide, text_wide):
    scale = jnp.exp(jnp.full((1, 1), log_temp_ref[0], F32))
    scores = scale * dot(wide[:, :WIDTH], text_wide[:, :WIDTH], 1, 1) + bias_ref[0]
    positive = dot(wide[:, WIDTH:], text_wide[:, WIDTH:], 1, 1) == 0.0
    small = jnp.exp(-jnp.abs(scores))
    losses = jnp.maximum(jnp.where(positive, -scores, scores), 0.0) + jnp.log1p(small)
    sigmoid = jnp.where(scores >= 0.0, 1.0, small) / (1.0 + small)
    coeffs = (sigmoid - jnp.where(positive, 1.0, 0.0)).astype(BF16)
    return jnp.sum(losses, axis=1, keepdims=True), coeffs


def first_tile(
    log_temp_ref, bias_ref, mine_ref, text_ref, coeffs_out, keep_out, mine, text, coeffs_now, keep_now, in_sem, out_sem
):
    wait(
        *start(
            pltpu.make_async_copy(mine_ref, mine, in_sem.at[0]),
            pltpu.make_async_copy(text_ref, text, in_sem.at[1]),
        )
    )
    loss, coeffs = half_tile(log_temp_ref, bias_ref, mine, text)
    coeffs_now[...] = coeffs
    (coeffs_copy,) = start(pltpu.make_async_copy(coeffs_now, coeffs_out, out_sem.at[0]))
    lane = lax.broadcasted_iota(jnp.int32, (loss.shape[0], 128), 1)
    keep_now[:, :WIDTH] = dot(coeffs, text[:, :WIDTH], 1, 0)
    keep_now[:, WIDTH:] = jnp.where(lane == 0, loss, 0.0)
    (keep_copy,) = start(pltpu.make_async_copy(keep_now, keep_out, out_sem.at[1]))
    wait(coeffs_copy, keep_copy)


def second_tile(
    order, log_temp_ref, bias_ref, other_ref, text_ref, mine_ref, coeffs_ref, give_out, text_out,
    other, text, mine, mine_coeffs, coeffs_now, give_now, text_now, in_sem, out_sem
):
    other_copy, text_copy, mine_copy, coeffs_copy = start(
        pltpu.make_async_copy(other_ref, other, in_sem.at[0]),
        pltpu.make_async_copy(text_ref, text, in_sem.at[1]),
        pltpu.make_async_copy(mine_ref, mine, in_sem.at[2]),
        pltpu.make_async_copy(coeffs_ref, mine_coeffs, in_sem.at[3]),
    )
    wait(other_copy, text_copy)
    loss, coeffs = half_tile(log_temp_ref, bias_ref, other, text)
    coeffs_now[...] = coeffs
    give_now[:, :WIDTH] = dot(coeffs, text[:, :WIDTH], 1, 0).astype(BF16)
    give_now[:, WIDTH:] = loss_pair(loss)
    copies = list(start(pltpu.make_async_copy(give_now, give_out, out_sem.at[0])))
    wait(mine_copy, coeffs_copy)
    chunk = 8
    for first in range(0, len(order), chunk):
        columns = pl.ds(first * ROWS, chunk * ROWS)
        total = dot(mine_coeffs[:, columns], mine[:, :WIDTH], 0, 0)
        total += dot(coeffs_now[:, columns], other[:, :WIDTH], 0, 0)
        for k in range(chunk):
            place = order[first + k]
            text_now[place] = total[k * ROWS : (k + 1) * ROWS].astype(BF16)
            copies += start(
                pltpu.make_async_copy(text_now.at[place], text_out.at[place], out_sem.at[1 + place])
            )
    wait(*copies)


def merged(keep_ref, got_ref, rows):
    body = keep_ref[rows, :WIDTH] + got_ref[rows, :WIDTH].astype(F32)
    loss = jnp.sum(
        keep_ref[rows, WIDTH:] + got_ref[rows, WIDTH:].astype(F32), axis=1, keepdims=True
    )
    return body, loss


def fold(side_ref, keep_ref, got_ref, keep_out, *give_outs):
    side = side_ref[0]
    size = len(give_outs) + 1
    lane = lax.broadcasted_iota(jnp.int32, (ROWS, 128), 1)
    for group in range(keep_out.shape[0] // ROWS):
        out = pl.ds(group * ROWS, ROWS)
        for shift in range(size):
            place = lax.rem(side + shift, size)
            body, loss = merged(keep_ref, got_ref, pl.ds((size * group + place) * ROWS, ROWS))
            if shift == 0:
                keep_out[out, :WIDTH] = body
                keep_out[out, WIDTH:] = jnp.where(lane == 0, loss, 0.0)
            else:
                give_outs[shift - 1][out, :WIDTH] = body.astype(BF16)
                give_outs[shift - 1][out, WIDTH:] = loss_pair(loss)


def last_fold(keep_ref, *refs):
    got_refs, out_ref = refs[:-2], refs[-1]
    for block in range(out_ref.shape[0]):
        rows = pl.ds(block * ROWS, ROWS)
        terms = keep_ref[rows, :]
        for got_ref in got_refs:
            terms += got_ref[rows, :].astype(F32)
        out_ref[block, :, :WIDTH] = terms[:, :WIDTH].astype(BF16)
        out_ref[block, :, WIDTH:] = loss_pair(jnp.sum(terms[:, WIDTH:], axis=1, keepdims=True))


def unproject(log_temp_ref, embed_ref, terms):
    scale = jnp.exp(jnp.full((1, 1), log_temp_ref[0], F32))
    unit, radius = unit_of(embed_ref[...])
    grad = scale * terms
    return (grad - unit * jnp.sum(unit * grad, axis=1, keepdims=True)) / radius


def fold_text(bit_ref, terms_ref, keep_out, give_out):
    bit = bit_ref[0]
    for pair in range(keep_out.shape[0]):
        for out_ref, place in ((keep_out, bit), (give_out, 1 - bit)):
            terms = terms_ref[0, 2 * pair + place].astype(F32)
            for k in range(1, terms_ref.shape[0]):
                terms += terms_ref[k, 2 * pair + place].astype(F32)
            out_ref[pair] = terms.astype(out_ref.dtype)


def fold_text_again(bit_ref, keep_ref, got_ref, keep_out, give_out):
    bit = bit_ref[0]
    keep_out[...] = keep_ref[bit] + got_ref[bit].astype(F32)
    give_out[...] = (keep_ref[1 - bit] + got_ref[1 - bit].astype(F32)).astype(BF16)


def finish_text(log_temp_ref, embed_ref, keep_ref, got_ref, grad_out):
    terms = keep_ref[...] + got_ref[...].astype(F32)
    grad_out[...] = unproject(log_temp_ref, embed_ref, terms)


def finish_image(total, log_temp_ref, embed_ref, terms_ref, grad_out, loss_out):
    terms = terms_ref[0].astype(F32)
    for k in range(1, terms_ref.shape[0]):
        terms += terms_ref[k].astype(F32)
    grad_out[...] = unproject(log_temp_ref, embed_ref, terms[:, :WIDTH])
    loss = jnp.sum(terms[:, WIDTH:], axis=1, keepdims=True) / total
    row = lax.broadcasted_iota(jnp.int32, (ROWS, 128), 0)
    lane = lax.broadcasted_iota(jnp.int32, (ROWS, 128), 1)
    loss_out[...] = jnp.sum(jnp.where(row == lane, loss, 0.0), axis=0, keepdims=True)[:, :ROWS]


def in_hbm(array):
    return pltpu.with_memory_space_constraint(array, pltpu.HBM)


def place_of(axis):
    return lax.axis_index(axis).astype(jnp.int32).reshape(1)


def swap_cores(part):
    return lax.ppermute(part, "core", [(0, 1), (1, 0)])


def on_device(image_embed, text_embed, labels, log_temp, bias):
    total = ROWS * lax.axis_size(AXES)
    plane, column = lax.axis_size(PLANE), lax.axis_size(COLUMN)
    shape = jax.ShapeDtypeStruct

    image_wide, text_wide = call(
        prepare,
        [(VMEM, shape((ROWS, WIDE), BF16)), (HBM, shape((plane, ROWS, WIDE), BF16))],
        [HBM, HBM, HBM],
        [
            pltpu.SMEM((ROWS,), jnp.int32),
            pltpu.VMEM((ROWS, WIDTH), BF16),
            pltpu.VMEM((ROWS, WIDTH), BF16),
            pltpu.VMEM((ROWS, WIDE), BF16),
            pltpu.SemaphoreType.DMA((3,)),
            pltpu.SemaphoreType.DMA((plane,)),
        ],
        bytes_accessed=plane * ROWS * WIDE * 2,
    )(in_hbm(labels), in_hbm(image_embed), in_hbm(text_embed))

    group_text = lax.all_to_all(text_wide, PLANE, 0, 0, tiled=True).reshape(-1, WIDE)
    mine = lax.all_gather(image_wide, COLUMN, axis=0, tiled=True)
    other = swap_cores(mine)

    half, texts = column * ROWS, plane * ROWS

    coeffs, keep = call(
        first_tile,
        [(HBM, shape((half, texts), BF16)), (HBM, shape((half, WIDE), F32))],
        [SMEM, SMEM, HBM, HBM],
        [
            pltpu.VMEM((half, WIDE), BF16),
            pltpu.VMEM((texts, WIDE), BF16),
            pltpu.VMEM((half, texts), BF16),
            pltpu.VMEM((half, WIDE), F32),
            pltpu.SemaphoreType.DMA((2,)),
            pltpu.SemaphoreType.DMA((2,)),
        ],
        flops=4 * half * texts * WIDTH,
        bytes_accessed=4 * texts * WIDE,
    )(log_temp, bias, mine, group_text)

    far, low = lax.axis_size("y_hi"), lax.axis_size("y_lo")
    near = plane // far
    order = [((b // low // far) * low + b % low) * far + (b // low) % far for b in range(plane)]
    give, text_part = call(
        functools.partial(second_tile, order),
        [(HBM, shape((half, WIDE), BF16)), (HBM, shape((plane, ROWS, WIDTH), BF16))],
        [SMEM, SMEM, HBM, HBM, HBM, HBM],
        [
            pltpu.VMEM((half, WIDE), BF16),
            pltpu.VMEM((texts, WIDE), BF16),
            pltpu.VMEM((half, WIDE), BF16),
            pltpu.VMEM((half, texts), BF16),
            pltpu.VMEM((half, texts), BF16),
            pltpu.VMEM((half, WIDE), BF16),
            pltpu.VMEM((plane, ROWS, WIDTH), BF16),
            pltpu.SemaphoreType.DMA((4,)),
            pltpu.SemaphoreType.DMA((plane + 1,)),
        ],
        flops=8 * half * texts * WIDTH,
        bytes_accessed=6 * texts * WIDE,
    )(log_temp, bias, other, group_text, mine, coeffs)

    text_terms = lax.all_to_all(text_part, ("x", "y_lo"), 0, 0, tiled=True)
    text_terms = text_terms.reshape(near, far, ROWS, WIDTH)
    place = lax.axis_index("y_hi").astype(jnp.int32)
    text_keep, text_give = call(
        fold_text,
        [(VMEM, shape((far // 2, ROWS, WIDTH), F32)), (VMEM, shape((far // 2, ROWS, WIDTH), BF16))],
        [SMEM, VMEM],
        bytes_accessed=3 * texts * WIDTH,
    )((place % 2).reshape(1), text_terms)
    text_got = lax.ppermute(text_give, "y_hi", [(i, i ^ 1) for i in range(far)])
    first_got = text_got
    text_keep, text_give = call(
        fold_text_again,
        [(VMEM, shape((ROWS, WIDTH), F32)), (VMEM, shape((ROWS, WIDTH), BF16))],
        [SMEM, VMEM, VMEM],
        bytes_accessed=10 * ROWS * WIDTH,
    )((place // 2).reshape(1), text_keep, text_got)
    text_got = lax.ppermute(text_give, "y_hi", [(i, i ^ 2) for i in range(far)])

    got = swap_cores(give)
    side = lax.axis_index("z_lo").astype(jnp.int32).reshape(1)
    size, blocks = lax.axis_size("z_lo"), lax.axis_size("z_hi")
    rows = blocks * ROWS
    keep, *gives = call(
        fold,
        [(VMEM, shape((rows, WIDE), F32))] + [(VMEM, shape((rows, WIDE), BF16))] * (size - 1),
        [SMEM, VMEM, VMEM],
        bytes_accessed=32 * rows * WIDE,
    )(side, keep, got)
    gots = [
        lax.ppermute(give, "z_lo", [(i, (i + shift) % size) for i in range(size)])
        for shift, give in enumerate(gives, 1)
    ]
    (image_terms,) = call(
        last_fold,
        [(VMEM, shape((blocks, ROWS, WIDE), BF16))],
        [VMEM] * size + [HBM],
        bytes_accessed=12 * rows * WIDE,
    )(keep, *gots, first_got)
    image_terms = lax.all_to_all(image_terms, "z_hi", 0, 0, tiled=True)

    (grad_text,) = call(
        finish_text,
        [(VMEM, shape((ROWS, WIDTH), F32))],
        [SMEM, VMEM, VMEM, VMEM],
        bytes_accessed=12 * ROWS * WIDTH,
    )(log_temp, text_embed, text_keep, text_got)
    grad_image, loss = call(
        functools.partial(finish_image, total),
        [(VMEM, shape((ROWS, WIDTH), F32)), (VMEM, shape((1, ROWS), F32))],
        [SMEM, VMEM, VMEM],
        bytes_accessed=2 * blocks * ROWS * WIDE,
    )(log_temp, image_embed, image_terms)
    return (grad_image, grad_text, loss.reshape(ROWS))


def solution(mesh):
    parts = Mesh(mesh.devices.reshape(4, 4, 2, 2, 4, 4), AXES)
    placed = (P(AXES, None), P(AXES, None), P(AXES), P(), P())
    return jax.shard_map(
        on_device,
        mesh=parts,
        in_specs=placed,
        out_specs=(P(AXES, None), P(AXES, None), P(AXES)),
        check_vma=False,
    )
```

time: 134 us -> 123 us (0.918)
  the two profiles are of different devices: /device:TPU:8 before, /device:TPU:66 now
where the time goes in v3:
time: 123 us; the launch traced here: 122 us
  starting transfers between devices  45.3 us (37%)
  blocking collectives  43 us (35%)
  waiting for transfers between devices  18.2 us (15%)
  Pallas kernels  12.3 us (10%)
  between operations  2.09 us (2%)
    all_gather x1, blocking collectives, on_device(): mine = lax.all_gather(image_wide, COLUMN, axis=0, tiled=True)  43 us
    ppermute x3, starting transfers between devices, on_device(): lax.ppermute(give, 'z_lo', [(i, (i + shift) % size) for i in range(size)])  10.9 us
    all_to_all x1, starting transfers between devices, on_device(): lax.all_to_all(text_wide, PLANE, 0, 0, tiled=True).reshape(-1, WIDE)  10.3 us
    ppermute x3, waiting for transfers between devices, on_device(): lax.ppermute(give, 'z_lo', [(i, (i + shift) % size) for i in range(size)])  6.58 us
    ppermute x1, starting transfers between devices, on_device(): text_got = lax.ppermute(text_give, 'y_hi', [(i, i ^ 2) for i in range(far)])  6.28 us
    all_to_all x1, starting transfers between devices, on_device(): text_terms = lax.all_to_all(text_part, ('x', 'y_lo'), 0, 0, tiled=True)  5.85 us
    all_to_all x1, waiting for transfers between devices, on_device(): image_terms = lax.all_to_all(image_terms, 'z_hi', 0, 0, tiled=True)  5.74 us
    ppermute x1, starting transfers between devices, on_device(): text_got = lax.ppermute(text_give, 'y_hi', [(i, i ^ 1) for i in range(far)])  4.33 us
  transfers between devices with their start and end apart: 10, of which 5 were waited for; matrix products, arithmetic and copies ran while one was open for 0% of the time, Pallas kernels for 4%

profile of v3, /device:TPU:66, one launch (start us, length us, event | category | flops | bytes accessed | tf_op | source)
XLA Modules:
  0.0 121.8 jit_solution(13318863448211435056)
XLA Ops:
  0.6 2.3 %shard_map.76 = (bf16[16,1280]{1,0:T(8,128)(2,1)S(1)}, bf16[32,16,1280]{2,1,0:T(8,128)(2,1)}) custom-call(s32[16]{0:T(128)} %labels_ref.1, bf16[16,1152]{1,0:T(8,128)(2,1)} %embed_ref.2, bf16[16,1152]{1,0:T(8,128)(2,1)} %embed_ref.3), custom_call_target="tpu_custom_call" | custom-call | bytes 1310720 | tf_op jit(solution)/shard_map/pallas_call | solution.py:262
  2.9 10.3 %all-to-all-start = ((bf16[32,16,1280]{2,1,0:T(8,128)(2,1)}), bf16[32,16,1280]{2,1,0:T(8,128)(2,1)S(1)}, u32[]{:S(2)}, u32[]{:S(2)}) async-start(bf16[32,16,1280]{2,1,0:T(8,128)(2,1)} %get-tuple-element.20), calls=%async_computation | async-start | bytes 2621440 | tf_op jit(solution)/shard_map/all_to_all | solution.py:277
  13.2 43.0 %all_gather.3.mine_ref = bf16[256,1280]{1,0:T(8,128)(2,1)S(1)} all-gather(bf16[16,1280]{1,0:T(8,128)(2,1)S(1)} %get-tuple-element.19), channel_id=1, replica_groups=mesh['x'=4,'y_hi'=4,'core'=2,'y_lo'=2,'z_hi'=4,'z_lo'=4] {'z_hi','z_lo'}, dimensions={0}, use_global_device_ids=true | all-gather | bytes 696320 | tf_op jit(solution)/shard_map/all_gather | solution.py:278
  56.2 1.9 %collective-permute-start = (bf16[256,1280]{1,0:T(8,128)(2,1)S(1)}, bf16[256,1280]{1,0:T(8,128)(2,1)S(1)}, u32[]{:S(2)}, u32[]{:S(2)}) collective-permute-start(bf16[256,1280]{1,0:T(8,128)(2,1)S(1)} %all_gather.3.mine_ref), channel_id=1, source_target_pairs={{0,32},{32,0},{1,33},{33,1},{2,34},{34,2},{3,35},{35,3},{4,36},{36... | collective-permute-start | bytes 1966088 | tf_op jit(solution)/shard_map/ppermute | solution.py:254
  59.4 0.0 all-to-all-done
  59.4 2.8 %shard_map.77 = (bf16[256,512]{1,0:T(8,128)(2,1)}, f32[256,1280]{1,0:T(8,128)}) custom-call(f32[1]{0:T(128)S(6)} %copy.8.log_temp_ref, f32[1]{0:T(128)S(6)} %copy.9.bias_ref, bf16[256,1280]{1,0:T(8,128)(2,1)S(1)} %all_gather.3.mine_ref, bf16[512,1280]{1,0:T(8,128)(2,1)S(1)} %bitcast.7), custom_call_target="tpu_custom_call" | custom-call | flops 603979776 | bytes 2621440 | tf_op jit(solution)/shard_map/pallas_call | solution.py:283
  62.2 0.0 collective-permute-done.other_ref
  62.2 0.0 copy-start.3
  62.2 0.9 copy-done.3
  63.1 3.8 %shard_map.78 = (bf16[256,1280]{1,0:T(8,128)(2,1)}, bf16[32,16,1152]{2,1,0:T(8,128)(2,1)}) custom-call(f32[1]{0:T(128)S(6)} %copy.8.log_temp_ref, f32[1]{0:T(128)S(6)} %copy.9.bias_ref, bf16[256,1280]{1,0:T(8,128)(2,1)S(1)} %collective-permute-done.other_ref, bf16[512,1280]{1,0:T(8,128)(2,1)S(1)} %bitcast.8, bf16[256,1280]{1,0:T(8,128)(2,1)S(1)} %all_gather.3.mine_ref, ...), custom_call_target="tpu_custom_call" | custom-call | flops 1207959552 | bytes 3932160 | tf_op jit(solution)/shard_map/pallas_call | solution.py:302
  66.9 5.8 %all-to-all-start.1 = ((bf16[32,16,1152]{2,1,0:T(8,128)(2,1)}), bf16[32,16,1152]{2,1,0:T(8,128)(2,1)S(1)}, u32[]{:S(2)}, u32[]{:S(2)}) async-start(bf16[32,16,1152]{2,1,0:T(8,128)(2,1)} %get-tuple-element.28), calls=%async_computation.1 | async-start | bytes 2359296 | tf_op jit(solution)/shard_map/all_to_all | solution.py:321
  72.8 1.9 %collective-permute-start.1 = (bf16[256,1280]{1,0:T(8,128)(2,1)}, bf16[256,1280]{1,0:T(8,128)(2,1)S(1)}, u32[]{:S(2)}, u32[]{:S(2)}) collective-permute-start(bf16[256,1280]{1,0:T(8,128)(2,1)} %get-tuple-element.23), channel_id=1, source_target_pairs={{0,32},{32,0},{1,33},{33,1},{2,34},{34,2},{3,35},{35,3},{4,36},{36... | collective-permute-start | bytes 1966088 | tf_op jit(solution)/shard_map/ppermute | solution.py:254
  74.7 2.3 %collective-permute-done.1.got_ref = bf16[256,1280]{1,0:T(8,128)(2,1)S(1)} collective-permute-done((bf16[256,1280]{1,0:T(8,128)(2,1)}, bf16[256,1280]{1,0:T(8,128)(2,1)S(1)}, u32[]{:S(2)}, u32[]{:S(2)}) %collective-permute-start.1) | collective-permute-done | bytes 655392 | tf_op jit(solution)/shard_map/ppermute | solution.py:254
  77.0 0.9 shard_map.79
  77.9 3.5 %collective-permute-start.2 = (bf16[64,1280]{1,0:T(8,128)(2,1)}, bf16[64,1280]{1,0:T(8,128)(2,1)S(1)}, u32[]{:S(2)}, u32[]{:S(2)}) collective-permute-start(bf16[64,1280]{1,0:T(8,128)(2,1)} %get-tuple-element.25), channel_id=1, source_target_pairs={{0,1},{1,2},{2,3},{3,0},{4,5},{5,6},{6,7},{7,4},{8,9},{9,10},{10,1... | collective-permute-start | bytes 491528 | tf_op jit(solution)/shard_map/ppermute | solution.py:351
  81.4 5.5 %collective-permute-start.3 = (bf16[64,1280]{1,0:T(8,128)(2,1)}, bf16[64,1280]{1,0:T(8,128)(2,1)S(1)}, u32[]{:S(2)}, u32[]{:S(2)}) collective-permute-start(bf16[64,1280]{1,0:T(8,128)(2,1)} %get-tuple-element.26), channel_id=1, source_target_pairs={{0,2},{1,3},{2,0},{3,1},{4,6},{5,7},{6,4},{7,5},{8,10},{9,11},{10,... | collective-permute-start | bytes 491528 | tf_op jit(solution)/shard_map/ppermute | solution.py:351
  86.8 1.9 %collective-permute-start.4 = (bf16[64,1280]{1,0:T(8,128)(2,1)}, bf16[64,1280]{1,0:T(8,128)(2,1)S(1)}, u32[]{:S(2)}, u32[]{:S(2)}) collective-permute-start(bf16[64,1280]{1,0:T(8,128)(2,1)} %get-tuple-element.27), channel_id=1, source_target_pairs={{0,3},{1,0},{2,1},{3,2},{4,7},{5,4},{6,5},{7,6},{8,11},{9,8},{10,9... | collective-permute-start | bytes 491528 | tf_op jit(solution)/shard_map/ppermute | solution.py:351
  88.8 0.0 all-to-all-done.1
  88.8 0.2 shard_map.80
  89.0 4.3 %collective-permute-start.5 = (bf16[2,16,1152]{2,1,0:T(8,128)(2,1)S(1)}, bf16[2,16,1152]{2,1,0:T(8,128)(2,1)S(1)}, u32[]{:S(2)}, u32[]{:S(2)}) collective-permute-start(bf16[2,16,1152]{2,1,0:T(8,128)(2,1)S(1)} %get-tuple-element.29), channel_id=1, source_target_pairs={{0,64},{64,0},{128,192},{192,128},{1,65},{65,1},{129,193},{193,129... | collective-permute-start | bytes 221192 | tf_op jit(solution)/shard_map/ppermute | solution.py:330
  93.3 0.0 collective-permute-done.2.refs_0_
  93.3 3.6 %collective-permute-done.3.refs_1_ = bf16[64,1280]{1,0:T(8,128)(2,1)S(1)} collective-permute-done((bf16[64,1280]{1,0:T(8,128)(2,1)}, bf16[64,1280]{1,0:T(8,128)(2,1)S(1)}, u32[]{:S(2)}, u32[]{:S(2)}) %collective-permute-start.3) | collective-permute-done | bytes 163872 | tf_op jit(solution)/shard_map/ppermute | solution.py:351
  96.9 3.0 %collective-permute-done.4.refs_2_ = bf16[64,1280]{1,0:T(8,128)(2,1)S(1)} collective-permute-done((bf16[64,1280]{1,0:T(8,128)(2,1)}, bf16[64,1280]{1,0:T(8,128)(2,1)S(1)}, u32[]{:S(2)}, u32[]{:S(2)}) %collective-permute-start.4) | collective-permute-done | bytes 163872 | tf_op jit(solution)/shard_map/ppermute | solution.py:351
  99.9 0.0 collective-permute-done.5.refs_3_.got_ref
  99.9 0.8 shard_map.81
  100.7 3.9 %all-to-all-start.2 = ((bf16[4,16,1280]{2,1,0:T(8,128)(2,1)}), bf16[4,16,1280]{2,1,0:T(8,128)(2,1)S(1)}, u32[]{:S(2)}, u32[]{:S(2)}) async-start(bf16[4,16,1280]{2,1,0:T(8,128)(2,1)} %shard_map.81), calls=%async_computation.2 | async-start | bytes 327680 | tf_op jit(solution)/shard_map/all_to_all | solution.py:360
  104.6 6.3 %collective-permute-start.6 = (bf16[16,1152]{1,0:T(8,128)(2,1)S(1)}, bf16[16,1152]{1,0:T(8,128)(2,1)S(1)}, u32[]{:S(2)}, u32[]{:S(2)}) collective-permute-start(bf16[16,1152]{1,0:T(8,128)(2,1)S(1)} %get-tuple-element.33), channel_id=1, source_target_pairs={{0,128},{64,192},{128,0},{192,64},{1,129},{65,193},{129,1},{193,65... | collective-permute-start | bytes 110600 | tf_op jit(solution)/shard_map/ppermute | solution.py:338
  110.9 3.6 %collective-permute-done.6.got_ref = bf16[16,1152]{1,0:T(8,128)(2,1)S(1)} collective-permute-done((bf16[16,1152]{1,0:T(8,128)(2,1)S(1)}, bf16[16,1152]{1,0:T(8,128)(2,1)S(1)}, u32[]{:S(2)}, u32[]{:S(2)}) %collective-permute-start.6) | collective-permute-done | bytes 36896 | tf_op jit(solution)/shard_map/ppermute | solution.py:338
  114.4 0.8 shard_map.84
  115.3 5.7 %all-to-all-done.2.terms_ref = bf16[4,16,1280]{2,1,0:T(8,128)(2,1)S(1)} async-done(((bf16[4,16,1280]{2,1,0:T(8,128)(2,1)}), bf16[4,16,1280]{2,1,0:T(8,128)(2,1)S(1)}, u32[]{:S(2)}, u32[]{:S(2)}) %all-to-all-start.2) | async-done | bytes 163872 | tf_op jit(solution)/shard_map/all_to_all | solution.py:360
  121.0 0.0 copy-done.2
  121.0 0.8 shard_map.82
  (6 shorter events, 0.0 us)
Async XLA Ops:
  2.9 56.5 %all-to-all-start = ((bf16[32,16,1280]{2,1,0:T(8,128)(2,1)}), bf16[32,16,1280]{2,1,0:T(8,128)(2,1)S(1)}, u32[]{:S(2)}, u32[]{:S(2)}) async-start(bf16[32,16,1280]{2,1,0:T(8,128)(2,1)} %get-tuple-element.20), calls=%async_computation | async-start | bytes 2621440 | tf_op jit(solution)/shard_map/all_to_all | solution.py:277
  56.2 6.0 %collective-permute-start = (bf16[256,1280]{1,0:T(8,128)(2,1)S(1)}, bf16[256,1280]{1,0:T(8,128)(2,1)S(1)}, u32[]{:S(2)}, u32[]{:S(2)}) collective-permute-start(bf16[256,1280]{1,0:T(8,128)(2,1)S(1)} %all_gather.3.mine_ref), channel_id=1, source_target_pairs={{0,32},{32,0},{1,33},{33,1},{2,34},{34,2},{3,35},{35,3},{4,36},{36... | collective-permute-start | bytes 1966088 | tf_op jit(solution)/shard_map/ppermute | solution.py:254
  62.2 1.0 copy-start.3
  66.9 10.1 %copy-start = (f32[256,1280]{1,0:T(8,128)S(1)}, f32[256,1280]{1,0:T(8,128)}, u32[]{:S(2)}) copy-start(f32[256,1280]{1,0:T(8,128)} %get-tuple-element.21.keep_ref) | copy-start | bytes 3932164
  66.9 21.9 %all-to-all-start.1 = ((bf16[32,16,1152]{2,1,0:T(8,128)(2,1)}), bf16[32,16,1152]{2,1,0:T(8,128)(2,1)S(1)}, u32[]{:S(2)}, u32[]{:S(2)}) async-start(bf16[32,16,1152]{2,1,0:T(8,128)(2,1)} %get-tuple-element.28), calls=%async_computation.1 | async-start | bytes 2359296 | tf_op jit(solution)/shard_map/all_to_all | solution.py:321
  72.8 4.2 %collective-permute-start.1 = (bf16[256,1280]{1,0:T(8,128)(2,1)}, bf16[256,1280]{1,0:T(8,128)(2,1)S(1)}, u32[]{:S(2)}, u32[]{:S(2)}) collective-permute-start(bf16[256,1280]{1,0:T(8,128)(2,1)} %get-tuple-element.23), channel_id=1, source_target_pairs={{0,32},{32,0},{1,33},{33,1},{2,34},{34,2},{3,35},{35,3},{4,36},{36... | collective-permute-start | bytes 1966088 | tf_op jit(solution)/shard_map/ppermute | solution.py:254
  77.9 15.5 %collective-permute-start.2 = (bf16[64,1280]{1,0:T(8,128)(2,1)}, bf16[64,1280]{1,0:T(8,128)(2,1)S(1)}, u32[]{:S(2)}, u32[]{:S(2)}) collective-permute-start(bf16[64,1280]{1,0:T(8,128)(2,1)} %get-tuple-element.25), channel_id=1, source_target_pairs={{0,1},{1,2},{2,3},{3,0},{4,5},{5,6},{6,7},{7,4},{8,9},{9,10},{10,1... | collective-permute-start | bytes 491528 | tf_op jit(solution)/shard_map/ppermute | solution.py:351
  81.4 15.5 %collective-permute-start.3 = (bf16[64,1280]{1,0:T(8,128)(2,1)}, bf16[64,1280]{1,0:T(8,128)(2,1)S(1)}, u32[]{:S(2)}, u32[]{:S(2)}) collective-permute-start(bf16[64,1280]{1,0:T(8,128)(2,1)} %get-tuple-element.26), channel_id=1, source_target_pairs={{0,2},{1,3},{2,0},{3,1},{4,6},{5,7},{6,4},{7,5},{8,10},{9,11},{10,... | collective-permute-start | bytes 491528 | tf_op jit(solution)/shard_map/ppermute | solution.py:351
  86.8 13.1 %collective-permute-start.4 = (bf16[64,1280]{1,0:T(8,128)(2,1)}, bf16[64,1280]{1,0:T(8,128)(2,1)S(1)}, u32[]{:S(2)}, u32[]{:S(2)}) collective-permute-start(bf16[64,1280]{1,0:T(8,128)(2,1)} %get-tuple-element.27), channel_id=1, source_target_pairs={{0,3},{1,0},{2,1},{3,2},{4,7},{5,4},{6,5},{7,6},{8,11},{9,8},{10,9... | collective-permute-start | bytes 491528 | tf_op jit(solution)/shard_map/ppermute | solution.py:351
  88.8 25.6 %copy-start.1 = (bf16[16,1152]{1,0:T(8,128)(2,1)S(1)}, bf16[16,1152]{1,0:T(8,128)(2,1)}, u32[]{:S(2)}) copy-start(bf16[16,1152]{1,0:T(8,128)(2,1)} %embed_ref.3) | copy-start | bytes 110596
  88.8 32.2 %copy-start.2 = (bf16[16,1152]{1,0:T(8,128)(2,1)S(1)}, bf16[16,1152]{1,0:T(8,128)(2,1)}, u32[]{:S(2)}) copy-start(bf16[16,1152]{1,0:T(8,128)(2,1)} %embed_ref.2) | copy-start | bytes 110596
  89.0 10.9 %collective-permute-start.5 = (bf16[2,16,1152]{2,1,0:T(8,128)(2,1)S(1)}, bf16[2,16,1152]{2,1,0:T(8,128)(2,1)S(1)}, u32[]{:S(2)}, u32[]{:S(2)}) collective-permute-start(bf16[2,16,1152]{2,1,0:T(8,128)(2,1)S(1)} %get-tuple-element.29), channel_id=1, source_target_pairs={{0,64},{64,0},{128,192},{192,128},{1,65},{65,1},{129,193},{193,129... | collective-permute-start | bytes 221192 | tf_op jit(solution)/shard_map/ppermute | solution.py:330
  100.7 20.3 %all-to-all-start.2 = ((bf16[4,16,1280]{2,1,0:T(8,128)(2,1)}), bf16[4,16,1280]{2,1,0:T(8,128)(2,1)S(1)}, u32[]{:S(2)}, u32[]{:S(2)}) async-start(bf16[4,16,1280]{2,1,0:T(8,128)(2,1)} %shard_map.81), calls=%async_computation.2 | async-start | bytes 327680 | tf_op jit(solution)/shard_map/all_to_all | solution.py:360
  104.6 9.9 %collective-permute-start.6 = (bf16[16,1152]{1,0:T(8,128)(2,1)S(1)}, bf16[16,1152]{1,0:T(8,128)(2,1)S(1)}, u32[]{:S(2)}, u32[]{:S(2)}) collective-permute-start(bf16[16,1152]{1,0:T(8,128)(2,1)S(1)} %get-tuple-element.33), channel_id=1, source_target_pairs={{0,128},{64,192},{128,0},{192,64},{1,129},{65,193},{129,1},{193,65... | collective-permute-start | bytes 110600 | tf_op jit(solution)/shard_map/ppermute | solution.py:338

commit v4 on v3

--- a/solution.py
+++ b/solution.py
@@ -129,9 +129,8 @@
     loss, coeffs = half_tile(log_temp_ref, bias_ref, mine, text)
     coeffs_now[...] = coeffs
     (coeffs_copy,) = start(pltpu.make_async_copy(coeffs_now, coeffs_out, out_sem.at[0]))
-    lane = lax.broadcasted_iota(jnp.int32, (loss.shape[0], 128), 1)
     keep_now[:, :WIDTH] = dot(coeffs, text[:, :WIDTH], 1, 0)
-    keep_now[:, WIDTH:] = jnp.where(lane == 0, loss, 0.0)
+    keep_now[:, WIDTH:] = loss_lane(loss)
     (keep_copy,) = start(pltpu.make_async_copy(keep_now, keep_out, out_sem.at[1]))
     wait(coeffs_copy, keep_copy)
 
@@ -167,40 +166,43 @@
     wait(*copies)
 
 
-def merged(keep_ref, got_ref, rows):
-    body = keep_ref[rows, :WIDTH] + got_ref[rows, :WIDTH].astype(F32)
-    loss = jnp.sum(
-        keep_ref[rows, WIDTH:] + got_ref[rows, WIDTH:].astype(F32), axis=1, keepdims=True
-    )
-    return body, loss
-
-
-def fold(side_ref, keep_ref, got_ref, keep_out, *give_outs):
-    side = side_ref[0]
-    size = len(give_outs) + 1
-    lane = lax.broadcasted_iota(jnp.int32, (ROWS, 128), 1)
-    for group in range(keep_out.shape[0] // ROWS):
-        out = pl.ds(group * ROWS, ROWS)
-        for shift in range(size):
-            place = lax.rem(side + shift, size)
-            body, loss = merged(keep_ref, got_ref, pl.ds((size * group + place) * ROWS, ROWS))
-            if shift == 0:
-                keep_out[out, :WIDTH] = body
-                keep_out[out, WIDTH:] = jnp.where(lane == 0, loss, 0.0)
+def loss_lane(loss):
+    lane = lax.broadcasted_iota(jnp.int32, (loss.shape[0], 128), 1)
+    return jnp.where(lane == 0, loss, 0.0)
+
+
+def fold(bit_ref, keep_ref, got_ref, keep_out, left_out, right_out):
+    bit = bit_ref[0]
+    split = left_out.shape[1]
+    for pair in range(keep_out.shape[0] // ROWS):
+        out = pl.ds(pair * ROWS, ROWS)
+        for place in (bit, 1 - bit):
+            rows = pl.ds((2 * pair + place) * ROWS, ROWS)
+            terms = keep_ref[rows, :] + got_ref[rows, :].astype(F32)
+            loss = jnp.sum(terms[:, WIDTH:], axis=1, keepdims=True)
+            if place is bit:
+                keep_out[out, :WIDTH] = terms[:, :WIDTH]
+                keep_out[out, WIDTH:] = loss_lane(loss)
             else:
-                give_outs[shift - 1][out, :WIDTH] = body.astype(BF16)
-                give_outs[shift - 1][out, WIDTH:] = loss_pair(loss)
-
-
-def last_fold(keep_ref, *refs):
-    got_refs, out_ref = refs[:-2], refs[-1]
+                left_out[out, :] = terms[:, :split].astype(BF16)
+                right_out[out, : WIDTH - split] = terms[:, split:WIDTH].astype(BF16)
+                right_out[out, WIDTH - split :] = loss_pair(loss)
+
+
+def last_fold(keep_ref, left_ref, right_ref, part_out, out_ref, out_sem):
+    copies = []
+    split = left_ref.shape[1]
     for block in range(out_ref.shape[0]):
         rows = pl.ds(block * ROWS, ROWS)
-        terms = keep_ref[rows, :]
-        for got_ref in got_refs:
-            terms += got_ref[rows, :].astype(F32)
-        out_ref[block, :, :WIDTH] = terms[:, :WIDTH].astype(BF16)
-        out_ref[block, :, WIDTH:] = loss_pair(jnp.sum(terms[:, WIDTH:], axis=1, keepdims=True))
+        out_ref[block, :, :split] = (keep_ref[rows, :split] + left_ref[rows, :].astype(F32)).astype(BF16)
+        terms = keep_ref[rows, split:] + right_ref[rows, :].astype(F32)
+        out_ref[block, :, split:WIDTH] = terms[:, : WIDTH - split].astype(BF16)
+        loss = jnp.sum(terms[:, WIDTH - split :], axis=1, keepdims=True)
+        out_ref[block, :, WIDTH:] = loss_pair(loss)
+        copies += start(
+            pltpu.make_async_copy(out_ref.at[block], part_out.at[block], out_sem.at[block])
+        )
+    wait(*copies)
 
 
 def unproject(log_temp_ref, embed_ref, terms):
@@ -316,9 +318,31 @@
         ],
         flops=8 * half * texts * WIDTH,
         bytes_accessed=6 * texts * WIDE,
-    )(log_temp, bias, other, group_text, mine, coeffs)
+    )(log_temp, bias, other, group_text, mine, in_hbm(coeffs))
 
     text_terms = lax.all_to_all(text_part, ("x", "y_lo"), 0, 0, tiled=True)
+    got = swap_cores(give)
+    blocks = lax.axis_size("z_hi")
+    rows = blocks * ROWS
+    split = WIDE // 2
+    keep, left, right = call(
+        fold,
+        [(VMEM, shape((rows, WIDE), F32)), (VMEM, shape((rows, split), BF16)), (VMEM, shape((rows, WIDE - split), BF16))],
+        [SMEM, VMEM, VMEM],
+        bytes_accessed=16 * rows * WIDE,
+    )(place_of("z_lo"), keep, got)
+    left = lax.ppermute(left, COLUMN, [(i, i ^ 1) for i in range(column)])
+    right = lax.ppermute(
+        right, COLUMN, [(i, (i + (1 if i % 2 else -1)) % column) for i in range(column)]
+    )
+    (image_terms,) = call(
+        last_fold,
+        [(HBM, shape((blocks, ROWS, WIDE), BF16))],
+        [VMEM, VMEM, VMEM],
+        [pltpu.VMEM((blocks, ROWS, WIDE), BF16), pltpu.SemaphoreType.DMA((blocks,))],
+        bytes_accessed=8 * rows * WIDE,
+    )(keep, left, right)
+    image_terms, text_terms = lax.optimization_barrier((image_terms, text_terms))
     text_terms = text_terms.reshape(near, far, ROWS, WIDTH)
     place = lax.axis_index("y_hi").astype(jnp.int32)
     text_keep, text_give = call(
@@ -328,7 +352,6 @@
         bytes_accessed=3 * texts * WIDTH,
     )((place % 2).reshape(1), text_terms)
     text_got = lax.ppermute(text_give, "y_hi", [(i, i ^ 1) for i in range(far)])
-    first_got = text_got
     text_keep, text_give = call(
         fold_text_again,
         [(VMEM, shape((ROWS, WIDTH), F32)), (VMEM, shape((ROWS, WIDTH), BF16))],
@@ -337,26 +360,6 @@
     )((place // 2).reshape(1), text_keep, text_got)
     text_got = lax.ppermute(text_give, "y_hi", [(i, i ^ 2) for i in range(far)])
 
-    got = swap_cores(give)
-    side = lax.axis_index("z_lo").astype(jnp.int32).reshape(1)
-    size, blocks = lax.axis_size("z_lo"), lax.axis_size("z_hi")
-    rows = blocks * ROWS
-    keep, *gives = call(
-        fold,
-        [(VMEM, shape((rows, WIDE), F32))] + [(VMEM, shape((rows, WIDE), BF16))] * (size - 1),
-        [SMEM, VMEM, VMEM],
-        bytes_accessed=32 * rows * WIDE,
-    )(side, keep, got)
-    gots = [
-        lax.ppermute(give, "z_lo", [(i, (i + shift) % size) for i in range(size)])
-        for shift, give in enumerate(gives, 1)
-    ]
-    (image_terms,) = call(
-        last_fold,
-        [(VMEM, shape((blocks, ROWS, WIDE), BF16))],
-        [VMEM] * size + [HBM],
-        bytes_accessed=12 * rows * WIDE,
-    )(keep, *gots, first_got)
     image_terms = lax.all_to_all(image_terms, "z_hi", 0, 0, tiled=True)
 
     (grad_text,) = call(
@@ -375,7 +378,7 @@
 
 
 def solution(mesh):
-    parts = Mesh(mesh.devices.reshape(4, 4, 2, 2, 4, 4), AXES)
+    parts = Mesh(mesh.devices.reshape(4, 4, 2, 2, 8, 2), AXES)
     placed = (P(AXES, None), P(AXES, None), P(AXES), P(), P())
     return jax.shard_map(
         on_device,

time: 123 us -> 121 us (0.984)
  the two profiles are of different devices: /device:TPU:66 before, /device:TPU:16 now
where the time goes in v4:
time: 121 us; the launch traced here: 120 us
  starting transfers between devices  41.7 us (34%)
  blocking collectives  39.5 us (33%)
  waiting for transfers between devices  25 us (21%)
  Pallas kernels  11.7 us (10%)
  between operations  2.08 us (2%)
    all_gather x1, blocking collectives, on_device(): mine = lax.all_gather(image_wide, COLUMN, axis=0, tiled=True)  39.5 us
    all_to_all x1, starting transfers between devices, on_device(): lax.all_to_all(text_wide, PLANE, 0, 0, tiled=True).reshape(-1, WIDE)  16.6 us
    all_to_all x1, starting transfers between devices, on_device(): text_terms = lax.all_to_all(text_part, ('x', 'y_lo'), 0, 0, tiled=True)  5.29 us
    all_to_all x1, waiting for transfers between devices, on_device(): image_terms = lax.all_to_all(image_terms, 'z_hi', 0, 0, tiled=True)  5.27 us
    ppermute x1, waiting for transfers between devices, on_device(): text_got = lax.ppermute(text_give, 'y_hi', [(i, i ^ 2) for i in range(far)])  5.14 us
    ppermute x1, starting transfers between devices, on_device(): text_got = lax.ppermute(text_give, 'y_hi', [(i, i ^ 2) for i in range(far)])  4.71 us
    ppermute x1, waiting for transfers between devices, on_device(): text_got = lax.ppermute(text_give, 'y_hi', [(i, i ^ 1) for i in range(far)])  4.65 us
    ppermute x2, starting transfers between devices, swap_cores(): return lax.ppermute(part, 'core', [(0, 1), (1, 0)])  4.02 us
  transfers between devices with their start and end apart: 9, of which 7 were waited for; matrix products, arithmetic and copies ran while one was open for 0% of the time, Pallas kernels for 4%

profile of v4, /device:TPU:16, one launch (start us, length us, event | category | flops | bytes accessed | tf_op | source)
XLA Modules:
  0.0 120.0 jit_solution(1565044260456924367)
XLA Ops:
  0.6 2.3 %shard_map.76 = (bf16[16,1280]{1,0:T(8,128)(2,1)S(1)}, bf16[32,16,1280]{2,1,0:T(8,128)(2,1)}) custom-call(s32[16]{0:T(128)} %labels_ref.1, bf16[16,1152]{1,0:T(8,128)(2,1)} %embed_ref.2, bf16[16,1152]{1,0:T(8,128)(2,1)} %embed_ref.3), custom_call_target="tpu_custom_call" | custom-call | bytes 1310720 | tf_op jit(solution)/shard_map/pallas_call | solution.py:264
  2.9 16.6 %all-to-all-start = ((bf16[32,16,1280]{2,1,0:T(8,128)(2,1)}), bf16[32,16,1280]{2,1,0:T(8,128)(2,1)S(1)}, u32[]{:S(2)}, u32[]{:S(2)}) async-start(bf16[32,16,1280]{2,1,0:T(8,128)(2,1)} %get-tuple-element.21), calls=%async_computation | async-start | bytes 2621440 | tf_op jit(solution)/shard_map/all_to_all | solution.py:279
  19.5 39.5 %all_gather.3.mine_ref = bf16[256,1280]{1,0:T(8,128)(2,1)S(1)} all-gather(bf16[16,1280]{1,0:T(8,128)(2,1)S(1)} %get-tuple-element.20), channel_id=1, replica_groups=mesh['x'=4,'y_hi'=4,'core'=2,'y_lo'=2,'z_hi'=8,'z_lo'=2] {'z_hi','z_lo'}, dimensions={0}, use_global_device_ids=true | all-gather | bytes 696320 | tf_op jit(solution)/shard_map/all_gather | solution.py:280
  59.0 1.9 %collective-permute-start = (bf16[256,1280]{1,0:T(8,128)(2,1)S(1)}, bf16[256,1280]{1,0:T(8,128)(2,1)S(1)}, u32[]{:S(2)}, u32[]{:S(2)}) collective-permute-start(bf16[256,1280]{1,0:T(8,128)(2,1)S(1)} %all_gather.3.mine_ref), channel_id=1, source_target_pairs={{0,32},{32,0},{1,33},{33,1},{2,34},{34,2},{3,35},{35,3},{4,36},{36... | collective-permute-start | bytes 1966088 | tf_op jit(solution)/shard_map/ppermute | solution.py:256
  62.2 0.0 all-to-all-done
  62.2 2.8 %shard_map.77 = (bf16[256,512]{1,0:T(8,128)(2,1)}, f32[256,1280]{1,0:T(8,128)}) custom-call(f32[1]{0:T(128)S(6)} %copy.8.log_temp_ref, f32[1]{0:T(128)S(6)} %copy.9.bias_ref, bf16[256,1280]{1,0:T(8,128)(2,1)S(1)} %all_gather.3.mine_ref, bf16[512,1280]{1,0:T(8,128)(2,1)S(1)} %bitcast.7), custom_call_target="tpu_custom_call" | custom-call | flops 603979776 | bytes 2621440 | tf_op jit(solution)/shard_map/pallas_call | solution.py:285
  65.0 0.0 collective-permute-done.other_ref
  65.0 3.8 %shard_map.78 = (bf16[256,1280]{1,0:T(8,128)(2,1)}, bf16[32,16,1152]{2,1,0:T(8,128)(2,1)}) custom-call(f32[1]{0:T(128)S(6)} %copy.8.log_temp_ref, f32[1]{0:T(128)S(6)} %copy.9.bias_ref, bf16[256,1280]{1,0:T(8,128)(2,1)S(1)} %collective-permute-done.other_ref, bf16[512,1280]{1,0:T(8,128)(2,1)S(1)} %bitcast.8, bf16[256,1280]{1,0:T(8,128)(2,1)S(1)} %all_gather.3.mine_ref, ...), custom_call_target="tpu_custom_call" | custom-call | flops 1207959552 | bytes 3932160 | tf_op jit(solution)/shard_map/pallas_call | solution.py:304
  68.8 0.0 copy-start
  68.8 5.3 %all-to-all-start.1 = ((bf16[32,16,1152]{2,1,0:T(8,128)(2,1)}), bf16[32,16,1152]{2,1,0:T(8,128)(2,1)S(1)}, u32[]{:S(2)}, u32[]{:S(2)}) async-start(bf16[32,16,1152]{2,1,0:T(8,128)(2,1)} %get-tuple-element.28), calls=%async_computation.1 | async-start | bytes 2359296 | tf_op jit(solution)/shard_map/all_to_all | solution.py:323
  74.1 2.1 %collective-permute-start.1 = (bf16[256,1280]{1,0:T(8,128)(2,1)}, bf16[256,1280]{1,0:T(8,128)(2,1)S(1)}, u32[]{:S(2)}, u32[]{:S(2)}) collective-permute-start(bf16[256,1280]{1,0:T(8,128)(2,1)} %get-tuple-element.24), channel_id=1, source_target_pairs={{0,32},{32,0},{1,33},{33,1},{2,34},{34,2},{3,35},{35,3},{4,36},{36... | collective-permute-start | bytes 1966088 | tf_op jit(solution)/shard_map/ppermute | solution.py:256
  76.2 2.1 %collective-permute-done.1.got_ref = bf16[256,1280]{1,0:T(8,128)(2,1)S(1)} collective-permute-done((bf16[256,1280]{1,0:T(8,128)(2,1)}, bf16[256,1280]{1,0:T(8,128)(2,1)S(1)}, u32[]{:S(2)}, u32[]{:S(2)}) %collective-permute-start.1) | collective-permute-done | bytes 655392 | tf_op jit(solution)/shard_map/ppermute | solution.py:256
  78.3 0.0 copy-done
  78.3 0.2 shard_map.79
  78.5 1.9 %collective-permute-start.2 = (bf16[128,640]{1,0:T(8,128)(2,1)S(1)}, bf16[128,640]{1,0:T(8,128)(2,1)S(1)}, u32[]{:S(2)}, u32[]{:S(2)}) collective-permute-start(bf16[128,640]{1,0:T(8,128)(2,1)S(1)} %get-tuple-element.26), channel_id=1, source_target_pairs={{0,1},{1,0},{2,3},{3,2},{4,5},{5,4},{6,7},{7,6},{8,9},{9,8},{10,11... | collective-permute-start | bytes 491528 | tf_op jit(solution)/shard_map/ppermute | solution.py:334
  80.4 2.7 %collective-permute-start.3 = (bf16[128,640]{1,0:T(8,128)(2,1)S(1)}, bf16[128,640]{1,0:T(8,128)(2,1)S(1)}, u32[]{:S(2)}, u32[]{:S(2)}) collective-permute-start(bf16[128,640]{1,0:T(8,128)(2,1)S(1)} %get-tuple-element.27), channel_id=1, source_target_pairs={{0,15},{1,2},{2,1},{3,4},{4,3},{5,6},{6,5},{7,8},{8,7},{9,10},{10,... | collective-permute-start | bytes 491528 | tf_op jit(solution)/shard_map/ppermute | solution.py:335
  83.1 3.6 %collective-permute-done.2.left_ref = bf16[128,640]{1,0:T(8,128)(2,1)S(1)} collective-permute-done((bf16[128,640]{1,0:T(8,128)(2,1)S(1)}, bf16[128,640]{1,0:T(8,128)(2,1)S(1)}, u32[]{:S(2)}, u32[]{:S(2)}) %collective-permute-start.2) | collective-permute-done | bytes 163872 | tf_op jit(solution)/shard_map/ppermute | solution.py:334
  86.7 3.1 %collective-permute-done.3.right_ref = bf16[128,640]{1,0:T(8,128)(2,1)S(1)} collective-permute-done((bf16[128,640]{1,0:T(8,128)(2,1)S(1)}, bf16[128,640]{1,0:T(8,128)(2,1)S(1)}, u32[]{:S(2)}, u32[]{:S(2)}) %collective-permute-start.3) | collective-permute-done | bytes 163872 | tf_op jit(solution)/shard_map/ppermute | solution.py:335
  89.8 0.9 shard_map.80
  90.7 0.0 copy-start.1
  90.7 0.0 copy-start.2
  90.8 1.2 all-to-all-done.1
  91.9 3.9 %all-to-all-start.2 = ((bf16[8,16,1280]{2,1,0:T(8,128)(2,1)}), bf16[8,16,1280]{2,1,0:T(8,128)(2,1)S(1)}, u32[]{:S(2)}, u32[]{:S(2)}) async-start(bf16[8,16,1280]{2,1,0:T(8,128)(2,1)} %shard_map.80), calls=%async_computation.2 | async-start | bytes 655360 | tf_op jit(solution)/shard_map/all_to_all | solution.py:363
  95.8 0.2 shard_map.82
  96.0 2.6 %collective-permute-start.4 = (bf16[2,16,1152]{2,1,0:T(8,128)(2,1)S(1)}, bf16[2,16,1152]{2,1,0:T(8,128)(2,1)S(1)}, u32[]{:S(2)}, u32[]{:S(2)}) collective-permute-start(bf16[2,16,1152]{2,1,0:T(8,128)(2,1)S(1)} %get-tuple-element.33), channel_id=1, source_target_pairs={{0,64},{64,0},{128,192},{192,128},{1,65},{65,1},{129,193},{193,129... | collective-permute-start | bytes 221192 | tf_op jit(solution)/shard_map/ppermute | solution.py:354
  98.6 4.6 %collective-permute-done.4.got_ref = bf16[2,16,1152]{2,1,0:T(8,128)(2,1)S(1)} collective-permute-done((bf16[2,16,1152]{2,1,0:T(8,128)(2,1)S(1)}, bf16[2,16,1152]{2,1,0:T(8,128)(2,1)S(1)}, u32[]{:S(2)}, u32[]{:S(2)}) %collective-permute-start.4) | collective-permute-done | bytes 73760 | tf_op jit(solution)/shard_map/ppermute | solution.py:354
  103.2 4.7 %collective-permute-start.5 = (bf16[16,1152]{1,0:T(8,128)(2,1)S(1)}, bf16[16,1152]{1,0:T(8,128)(2,1)S(1)}, u32[]{:S(2)}, u32[]{:S(2)}) collective-permute-start(bf16[16,1152]{1,0:T(8,128)(2,1)S(1)} %get-tuple-element.35), channel_id=1, source_target_pairs={{0,128},{64,192},{128,0},{192,64},{1,129},{65,193},{129,1},{193,65... | collective-permute-start | bytes 110600 | tf_op jit(solution)/shard_map/ppermute | solution.py:361
  107.9 5.1 %collective-permute-done.5.got_ref = bf16[16,1152]{1,0:T(8,128)(2,1)S(1)} collective-permute-done((bf16[16,1152]{1,0:T(8,128)(2,1)S(1)}, bf16[16,1152]{1,0:T(8,128)(2,1)S(1)}, u32[]{:S(2)}, u32[]{:S(2)}) %collective-permute-start.5) | collective-permute-done | bytes 36896 | tf_op jit(solution)/shard_map/ppermute | solution.py:361
  113.1 0.8 shard_map.84
  113.9 5.3 %all-to-all-done.2.terms_ref = bf16[8,16,1280]{2,1,0:T(8,128)(2,1)S(1)} async-done(((bf16[8,16,1280]{2,1,0:T(8,128)(2,1)}), bf16[8,16,1280]{2,1,0:T(8,128)(2,1)S(1)}, u32[]{:S(2)}, u32[]{:S(2)}) %all-to-all-start.2) | async-done | bytes 327712 | tf_op jit(solution)/shard_map/all_to_all | solution.py:363
  119.2 0.0 copy-done.2
  119.2 0.8 shard_map.81
  (2 shorter events, 0.0 us)
Async XLA Ops:
  2.9 59.3 %all-to-all-start = ((bf16[32,16,1280]{2,1,0:T(8,128)(2,1)}), bf16[32,16,1280]{2,1,0:T(8,128)(2,1)S(1)}, u32[]{:S(2)}, u32[]{:S(2)}) async-start(bf16[32,16,1280]{2,1,0:T(8,128)(2,1)} %get-tuple-element.21), calls=%async_computation | async-start | bytes 2621440 | tf_op jit(solution)/shard_map/all_to_all | solution.py:279
  59.0 6.0 %collective-permute-start = (bf16[256,1280]{1,0:T(8,128)(2,1)S(1)}, bf16[256,1280]{1,0:T(8,128)(2,1)S(1)}, u32[]{:S(2)}, u32[]{:S(2)}) collective-permute-start(bf16[256,1280]{1,0:T(8,128)(2,1)S(1)} %all_gather.3.mine_ref), channel_id=1, source_target_pairs={{0,32},{32,0},{1,33},{33,1},{2,34},{34,2},{3,35},{35,3},{4,36},{36... | collective-permute-start | bytes 1966088 | tf_op jit(solution)/shard_map/ppermute | solution.py:256
  68.8 9.5 %copy-start = (f32[256,1280]{1,0:T(8,128)S(1)}, f32[256,1280]{1,0:T(8,128)}, u32[]{:S(2)}) copy-start(f32[256,1280]{1,0:T(8,128)} %get-tuple-element.22.keep_ref) | copy-start | bytes 3932164
  68.8 23.1 %all-to-all-start.1 = ((bf16[32,16,1152]{2,1,0:T(8,128)(2,1)}), bf16[32,16,1152]{2,1,0:T(8,128)(2,1)S(1)}, u32[]{:S(2)}, u32[]{:S(2)}) async-start(bf16[32,16,1152]{2,1,0:T(8,128)(2,1)} %get-tuple-element.28), calls=%async_computation.1 | async-start | bytes 2359296 | tf_op jit(solution)/shard_map/all_to_all | solution.py:323
  74.1 4.2 %collective-permute-start.1 = (bf16[256,1280]{1,0:T(8,128)(2,1)}, bf16[256,1280]{1,0:T(8,128)(2,1)S(1)}, u32[]{:S(2)}, u32[]{:S(2)}) collective-permute-start(bf16[256,1280]{1,0:T(8,128)(2,1)} %get-tuple-element.24), channel_id=1, source_target_pairs={{0,32},{32,0},{1,33},{33,1},{2,34},{34,2},{3,35},{35,3},{4,36},{36... | collective-permute-start | bytes 1966088 | tf_op jit(solution)/shard_map/ppermute | solution.py:256
  78.5 8.2 %collective-permute-start.2 = (bf16[128,640]{1,0:T(8,128)(2,1)S(1)}, bf16[128,640]{1,0:T(8,128)(2,1)S(1)}, u32[]{:S(2)}, u32[]{:S(2)}) collective-permute-start(bf16[128,640]{1,0:T(8,128)(2,1)S(1)} %get-tuple-element.26), channel_id=1, source_target_pairs={{0,1},{1,0},{2,3},{3,2},{4,5},{5,4},{6,7},{7,6},{8,9},{9,8},{10,11... | collective-permute-start | bytes 491528 | tf_op jit(solution)/shard_map/ppermute | solution.py:334
  80.4 9.4 %collective-permute-start.3 = (bf16[128,640]{1,0:T(8,128)(2,1)S(1)}, bf16[128,640]{1,0:T(8,128)(2,1)S(1)}, u32[]{:S(2)}, u32[]{:S(2)}) collective-permute-start(bf16[128,640]{1,0:T(8,128)(2,1)S(1)} %get-tuple-element.27), channel_id=1, source_target_pairs={{0,15},{1,2},{2,1},{3,4},{4,3},{5,6},{6,5},{7,8},{8,7},{9,10},{10,... | collective-permute-start | bytes 491528 | tf_op jit(solution)/shard_map/ppermute | solution.py:335
  90.7 22.4 %copy-start.1 = (bf16[16,1152]{1,0:T(8,128)(2,1)S(1)}, bf16[16,1152]{1,0:T(8,128)(2,1)}, u32[]{:S(2)}) copy-start(bf16[16,1152]{1,0:T(8,128)(2,1)} %embed_ref.3) | copy-start | bytes 110596
  90.7 28.5 %copy-start.2 = (bf16[16,1152]{1,0:T(8,128)(2,1)S(1)}, bf16[16,1152]{1,0:T(8,128)(2,1)}, u32[]{:S(2)}) copy-start(bf16[16,1152]{1,0:T(8,128)(2,1)} %embed_ref.2) | copy-start | bytes 110596
  91.9 27.3 %all-to-all-start.2 = ((bf16[8,16,1280]{2,1,0:T(8,128)(2,1)}), bf16[8,16,1280]{2,1,0:T(8,128)(2,1)S(1)}, u32[]{:S(2)}, u32[]{:S(2)}) async-start(bf16[8,16,1280]{2,1,0:T(8,128)(2,1)} %shard_map.80), calls=%async_computation.2 | async-start | bytes 655360 | tf_op jit(solution)/shard_map/all_to_all | solution.py:363
  96.0 7.2 %collective-permute-start.4 = (bf16[2,16,1152]{2,1,0:T(8,128)(2,1)S(1)}, bf16[2,16,1152]{2,1,0:T(8,128)(2,1)S(1)}, u32[]{:S(2)}, u32[]{:S(2)}) collective-permute-start(bf16[2,16,1152]{2,1,0:T(8,128)(2,1)S(1)} %get-tuple-element.33), channel_id=1, source_target_pairs={{0,64},{64,0},{128,192},{192,128},{1,65},{65,1},{129,193},{193,129... | collective-permute-start | bytes 221192 | tf_op jit(solution)/shard_map/ppermute | solution.py:354
  103.2 9.9 %collective-permute-start.5 = (bf16[16,1152]{1,0:T(8,128)(2,1)S(1)}, bf16[16,1152]{1,0:T(8,128)(2,1)S(1)}, u32[]{:S(2)}, u32[]{:S(2)}) collective-permute-start(bf16[16,1152]{1,0:T(8,128)(2,1)S(1)} %get-tuple-element.35), channel_id=1, source_target_pairs={{0,128},{64,192},{128,0},{192,64},{1,129},{65,193},{129,1},{193,65... | collective-permute-start | bytes 110600 | tf_op jit(solution)/shard_map/ppermute | solution.py:361

commit v5 on v4

--- a/solution.py
+++ b/solution.py
@@ -80,12 +80,16 @@
         return out.astype(F32).astype(BF16)
 
     wait(text_copy)
-    text_wide[:, :WIDTH] = unit_of(text_now[...])[0].astype(BF16)
-    text_wide[:, WIDTH:] = features((high, low, LABEL_BASE, 1, norm_high, norm_low))
+    text_low = unit_of(text_now[...])[0].astype(BF16)
+    marks = features((high, low, LABEL_BASE, 1, norm_high, norm_low))
+    copies = text_wide.shape[0]
+    for k in range(copies):
+        text_wide[k, :, :WIDTH] = text_low
+        text_wide[k, :, WIDTH:] = marks
     copies = start(
         *[
-            pltpu.make_async_copy(text_wide, text_out.at[k], out_sem.at[k])
-            for k in range(text_out.shape[0])
+            pltpu.make_async_copy(text_wide, text_out.at[pl.ds(k * copies, copies)], out_sem.at[k])
+            for k in range(text_out.shape[0] // copies)
         ]
     )
     wait(image_copy)
@@ -118,14 +122,8 @@
 
 
 def first_tile(
-    log_temp_ref, bias_ref, mine_ref, text_ref, coeffs_out, keep_out, mine, text, coeffs_now, keep_now, in_sem, out_sem
+    log_temp_ref, bias_ref, mine, text, coeffs_out, keep_out, coeffs_now, keep_now, out_sem
 ):
-    wait(
-        *start(
-            pltpu.make_async_copy(mine_ref, mine, in_sem.at[0]),
-            pltpu.make_async_copy(text_ref, text, in_sem.at[1]),
-        )
-    )
     loss, coeffs = half_tile(log_temp_ref, bias_ref, mine, text)
     coeffs_now[...] = coeffs
     (coeffs_copy,) = start(pltpu.make_async_copy(coeffs_now, coeffs_out, out_sem.at[0]))
@@ -269,9 +267,9 @@
             pltpu.SMEM((ROWS,), jnp.int32),
             pltpu.VMEM((ROWS, WIDTH), BF16),
             pltpu.VMEM((ROWS, WIDTH), BF16),
-            pltpu.VMEM((ROWS, WIDE), BF16),
+            pltpu.VMEM((8, ROWS, WIDE), BF16),
             pltpu.SemaphoreType.DMA((3,)),
-            pltpu.SemaphoreType.DMA((plane,)),
+            pltpu.SemaphoreType.DMA((plane // 8,)),
         ],
         bytes_accessed=plane * ROWS * WIDE * 2,
     )(in_hbm(labels), in_hbm(image_embed), in_hbm(text_embed))
@@ -285,13 +283,10 @@
     coeffs, keep = call(
         first_tile,
         [(HBM, shape((half, texts), BF16)), (HBM, shape((half, WIDE), F32))],
-        [SMEM, SMEM, HBM, HBM],
+        [SMEM, SMEM, VMEM, VMEM],
         [
-            pltpu.VMEM((half, WIDE), BF16),
-            pltpu.VMEM((texts, WIDE), BF16),
             pltpu.VMEM((half, texts), BF16),
             pltpu.VMEM((half, WIDE), F32),
-            pltpu.SemaphoreType.DMA((2,)),
             pltpu.SemaphoreType.DMA((2,)),
         ],
         flops=4 * half * texts * WIDTH,

time: 121 us -> 120 us (level)
  no operation moved by 1% of the time
where the time goes in v5:
time: 120 us; the launch traced here: 119 us
  starting transfers between devices  41.7 us (35%)
  blocking collectives  39.5 us (33%)
  waiting for transfers between devices  25 us (21%)
  Pallas kernels  11.2 us (9%)
  between operations  2.08 us (2%)
    all_gather x1, blocking collectives, on_device(): mine = lax.all_gather(image_wide, COLUMN, axis=0, tiled=True)  39.5 us
    all_to_all x1, starting transfers between devices, on_device(): lax.all_to_all(text_wide, PLANE, 0, 0, tiled=True).reshape(-1, WIDE)  16.6 us
    all_to_all x1, starting transfers between devices, on_device(): text_terms = lax.all_to_all(text_part, ('x', 'y_lo'), 0, 0, tiled=True)  5.3 us
    all_to_all x1, waiting for transfers between devices, on_device(): image_terms = lax.all_to_all(image_terms, 'z_hi', 0, 0, tiled=True)  5.27 us
    ppermute x1, waiting for transfers between devices, on_device(): text_got = lax.ppermute(text_give, 'y_hi', [(i, i ^ 2) for i in range(far)])  5.13 us
    ppermute x1, starting transfers between devices, on_device(): text_got = lax.ppermute(text_give, 'y_hi', [(i, i ^ 2) for i in range(far)])  4.72 us
    ppermute x1, waiting for transfers between devices, on_device(): text_got = lax.ppermute(text_give, 'y_hi', [(i, i ^ 1) for i in range(far)])  4.65 us
    ppermute x2, starting transfers between devices, swap_cores(): return lax.ppermute(part, 'core', [(0, 1), (1, 0)])  4.02 us
  transfers between devices with their start and end apart: 9, of which 7 were waited for; matrix products, arithmetic and copies ran while one was open for 0% of the time, Pallas kernels for 4%

profile of v5, /device:TPU:16, one launch (start us, length us, event | category | flops | bytes accessed | tf_op | source)
XLA Modules:
  0.0 119.5 jit_solution(8863093250279468819)
XLA Ops:
  0.6 2.0 %shard_map.76 = (bf16[16,1280]{1,0:T(8,128)(2,1)S(1)}, bf16[32,16,1280]{2,1,0:T(8,128)(2,1)}) custom-call(s32[16]{0:T(128)} %labels_ref.1, bf16[16,1152]{1,0:T(8,128)(2,1)} %embed_ref.2, bf16[16,1152]{1,0:T(8,128)(2,1)} %embed_ref.3), custom_call_target="tpu_custom_call" | custom-call | bytes 1310720 | tf_op jit(solution)/shard_map/pallas_call | solution.py:262
  2.7 16.6 %all-to-all-start = ((bf16[32,16,1280]{2,1,0:T(8,128)(2,1)}), bf16[32,16,1280]{2,1,0:T(8,128)(2,1)S(1)}, u32[]{:S(2)}, u32[]{:S(2)}) async-start(bf16[32,16,1280]{2,1,0:T(8,128)(2,1)} %get-tuple-element.21), calls=%async_computation | async-start | bytes 2621440 | tf_op jit(solution)/shard_map/all_to_all | solution.py:277
  19.3 39.5 %all_gather.3.mine.mine_ref = bf16[256,1280]{1,0:T(8,128)(2,1)S(1)} all-gather(bf16[16,1280]{1,0:T(8,128)(2,1)S(1)} %get-tuple-element.20), channel_id=1, replica_groups=mesh['x'=4,'y_hi'=4,'core'=2,'y_lo'=2,'z_hi'=8,'z_lo'=2] {'z_hi','z_lo'}, dimensions={0}, use_global_device_ids=true | all-gather | bytes 696320 | tf_op jit(solution)/shard_map/all_gather | solution.py:278
  58.8 1.9 %collective-permute-start = (bf16[256,1280]{1,0:T(8,128)(2,1)S(1)}, bf16[256,1280]{1,0:T(8,128)(2,1)S(1)}, u32[]{:S(2)}, u32[]{:S(2)}) collective-permute-start(bf16[256,1280]{1,0:T(8,128)(2,1)S(1)} %all_gather.3.mine.mine_ref), channel_id=1, source_target_pairs={{0,32},{32,0},{1,33},{33,1},{2,34},{34,2},{3,35},{35,3},{4,36},{36... | collective-permute-start | bytes 1966088 | tf_op jit(solution)/shard_map/ppermute | solution.py:254
  62.0 0.0 all-to-all-done
  62.0 2.5 %shard_map.77 = (bf16[256,512]{1,0:T(8,128)(2,1)}, f32[256,1280]{1,0:T(8,128)}) custom-call(f32[1]{0:T(128)S(6)} %copy.8.log_temp_ref, f32[1]{0:T(128)S(6)} %copy.9.bias_ref, bf16[256,1280]{1,0:T(8,128)(2,1)S(1)} %all_gather.3.mine.mine_ref, bf16[512,1280]{1,0:T(8,128)(2,1)S(1)} %bitcast.7), custom_call_target="tpu_custom_call" | custom-call | flops 603979776 | bytes 2621440 | tf_op jit(solution)/shard_map/pallas_call | solution.py:283
  64.5 0.0 collective-permute-done.other_ref
  64.5 3.8 %shard_map.78 = (bf16[256,1280]{1,0:T(8,128)(2,1)}, bf16[32,16,1152]{2,1,0:T(8,128)(2,1)}) custom-call(f32[1]{0:T(128)S(6)} %copy.8.log_temp_ref, f32[1]{0:T(128)S(6)} %copy.9.bias_ref, bf16[256,1280]{1,0:T(8,128)(2,1)S(1)} %collective-permute-done.other_ref, bf16[512,1280]{1,0:T(8,128)(2,1)S(1)} %bitcast.8, bf16[256,1280]{1,0:T(8,128)(2,1)S(1)} %all_gather.3.mine.mine_ref, ...), custom_call_target="tpu_custom_call" | custom-call | flops 1207959552 | bytes 3932160 | tf_op jit(solution)/shard_map/pallas_call | solution.py:299
  68.2 0.0 copy-start
  68.3 5.3 %all-to-all-start.1 = ((bf16[32,16,1152]{2,1,0:T(8,128)(2,1)}), bf16[32,16,1152]{2,1,0:T(8,128)(2,1)S(1)}, u32[]{:S(2)}, u32[]{:S(2)}) async-start(bf16[32,16,1152]{2,1,0:T(8,128)(2,1)} %get-tuple-element.28), calls=%async_computation.1 | async-start | bytes 2359296 | tf_op jit(solution)/shard_map/all_to_all | solution.py:318
  73.6 2.1 %collective-permute-start.1 = (bf16[256,1280]{1,0:T(8,128)(2,1)}, bf16[256,1280]{1,0:T(8,128)(2,1)S(1)}, u32[]{:S(2)}, u32[]{:S(2)}) collective-permute-start(bf16[256,1280]{1,0:T(8,128)(2,1)} %get-tuple-element.24), channel_id=1, source_target_pairs={{0,32},{32,0},{1,33},{33,1},{2,34},{34,2},{3,35},{35,3},{4,36},{36... | collective-permute-start | bytes 1966088 | tf_op jit(solution)/shard_map/ppermute | solution.py:254
  75.7 2.1 %collective-permute-done.1.got_ref = bf16[256,1280]{1,0:T(8,128)(2,1)S(1)} collective-permute-done((bf16[256,1280]{1,0:T(8,128)(2,1)}, bf16[256,1280]{1,0:T(8,128)(2,1)S(1)}, u32[]{:S(2)}, u32[]{:S(2)}) %collective-permute-start.1) | collective-permute-done | bytes 655392 | tf_op jit(solution)/shard_map/ppermute | solution.py:254
  77.7 0.0 copy-done
  77.8 0.2 shard_map.79
  77.9 1.9 %collective-permute-start.2 = (bf16[128,640]{1,0:T(8,128)(2,1)S(1)}, bf16[128,640]{1,0:T(8,128)(2,1)S(1)}, u32[]{:S(2)}, u32[]{:S(2)}) collective-permute-start(bf16[128,640]{1,0:T(8,128)(2,1)S(1)} %get-tuple-element.26), channel_id=1, source_target_pairs={{0,1},{1,0},{2,3},{3,2},{4,5},{5,4},{6,7},{7,6},{8,9},{9,8},{10,11... | collective-permute-start | bytes 491528 | tf_op jit(solution)/shard_map/ppermute | solution.py:329
  79.9 2.7 %collective-permute-start.3 = (bf16[128,640]{1,0:T(8,128)(2,1)S(1)}, bf16[128,640]{1,0:T(8,128)(2,1)S(1)}, u32[]{:S(2)}, u32[]{:S(2)}) collective-permute-start(bf16[128,640]{1,0:T(8,128)(2,1)S(1)} %get-tuple-element.27), channel_id=1, source_target_pairs={{0,15},{1,2},{2,1},{3,4},{4,3},{5,6},{6,5},{7,8},{8,7},{9,10},{10,... | collective-permute-start | bytes 491528 | tf_op jit(solution)/shard_map/ppermute | solution.py:330
  82.6 3.6 %collective-permute-done.2.left_ref = bf16[128,640]{1,0:T(8,128)(2,1)S(1)} collective-permute-done((bf16[128,640]{1,0:T(8,128)(2,1)S(1)}, bf16[128,640]{1,0:T(8,128)(2,1)S(1)}, u32[]{:S(2)}, u32[]{:S(2)}) %collective-permute-start.2) | collective-permute-done | bytes 163872 | tf_op jit(solution)/shard_map/ppermute | solution.py:329
  86.1 3.1 %collective-permute-done.3.right_ref = bf16[128,640]{1,0:T(8,128)(2,1)S(1)} collective-permute-done((bf16[128,640]{1,0:T(8,128)(2,1)S(1)}, bf16[128,640]{1,0:T(8,128)(2,1)S(1)}, u32[]{:S(2)}, u32[]{:S(2)}) %collective-permute-start.3) | collective-permute-done | bytes 163872 | tf_op jit(solution)/shard_map/ppermute | solution.py:330
  89.3 0.9 shard_map.80
  90.2 0.0 copy-start.1
  90.2 0.0 copy-start.2
  90.2 1.2 all-to-all-done.1
  91.4 3.9 %all-to-all-start.2 = ((bf16[8,16,1280]{2,1,0:T(8,128)(2,1)}), bf16[8,16,1280]{2,1,0:T(8,128)(2,1)S(1)}, u32[]{:S(2)}, u32[]{:S(2)}) async-start(bf16[8,16,1280]{2,1,0:T(8,128)(2,1)} %shard_map.80), calls=%async_computation.2 | async-start | bytes 655360 | tf_op jit(solution)/shard_map/all_to_all | solution.py:358
  95.3 0.2 shard_map.82
  95.4 2.6 %collective-permute-start.4 = (bf16[2,16,1152]{2,1,0:T(8,128)(2,1)S(1)}, bf16[2,16,1152]{2,1,0:T(8,128)(2,1)S(1)}, u32[]{:S(2)}, u32[]{:S(2)}) collective-permute-start(bf16[2,16,1152]{2,1,0:T(8,128)(2,1)S(1)} %get-tuple-element.33), channel_id=1, source_target_pairs={{0,64},{64,0},{128,192},{192,128},{1,65},{65,1},{129,193},{193,129... | collective-permute-start | bytes 221192 | tf_op jit(solution)/shard_map/ppermute | solution.py:349
  98.0 4.7 %collective-permute-done.4.got_ref = bf16[2,16,1152]{2,1,0:T(8,128)(2,1)S(1)} collective-permute-done((bf16[2,16,1152]{2,1,0:T(8,128)(2,1)S(1)}, bf16[2,16,1152]{2,1,0:T(8,128)(2,1)S(1)}, u32[]{:S(2)}, u32[]{:S(2)}) %collective-permute-start.4) | collective-permute-done | bytes 73760 | tf_op jit(solution)/shard_map/ppermute | solution.py:349
  102.7 4.7 %collective-permute-start.5 = (bf16[16,1152]{1,0:T(8,128)(2,1)S(1)}, bf16[16,1152]{1,0:T(8,128)(2,1)S(1)}, u32[]{:S(2)}, u32[]{:S(2)}) collective-permute-start(bf16[16,1152]{1,0:T(8,128)(2,1)S(1)} %get-tuple-element.35), channel_id=1, source_target_pairs={{0,128},{64,192},{128,0},{192,64},{1,129},{65,193},{129,1},{193,65... | collective-permute-start | bytes 110600 | tf_op jit(solution)/shard_map/ppermute | solution.py:356
  107.4 5.1 %collective-permute-done.5.got_ref = bf16[16,1152]{1,0:T(8,128)(2,1)S(1)} collective-permute-done((bf16[16,1152]{1,0:T(8,128)(2,1)S(1)}, bf16[16,1152]{1,0:T(8,128)(2,1)S(1)}, u32[]{:S(2)}, u32[]{:S(2)}) %collective-permute-start.5) | collective-permute-done | bytes 36896 | tf_op jit(solution)/shard_map/ppermute | solution.py:356
  112.5 0.0 copy-done.1
  112.5 0.8 shard_map.84
  113.4 5.3 %all-to-all-done.2.terms_ref = bf16[8,16,1280]{2,1,0:T(8,128)(2,1)S(1)} async-done(((bf16[8,16,1280]{2,1,0:T(8,128)(2,1)}), bf16[8,16,1280]{2,1,0:T(8,128)(2,1)S(1)}, u32[]{:S(2)}, u32[]{:S(2)}) %all-to-all-start.2) | async-done | bytes 327712 | tf_op jit(solution)/shard_map/all_to_all | solution.py:358
  118.6 0.8 shard_map.81
  (2 shorter events, 0.0 us)
Async XLA Ops:
  2.7 59.3 %all-to-all-start = ((bf16[32,16,1280]{2,1,0:T(8,128)(2,1)}), bf16[32,16,1280]{2,1,0:T(8,128)(2,1)S(1)}, u32[]{:S(2)}, u32[]{:S(2)}) async-start(bf16[32,16,1280]{2,1,0:T(8,128)(2,1)} %get-tuple-element.21), calls=%async_computation | async-start | bytes 2621440 | tf_op jit(solution)/shard_map/all_to_all | solution.py:277
  58.8 5.7 %collective-permute-start = (bf16[256,1280]{1,0:T(8,128)(2,1)S(1)}, bf16[256,1280]{1,0:T(8,128)(2,1)S(1)}, u32[]{:S(2)}, u32[]{:S(2)}) collective-permute-start(bf16[256,1280]{1,0:T(8,128)(2,1)S(1)} %all_gather.3.mine.mine_ref), channel_id=1, source_target_pairs={{0,32},{32,0},{1,33},{33,1},{2,34},{34,2},{3,35},{35,3},{4,36},{36... | collective-permute-start | bytes 1966088 | tf_op jit(solution)/shard_map/ppermute | solution.py:254
  68.2 9.5 %copy-start = (f32[256,1280]{1,0:T(8,128)S(1)}, f32[256,1280]{1,0:T(8,128)}, u32[]{:S(2)}) copy-start(f32[256,1280]{1,0:T(8,128)} %get-tuple-element.22.keep_ref) | copy-start | bytes 3932164
  68.3 23.1 %all-to-all-start.1 = ((bf16[32,16,1152]{2,1,0:T(8,128)(2,1)}), bf16[32,16,1152]{2,1,0:T(8,128)(2,1)S(1)}, u32[]{:S(2)}, u32[]{:S(2)}) async-start(bf16[32,16,1152]{2,1,0:T(8,128)(2,1)} %get-tuple-element.28), calls=%async_computation.1 | async-start | bytes 2359296 | tf_op jit(solution)/shard_map/all_to_all | solution.py:318
  73.6 4.2 %collective-permute-start.1 = (bf16[256,1280]{1,0:T(8,128)(2,1)}, bf16[256,1280]{1,0:T(8,128)(2,1)S(1)}, u32[]{:S(2)}, u32[]{:S(2)}) collective-permute-start(bf16[256,1280]{1,0:T(8,128)(2,1)} %get-tuple-element.24), channel_id=1, source_target_pairs={{0,32},{32,0},{1,33},{33,1},{2,34},{34,2},{3,35},{35,3},{4,36},{36... | collective-permute-start | bytes 1966088 | tf_op jit(solution)/shard_map/ppermute | solution.py:254
  77.9 8.2 %collective-permute-start.2 = (bf16[128,640]{1,0:T(8,128)(2,1)S(1)}, bf16[128,640]{1,0:T(8,128)(2,1)S(1)}, u32[]{:S(2)}, u32[]{:S(2)}) collective-permute-start(bf16[128,640]{1,0:T(8,128)(2,1)S(1)} %get-tuple-element.26), channel_id=1, source_target_pairs={{0,1},{1,0},{2,3},{3,2},{4,5},{5,4},{6,7},{7,6},{8,9},{9,8},{10,11... | collective-permute-start | bytes 491528 | tf_op jit(solution)/shard_map/ppermute | solution.py:329
  79.9 9.4 %collective-permute-start.3 = (bf16[128,640]{1,0:T(8,128)(2,1)S(1)}, bf16[128,640]{1,0:T(8,128)(2,1)S(1)}, u32[]{:S(2)}, u32[]{:S(2)}) collective-permute-start(bf16[128,640]{1,0:T(8,128)(2,1)S(1)} %get-tuple-element.27), channel_id=1, source_target_pairs={{0,15},{1,2},{2,1},{3,4},{4,3},{5,6},{6,5},{7,8},{8,7},{9,10},{10,... | collective-permute-start | bytes 491528 | tf_op jit(solution)/shard_map/ppermute | solution.py:330
  90.2 22.4 %copy-start.1 = (bf16[16,1152]{1,0:T(8,128)(2,1)S(1)}, bf16[16,1152]{1,0:T(8,128)(2,1)}, u32[]{:S(2)}) copy-start(bf16[16,1152]{1,0:T(8,128)(2,1)} %embed_ref.3) | copy-start | bytes 110596
  90.2 28.4 %copy-start.2 = (bf16[16,1152]{1,0:T(8,128)(2,1)S(1)}, bf16[16,1152]{1,0:T(8,128)(2,1)}, u32[]{:S(2)}) copy-start(bf16[16,1152]{1,0:T(8,128)(2,1)} %embed_ref.2) | copy-start | bytes 110596
  91.4 27.3 %all-to-all-start.2 = ((bf16[8,16,1280]{2,1,0:T(8,128)(2,1)}), bf16[8,16,1280]{2,1,0:T(8,128)(2,1)S(1)}, u32[]{:S(2)}, u32[]{:S(2)}) async-start(bf16[8,16,1280]{2,1,0:T(8,128)(2,1)} %shard_map.80), calls=%async_computation.2 | async-start | bytes 655360 | tf_op jit(solution)/shard_map/all_to_all | solution.py:358
  95.4 7.2 %collective-permute-start.4 = (bf16[2,16,1152]{2,1,0:T(8,128)(2,1)S(1)}, bf16[2,16,1152]{2,1,0:T(8,128)(2,1)S(1)}, u32[]{:S(2)}, u32[]{:S(2)}) collective-permute-start(bf16[2,16,1152]{2,1,0:T(8,128)(2,1)S(1)} %get-tuple-element.33), channel_id=1, source_target_pairs={{0,64},{64,0},{128,192},{192,128},{1,65},{65,1},{129,193},{193,129... | collective-permute-start | bytes 221192 | tf_op jit(solution)/shard_map/ppermute | solution.py:349
  102.7 9.9 %collective-permute-start.5 = (bf16[16,1152]{1,0:T(8,128)(2,1)S(1)}, bf16[16,1152]{1,0:T(8,128)(2,1)S(1)}, u32[]{:S(2)}, u32[]{:S(2)}) collective-permute-start(bf16[16,1152]{1,0:T(8,128)(2,1)S(1)} %get-tuple-element.35), channel_id=1, source_target_pairs={{0,128},{64,192},{128,0},{192,64},{1,129},{65,193},{129,1},{193,65... | collective-permute-start | bytes 110600 | tf_op jit(solution)/shard_map/ppermute | solution.py:356

commit v6 on v5

--- a/solution.py
+++ b/solution.py
@@ -295,7 +295,8 @@
 
     far, low = lax.axis_size("y_hi"), lax.axis_size("y_lo")
     near = plane // far
-    order = [((b // low // far) * low + b % low) * far + (b // low) % far for b in range(plane)]
+    wide = plane // far // low
+    order = [((b % low) * wide + b // low // far) * far + (b // low) % far for b in range(plane)]
     give, text_part = call(
         functools.partial(second_tile, order),
         [(HBM, shape((half, WIDE), BF16)), (HBM, shape((plane, ROWS, WIDTH), BF16))],
@@ -315,7 +316,7 @@
         bytes_accessed=6 * texts * WIDE,
     )(log_temp, bias, other, group_text, mine, in_hbm(coeffs))
 
-    text_terms = lax.all_to_all(text_part, ("x", "y_lo"), 0, 0, tiled=True)
+    text_terms = lax.all_to_all(text_part, ("y_lo", "x"), 0, 0, tiled=True)
     got = swap_cores(give)
     blocks = lax.axis_size("z_hi")
     rows = blocks * ROWS

time: 120 us -> 120 us (level)
  the two profiles are of different devices: /device:TPU:16 before, /device:TPU:8 now
where the time goes in v6:
time: 120 us; the launch traced here: 119 us
  starting transfers between devices  45.9 us (38%)
  blocking collectives  39.5 us (33%)
  waiting for transfers between devices  20.2 us (17%)
  Pallas kernels  11.2 us (9%)
  between operations  2.09 us (2%)
    all_gather x1, blocking collectives, on_device(): mine = lax.all_gather(image_wide, COLUMN, axis=0, tiled=True)  39.5 us
    all_to_all x1, starting transfers between devices, on_device(): lax.all_to_all(text_wide, PLANE, 0, 0, tiled=True).reshape(-1, WIDE)  16.7 us
    ppermute x1, starting transfers between devices, on_device(): text_got = lax.ppermute(text_give, 'y_hi', [(i, i ^ 2) for i in range(far)])  6.4 us
    all_to_all x1, starting transfers between devices, on_device(): text_terms = lax.all_to_all(text_part, ('y_lo', 'x'), 0, 0, tiled=True)  5.95 us
    all_to_all x1, waiting for transfers between devices, on_device(): image_terms = lax.all_to_all(image_terms, 'z_hi', 0, 0, tiled=True)  5.14 us
    ppermute x1, starting transfers between devices, on_device(): text_got = lax.ppermute(text_give, 'y_hi', [(i, i ^ 1) for i in range(far)])  4.27 us
    all_to_all x1, starting transfers between devices, on_device(): image_terms = lax.all_to_all(image_terms, 'z_hi', 0, 0, tiled=True)  4.16 us
    ppermute x2, starting transfers between devices, swap_cores(): return lax.ppermute(part, 'core', [(0, 1), (1, 0)])  3.82 us
  transfers between devices with their start and end apart: 9, of which 6 were waited for; matrix products, arithmetic and copies ran while one was open for 0% of the time, Pallas kernels for 4%

profile of v6, /device:TPU:8, one launch (start us, length us, event | category | flops | bytes accessed | tf_op | source)
XLA Modules:
  0.0 119.0 jit_solution(10949177381834645812)
XLA Ops:
  0.6 2.0 %shard_map.76 = (bf16[16,1280]{1,0:T(8,128)(2,1)S(1)}, bf16[32,16,1280]{2,1,0:T(8,128)(2,1)}) custom-call(s32[16]{0:T(128)} %labels_ref.1, bf16[16,1152]{1,0:T(8,128)(2,1)} %embed_ref.2, bf16[16,1152]{1,0:T(8,128)(2,1)} %embed_ref.3), custom_call_target="tpu_custom_call" | custom-call | bytes 1310720 | tf_op jit(solution)/shard_map/pallas_call | solution.py:262
  2.7 16.7 %all-to-all-start = ((bf16[32,16,1280]{2,1,0:T(8,128)(2,1)}), bf16[32,16,1280]{2,1,0:T(8,128)(2,1)S(1)}, u32[]{:S(2)}, u32[]{:S(2)}) async-start(bf16[32,16,1280]{2,1,0:T(8,128)(2,1)} %get-tuple-element.21), calls=%async_computation | async-start | bytes 2621440 | tf_op jit(solution)/shard_map/all_to_all | solution.py:277
  19.4 39.5 %all_gather.3.mine.mine_ref = bf16[256,1280]{1,0:T(8,128)(2,1)S(1)} all-gather(bf16[16,1280]{1,0:T(8,128)(2,1)S(1)} %get-tuple-element.20), channel_id=1, replica_groups=mesh['x'=4,'y_hi'=4,'core'=2,'y_lo'=2,'z_hi'=8,'z_lo'=2] {'z_hi','z_lo'}, dimensions={0}, use_global_device_ids=true | all-gather | bytes 696320 | tf_op jit(solution)/shard_map/all_gather | solution.py:278
  58.9 1.9 %collective-permute-start = (bf16[256,1280]{1,0:T(8,128)(2,1)S(1)}, bf16[256,1280]{1,0:T(8,128)(2,1)S(1)}, u32[]{:S(2)}, u32[]{:S(2)}) collective-permute-start(bf16[256,1280]{1,0:T(8,128)(2,1)S(1)} %all_gather.3.mine.mine_ref), channel_id=1, source_target_pairs={{0,32},{32,0},{1,33},{33,1},{2,34},{34,2},{3,35},{35,3},{4,36},{36... | collective-permute-start | bytes 1966088 | tf_op jit(solution)/shard_map/ppermute | solution.py:254
  62.1 0.0 all-to-all-done
  62.1 2.5 %shard_map.77 = (bf16[256,512]{1,0:T(8,128)(2,1)}, f32[256,1280]{1,0:T(8,128)}) custom-call(f32[1]{0:T(128)S(6)} %copy.8.log_temp_ref, f32[1]{0:T(128)S(6)} %copy.9.bias_ref, bf16[256,1280]{1,0:T(8,128)(2,1)S(1)} %all_gather.3.mine.mine_ref, bf16[512,1280]{1,0:T(8,128)(2,1)S(1)} %bitcast.7), custom_call_target="tpu_custom_call" | custom-call | flops 603979776 | bytes 2621440 | tf_op jit(solution)/shard_map/pallas_call | solution.py:283
  64.6 0.0 collective-permute-done.other_ref
  64.6 3.8 %shard_map.78 = (bf16[256,1280]{1,0:T(8,128)(2,1)}, bf16[32,16,1152]{2,1,0:T(8,128)(2,1)}) custom-call(f32[1]{0:T(128)S(6)} %copy.8.log_temp_ref, f32[1]{0:T(128)S(6)} %copy.9.bias_ref, bf16[256,1280]{1,0:T(8,128)(2,1)S(1)} %collective-permute-done.other_ref, bf16[512,1280]{1,0:T(8,128)(2,1)S(1)} %bitcast.8, bf16[256,1280]{1,0:T(8,128)(2,1)S(1)} %all_gather.3.mine.mine_ref, ...), custom_call_target="tpu_custom_call" | custom-call | flops 1207959552 | bytes 3932160 | tf_op jit(solution)/shard_map/pallas_call | solution.py:300
  68.4 0.0 copy-start
  68.4 5.9 %all-to-all-start.1 = ((bf16[32,16,1152]{2,1,0:T(8,128)(2,1)}), bf16[32,16,1152]{2,1,0:T(8,128)(2,1)S(1)}, u32[]{:S(2)}, u32[]{:S(2)}) async-start(bf16[32,16,1152]{2,1,0:T(8,128)(2,1)} %get-tuple-element.28), calls=%async_computation.1 | async-start | bytes 2359296 | tf_op jit(solution)/shard_map/all_to_all | solution.py:319
  74.3 1.9 %collective-permute-start.1 = (bf16[256,1280]{1,0:T(8,128)(2,1)}, bf16[256,1280]{1,0:T(8,128)(2,1)S(1)}, u32[]{:S(2)}, u32[]{:S(2)}) collective-permute-start(bf16[256,1280]{1,0:T(8,128)(2,1)} %get-tuple-element.24), channel_id=1, source_target_pairs={{0,32},{32,0},{1,33},{33,1},{2,34},{34,2},{3,35},{35,3},{4,36},{36... | collective-permute-start | bytes 1966088 | tf_op jit(solution)/shard_map/ppermute | solution.py:254
  76.3 2.3 %collective-permute-done.1.got_ref = bf16[256,1280]{1,0:T(8,128)(2,1)S(1)} collective-permute-done((bf16[256,1280]{1,0:T(8,128)(2,1)}, bf16[256,1280]{1,0:T(8,128)(2,1)S(1)}, u32[]{:S(2)}, u32[]{:S(2)}) %collective-permute-start.1) | collective-permute-done | bytes 655392 | tf_op jit(solution)/shard_map/ppermute | solution.py:254
  78.5 0.0 copy-done
  78.5 0.2 shard_map.79
  78.7 1.9 %collective-permute-start.2 = (bf16[128,640]{1,0:T(8,128)(2,1)S(1)}, bf16[128,640]{1,0:T(8,128)(2,1)S(1)}, u32[]{:S(2)}, u32[]{:S(2)}) collective-permute-start(bf16[128,640]{1,0:T(8,128)(2,1)S(1)} %get-tuple-element.26), channel_id=1, source_target_pairs={{0,1},{1,0},{2,3},{3,2},{4,5},{5,4},{6,7},{7,6},{8,9},{9,8},{10,11... | collective-permute-start | bytes 491528 | tf_op jit(solution)/shard_map/ppermute | solution.py:330
  80.6 2.7 %collective-permute-start.3 = (bf16[128,640]{1,0:T(8,128)(2,1)S(1)}, bf16[128,640]{1,0:T(8,128)(2,1)S(1)}, u32[]{:S(2)}, u32[]{:S(2)}) collective-permute-start(bf16[128,640]{1,0:T(8,128)(2,1)S(1)} %get-tuple-element.27), channel_id=1, source_target_pairs={{0,15},{1,2},{2,1},{3,4},{4,3},{5,6},{6,5},{7,8},{8,7},{9,10},{10,... | collective-permute-start | bytes 491528 | tf_op jit(solution)/shard_map/ppermute | solution.py:331
  83.4 3.5 %collective-permute-done.2.left_ref = bf16[128,640]{1,0:T(8,128)(2,1)S(1)} collective-permute-done((bf16[128,640]{1,0:T(8,128)(2,1)S(1)}, bf16[128,640]{1,0:T(8,128)(2,1)S(1)}, u32[]{:S(2)}, u32[]{:S(2)}) %collective-permute-start.2) | collective-permute-done | bytes 163872 | tf_op jit(solution)/shard_map/ppermute | solution.py:330
  86.8 3.1 %collective-permute-done.3.right_ref = bf16[128,640]{1,0:T(8,128)(2,1)S(1)} collective-permute-done((bf16[128,640]{1,0:T(8,128)(2,1)S(1)}, bf16[128,640]{1,0:T(8,128)(2,1)S(1)}, u32[]{:S(2)}, u32[]{:S(2)}) %collective-permute-start.3) | collective-permute-done | bytes 163872 | tf_op jit(solution)/shard_map/ppermute | solution.py:331
  90.0 0.9 shard_map.80
  90.9 0.0 copy-start.1
  90.9 0.0 copy-start.2
  90.9 0.0 all-to-all-done.1
  90.9 4.2 %all-to-all-start.2 = ((bf16[8,16,1280]{2,1,0:T(8,128)(2,1)}), bf16[8,16,1280]{2,1,0:T(8,128)(2,1)S(1)}, u32[]{:S(2)}, u32[]{:S(2)}) async-start(bf16[8,16,1280]{2,1,0:T(8,128)(2,1)} %shard_map.80), calls=%async_computation.2 | async-start | bytes 655360 | tf_op jit(solution)/shard_map/all_to_all | solution.py:359
  95.1 0.2 shard_map.82
  95.2 4.3 %collective-permute-start.4 = (bf16[2,16,1152]{2,1,0:T(8,128)(2,1)S(1)}, bf16[2,16,1152]{2,1,0:T(8,128)(2,1)S(1)}, u32[]{:S(2)}, u32[]{:S(2)}) collective-permute-start(bf16[2,16,1152]{2,1,0:T(8,128)(2,1)S(1)} %get-tuple-element.33), channel_id=1, source_target_pairs={{0,64},{64,0},{128,192},{192,128},{1,65},{65,1},{129,193},{193,129... | collective-permute-start | bytes 221192 | tf_op jit(solution)/shard_map/ppermute | solution.py:350
  99.5 2.9 %collective-permute-done.4.got_ref = bf16[2,16,1152]{2,1,0:T(8,128)(2,1)S(1)} collective-permute-done((bf16[2,16,1152]{2,1,0:T(8,128)(2,1)S(1)}, bf16[2,16,1152]{2,1,0:T(8,128)(2,1)S(1)}, u32[]{:S(2)}, u32[]{:S(2)}) %collective-permute-start.4) | collective-permute-done | bytes 73760 | tf_op jit(solution)/shard_map/ppermute | solution.py:350
  102.4 6.4 %collective-permute-start.5 = (bf16[16,1152]{1,0:T(8,128)(2,1)S(1)}, bf16[16,1152]{1,0:T(8,128)(2,1)S(1)}, u32[]{:S(2)}, u32[]{:S(2)}) collective-permute-start(bf16[16,1152]{1,0:T(8,128)(2,1)S(1)} %get-tuple-element.35), channel_id=1, source_target_pairs={{0,128},{64,192},{128,0},{192,64},{1,129},{65,193},{129,1},{193,65... | collective-permute-start | bytes 110600 | tf_op jit(solution)/shard_map/ppermute | solution.py:357
  108.8 3.4 %collective-permute-done.5.got_ref = bf16[16,1152]{1,0:T(8,128)(2,1)S(1)} collective-permute-done((bf16[16,1152]{1,0:T(8,128)(2,1)S(1)}, bf16[16,1152]{1,0:T(8,128)(2,1)S(1)}, u32[]{:S(2)}, u32[]{:S(2)}) %collective-permute-start.5) | collective-permute-done | bytes 36896 | tf_op jit(solution)/shard_map/ppermute | solution.py:357
  112.2 0.0 copy-done.1
  112.2 0.8 shard_map.84
  113.0 5.1 %all-to-all-done.2.terms_ref = bf16[8,16,1280]{2,1,0:T(8,128)(2,1)S(1)} async-done(((bf16[8,16,1280]{2,1,0:T(8,128)(2,1)}), bf16[8,16,1280]{2,1,0:T(8,128)(2,1)S(1)}, u32[]{:S(2)}, u32[]{:S(2)}) %all-to-all-start.2) | async-done | bytes 327712 | tf_op jit(solution)/shard_map/all_to_all | solution.py:359
  118.1 0.8 shard_map.81
  (2 shorter events, 0.0 us)
Async XLA Ops:
  2.7 59.4 %all-to-all-start = ((bf16[32,16,1280]{2,1,0:T(8,128)(2,1)}), bf16[32,16,1280]{2,1,0:T(8,128)(2,1)S(1)}, u32[]{:S(2)}, u32[]{:S(2)}) async-start(bf16[32,16,1280]{2,1,0:T(8,128)(2,1)} %get-tuple-element.21), calls=%async_computation | async-start | bytes 2621440 | tf_op jit(solution)/shard_map/all_to_all | solution.py:277
  58.9 5.7 %collective-permute-start = (bf16[256,1280]{1,0:T(8,128)(2,1)S(1)}, bf16[256,1280]{1,0:T(8,128)(2,1)S(1)}, u32[]{:S(2)}, u32[]{:S(2)}) collective-permute-start(bf16[256,1280]{1,0:T(8,128)(2,1)S(1)} %all_gather.3.mine.mine_ref), channel_id=1, source_target_pairs={{0,32},{32,0},{1,33},{33,1},{2,34},{34,2},{3,35},{35,3},{4,36},{36... | collective-permute-start | bytes 1966088 | tf_op jit(solution)/shard_map/ppermute | solution.py:254
  68.4 10.2 %copy-start = (f32[256,1280]{1,0:T(8,128)S(1)}, f32[256,1280]{1,0:T(8,128)}, u32[]{:S(2)}) copy-start(f32[256,1280]{1,0:T(8,128)} %get-tuple-element.22.keep_ref) | copy-start | bytes 3932164
  68.4 22.5 %all-to-all-start.1 = ((bf16[32,16,1152]{2,1,0:T(8,128)(2,1)}), bf16[32,16,1152]{2,1,0:T(8,128)(2,1)S(1)}, u32[]{:S(2)}, u32[]{:S(2)}) async-start(bf16[32,16,1152]{2,1,0:T(8,128)(2,1)} %get-tuple-element.28), calls=%async_computation.1 | async-start | bytes 2359296 | tf_op jit(solution)/shard_map/all_to_all | solution.py:319
  74.3 4.2 %collective-permute-start.1 = (bf16[256,1280]{1,0:T(8,128)(2,1)}, bf16[256,1280]{1,0:T(8,128)(2,1)S(1)}, u32[]{:S(2)}, u32[]{:S(2)}) collective-permute-start(bf16[256,1280]{1,0:T(8,128)(2,1)} %get-tuple-element.24), channel_id=1, source_target_pairs={{0,32},{32,0},{1,33},{33,1},{2,34},{34,2},{3,35},{35,3},{4,36},{36... | collective-permute-start | bytes 1966088 | tf_op jit(solution)/shard_map/ppermute | solution.py:254
  78.7 8.1 %collective-permute-start.2 = (bf16[128,640]{1,0:T(8,128)(2,1)S(1)}, bf16[128,640]{1,0:T(8,128)(2,1)S(1)}, u32[]{:S(2)}, u32[]{:S(2)}) collective-permute-start(bf16[128,640]{1,0:T(8,128)(2,1)S(1)} %get-tuple-element.26), channel_id=1, source_target_pairs={{0,1},{1,0},{2,3},{3,2},{4,5},{5,4},{6,7},{7,6},{8,9},{9,8},{10,11... | collective-permute-start | bytes 491528 | tf_op jit(solution)/shard_map/ppermute | solution.py:330
  80.6 9.3 %collective-permute-start.3 = (bf16[128,640]{1,0:T(8,128)(2,1)S(1)}, bf16[128,640]{1,0:T(8,128)(2,1)S(1)}, u32[]{:S(2)}, u32[]{:S(2)}) collective-permute-start(bf16[128,640]{1,0:T(8,128)(2,1)S(1)} %get-tuple-element.27), channel_id=1, source_target_pairs={{0,15},{1,2},{2,1},{3,4},{4,3},{5,6},{6,5},{7,8},{8,7},{9,10},{10,... | collective-permute-start | bytes 491528 | tf_op jit(solution)/shard_map/ppermute | solution.py:331
  90.9 21.3 %copy-start.1 = (bf16[16,1152]{1,0:T(8,128)(2,1)S(1)}, bf16[16,1152]{1,0:T(8,128)(2,1)}, u32[]{:S(2)}) copy-start(bf16[16,1152]{1,0:T(8,128)(2,1)} %embed_ref.3) | copy-start | bytes 110596
  90.9 27.2 %copy-start.2 = (bf16[16,1152]{1,0:T(8,128)(2,1)S(1)}, bf16[16,1152]{1,0:T(8,128)(2,1)}, u32[]{:S(2)}) copy-start(bf16[16,1152]{1,0:T(8,128)(2,1)} %embed_ref.2) | copy-start | bytes 110596
  90.9 27.2 %all-to-all-start.2 = ((bf16[8,16,1280]{2,1,0:T(8,128)(2,1)}), bf16[8,16,1280]{2,1,0:T(8,128)(2,1)S(1)}, u32[]{:S(2)}, u32[]{:S(2)}) async-start(bf16[8,16,1280]{2,1,0:T(8,128)(2,1)} %shard_map.80), calls=%async_computation.2 | async-start | bytes 655360 | tf_op jit(solution)/shard_map/all_to_all | solution.py:359
  95.2 7.1 %collective-permute-start.4 = (bf16[2,16,1152]{2,1,0:T(8,128)(2,1)S(1)}, bf16[2,16,1152]{2,1,0:T(8,128)(2,1)S(1)}, u32[]{:S(2)}, u32[]{:S(2)}) collective-permute-start(bf16[2,16,1152]{2,1,0:T(8,128)(2,1)S(1)} %get-tuple-element.33), channel_id=1, source_target_pairs={{0,64},{64,0},{128,192},{192,128},{1,65},{65,1},{129,193},{193,129... | collective-permute-start | bytes 221192 | tf_op jit(solution)/shard_map/ppermute | solution.py:350
  102.4 9.8 %collective-permute-start.5 = (bf16[16,1152]{1,0:T(8,128)(2,1)S(1)}, bf16[16,1152]{1,0:T(8,128)(2,1)S(1)}, u32[]{:S(2)}, u32[]{:S(2)}) collective-permute-start(bf16[16,1152]{1,0:T(8,128)(2,1)S(1)} %get-tuple-element.35), channel_id=1, source_target_pairs={{0,128},{64,192},{128,0},{192,64},{1,129},{65,193},{129,1},{193,65... | collective-permute-start | bytes 110600 | tf_op jit(solution)/shard_map/ppermute | solution.py:357

commit v7 on v6

--- a/solution.py
+++ b/solution.py
@@ -115,7 +115,7 @@
     scores = scale * dot(wide[:, :WIDTH], text_wide[:, :WIDTH], 1, 1) + bias_ref[0]
     positive = dot(wide[:, WIDTH:], text_wide[:, WIDTH:], 1, 1) == 0.0
     small = jnp.exp(-jnp.abs(scores))
-    losses = jnp.maximum(jnp.where(positive, -scores, scores), 0.0) + jnp.log1p(small)
+    losses = jnp.maximum(jnp.where(positive, -scores, scores), 0.0) + jnp.log(1.0 + small)
     sigmoid = jnp.where(scores >= 0.0, 1.0, small) / (1.0 + small)
     coeffs = (sigmoid - jnp.where(positive, 1.0, 0.0)).astype(BF16)
     return jnp.sum(losses, axis=1, keepdims=True), coeffs
@@ -134,7 +134,7 @@
 
 
 def second_tile(
-    order, log_temp_ref, bias_ref, other_ref, text_ref, mine_ref, coeffs_ref, give_out, text_out,
+    order, far, log_temp_ref, bias_ref, other_ref, text_ref, mine_ref, coeffs_ref, give_out, text_out,
     other, text, mine, mine_coeffs, coeffs_now, give_now, text_now, in_sem, out_sem
 ):
     other_copy, text_copy, mine_copy, coeffs_copy = start(
@@ -156,10 +156,12 @@
         total = dot(mine_coeffs[:, columns], mine[:, :WIDTH], 0, 0)
         total += dot(coeffs_now[:, columns], other[:, :WIDTH], 0, 0)
         for k in range(chunk):
-            place = order[first + k]
-            text_now[place] = total[k * ROWS : (k + 1) * ROWS].astype(BF16)
+            text_now[order[first + k]] = total[k * ROWS : (k + 1) * ROWS].astype(BF16)
+        places = sorted(order[first : first + chunk])
+        for run in range(0, chunk, far):
+            blocks = pl.ds(places[run], far)
             copies += start(
-                pltpu.make_async_copy(text_now.at[place], text_out.at[place], out_sem.at[1 + place])
+                pltpu.make_async_copy(text_now.at[blocks], text_out.at[blocks], out_sem.at[len(copies)])
             )
     wait(*copies)
 
@@ -298,7 +300,7 @@
     wide = plane // far // low
     order = [((b % low) * wide + b // low // far) * far + (b // low) % far for b in range(plane)]
     give, text_part = call(
-        functools.partial(second_tile, order),
+        functools.partial(second_tile, order, far),
         [(HBM, shape((half, WIDE), BF16)), (HBM, shape((plane, ROWS, WIDTH), BF16))],
         [SMEM, SMEM, HBM, HBM, HBM, HBM],
         [
@@ -310,7 +312,7 @@
             pltpu.VMEM((half, WIDE), BF16),
             pltpu.VMEM((plane, ROWS, WIDTH), BF16),
             pltpu.SemaphoreType.DMA((4,)),
-            pltpu.SemaphoreType.DMA((plane + 1,)),
+            pltpu.SemaphoreType.DMA((plane // far + 1,)),
         ],
         flops=8 * half * texts * WIDTH,
         bytes_accessed=6 * texts * WIDE,

time: 120 us -> 119 us (level)
  no operation moved by 1% of the time
where the time goes in v7:
time: 119 us
  starting transfers between devices  45.9 us (39%)
  blocking collectives  39.5 us (33%)
  waiting for transfers between devices  20.2 us (17%)
  Pallas kernels  10.8 us (9%)
  between operations  2.09 us (2%)
    all_gather x1, blocking collectives, on_device(): mine = lax.all_gather(image_wide, COLUMN, axis=0, tiled=True)  39.5 us
    all_to_all x1, starting transfers between devices, on_device(): lax.all_to_all(text_wide, PLANE, 0, 0, tiled=True).reshape(-1, WIDE)  16.7 us
    ppermute x1, starting transfers between devices, on_device(): text_got = lax.ppermute(text_give, 'y_hi', [(i, i ^ 2) for i in range(far)])  6.4 us
    all_to_all x1, starting transfers between devices, on_device(): text_terms = lax.all_to_all(text_part, ('y_lo', 'x'), 0, 0, tiled=True)  5.95 us
    all_to_all x1, waiting for transfers between devices, on_device(): image_terms = lax.all_to_all(image_terms, 'z_hi', 0, 0, tiled=True)  5.14 us
    ppermute x1, starting transfers between devices, on_device(): text_got = lax.ppermute(text_give, 'y_hi', [(i, i ^ 1) for i in range(far)])  4.27 us
    all_to_all x1, starting transfers between devices, on_device(): image_terms = lax.all_to_all(image_terms, 'z_hi', 0, 0, tiled=True)  4.16 us
    ppermute x2, starting transfers between devices, swap_cores(): return lax.ppermute(part, 'core', [(0, 1), (1, 0)])  3.82 us
  transfers between devices with their start and end apart: 9, of which 6 were waited for; matrix products, arithmetic and copies ran while one was open for 0% of the time, Pallas kernels for 4%

profile of v7, /device:TPU:8, one launch (start us, length us, event | category | flops | bytes accessed | tf_op | source)
XLA Modules:
  0.0 118.6 jit_solution(2541166866796942647)
XLA Ops:
  0.6 2.0 %shard_map.76 = (bf16[16,1280]{1,0:T(8,128)(2,1)S(1)}, bf16[32,16,1280]{2,1,0:T(8,128)(2,1)}) custom-call(s32[16]{0:T(128)} %labels_ref.1, bf16[16,1152]{1,0:T(8,128)(2,1)} %embed_ref.2, bf16[16,1152]{1,0:T(8,128)(2,1)} %embed_ref.3), custom_call_target="tpu_custom_call" | custom-call | bytes 1310720 | tf_op jit(solution)/shard_map/pallas_call | solution.py:264
  2.7 16.7 %all-to-all-start = ((bf16[32,16,1280]{2,1,0:T(8,128)(2,1)}), bf16[32,16,1280]{2,1,0:T(8,128)(2,1)S(1)}, u32[]{:S(2)}, u32[]{:S(2)}) async-start(bf16[32,16,1280]{2,1,0:T(8,128)(2,1)} %get-tuple-element.21), calls=%async_computation | async-start | bytes 2621440 | tf_op jit(solution)/shard_map/all_to_all | solution.py:279
  19.4 39.5 %all_gather.3.mine.mine_ref = bf16[256,1280]{1,0:T(8,128)(2,1)S(1)} all-gather(bf16[16,1280]{1,0:T(8,128)(2,1)S(1)} %get-tuple-element.20), channel_id=1, replica_groups=mesh['x'=4,'y_hi'=4,'core'=2,'y_lo'=2,'z_hi'=8,'z_lo'=2] {'z_hi','z_lo'}, dimensions={0}, use_global_device_ids=true | all-gather | bytes 696320 | tf_op jit(solution)/shard_map/all_gather | solution.py:280
  58.9 1.9 %collective-permute-start = (bf16[256,1280]{1,0:T(8,128)(2,1)S(1)}, bf16[256,1280]{1,0:T(8,128)(2,1)S(1)}, u32[]{:S(2)}, u32[]{:S(2)}) collective-permute-start(bf16[256,1280]{1,0:T(8,128)(2,1)S(1)} %all_gather.3.mine.mine_ref), channel_id=1, source_target_pairs={{0,32},{32,0},{1,33},{33,1},{2,34},{34,2},{3,35},{35,3},{4,36},{36... | collective-permute-start | bytes 1966088 | tf_op jit(solution)/shard_map/ppermute | solution.py:256
  62.1 0.0 all-to-all-done
  62.1 2.4 %shard_map.77 = (bf16[256,512]{1,0:T(8,128)(2,1)}, f32[256,1280]{1,0:T(8,128)}) custom-call(f32[1]{0:T(128)S(6)} %copy.8.log_temp_ref, f32[1]{0:T(128)S(6)} %copy.9.bias_ref, bf16[256,1280]{1,0:T(8,128)(2,1)S(1)} %all_gather.3.mine.mine_ref, bf16[512,1280]{1,0:T(8,128)(2,1)S(1)} %bitcast.7), custom_call_target="tpu_custom_call" | custom-call | flops 603979776 | bytes 2621440 | tf_op jit(solution)/shard_map/pallas_call | solution.py:285
  64.5 0.0 collective-permute-done.other_ref
  64.5 3.5 %shard_map.78 = (bf16[256,1280]{1,0:T(8,128)(2,1)}, bf16[32,16,1152]{2,1,0:T(8,128)(2,1)}) custom-call(f32[1]{0:T(128)S(6)} %copy.8.log_temp_ref, f32[1]{0:T(128)S(6)} %copy.9.bias_ref, bf16[256,1280]{1,0:T(8,128)(2,1)S(1)} %collective-permute-done.other_ref, bf16[512,1280]{1,0:T(8,128)(2,1)S(1)} %bitcast.8, bf16[256,1280]{1,0:T(8,128)(2,1)S(1)} %all_gather.3.mine.mine_ref, ...), custom_call_target="tpu_custom_call" | custom-call | flops 1207959552 | bytes 3932160 | tf_op jit(solution)/shard_map/pallas_call | solution.py:302
  68.0 0.0 copy-start
  68.0 6.0 %all-to-all-start.1 = ((bf16[32,16,1152]{2,1,0:T(8,128)(2,1)}), bf16[32,16,1152]{2,1,0:T(8,128)(2,1)S(1)}, u32[]{:S(2)}, u32[]{:S(2)}) async-start(bf16[32,16,1152]{2,1,0:T(8,128)(2,1)} %get-tuple-element.28), calls=%async_computation.1 | async-start | bytes 2359296 | tf_op jit(solution)/shard_map/all_to_all | solution.py:321
  74.0 1.9 %collective-permute-start.1 = (bf16[256,1280]{1,0:T(8,128)(2,1)}, bf16[256,1280]{1,0:T(8,128)(2,1)S(1)}, u32[]{:S(2)}, u32[]{:S(2)}) collective-permute-start(bf16[256,1280]{1,0:T(8,128)(2,1)} %get-tuple-element.24), channel_id=1, source_target_pairs={{0,32},{32,0},{1,33},{33,1},{2,34},{34,2},{3,35},{35,3},{4,36},{36... | collective-permute-start | bytes 1966088 | tf_op jit(solution)/shard_map/ppermute | solution.py:256
  75.9 2.3 %collective-permute-done.1.got_ref = bf16[256,1280]{1,0:T(8,128)(2,1)S(1)} collective-permute-done((bf16[256,1280]{1,0:T(8,128)(2,1)}, bf16[256,1280]{1,0:T(8,128)(2,1)S(1)}, u32[]{:S(2)}, u32[]{:S(2)}) %collective-permute-start.1) | collective-permute-done | bytes 655392 | tf_op jit(solution)/shard_map/ppermute | solution.py:256
  78.1 0.0 copy-done
  78.1 0.2 shard_map.79
  78.3 1.9 %collective-permute-start.2 = (bf16[128,640]{1,0:T(8,128)(2,1)S(1)}, bf16[128,640]{1,0:T(8,128)(2,1)S(1)}, u32[]{:S(2)}, u32[]{:S(2)}) collective-permute-start(bf16[128,640]{1,0:T(8,128)(2,1)S(1)} %get-tuple-element.26), channel_id=1, source_target_pairs={{0,1},{1,0},{2,3},{3,2},{4,5},{5,4},{6,7},{7,6},{8,9},{9,8},{10,11... | collective-permute-start | bytes 491528 | tf_op jit(solution)/shard_map/ppermute | solution.py:332
  80.3 2.7 %collective-permute-start.3 = (bf16[128,640]{1,0:T(8,128)(2,1)S(1)}, bf16[128,640]{1,0:T(8,128)(2,1)S(1)}, u32[]{:S(2)}, u32[]{:S(2)}) collective-permute-start(bf16[128,640]{1,0:T(8,128)(2,1)S(1)} %get-tuple-element.27), channel_id=1, source_target_pairs={{0,15},{1,2},{2,1},{3,4},{4,3},{5,6},{6,5},{7,8},{8,7},{9,10},{10,... | collective-permute-start | bytes 491528 | tf_op jit(solution)/shard_map/ppermute | solution.py:333
  83.0 3.5 %collective-permute-done.2.left_ref = bf16[128,640]{1,0:T(8,128)(2,1)S(1)} collective-permute-done((bf16[128,640]{1,0:T(8,128)(2,1)S(1)}, bf16[128,640]{1,0:T(8,128)(2,1)S(1)}, u32[]{:S(2)}, u32[]{:S(2)}) %collective-permute-start.2) | collective-permute-done | bytes 163872 | tf_op jit(solution)/shard_map/ppermute | solution.py:332
  86.5 3.1 %collective-permute-done.3.right_ref = bf16[128,640]{1,0:T(8,128)(2,1)S(1)} collective-permute-done((bf16[128,640]{1,0:T(8,128)(2,1)S(1)}, bf16[128,640]{1,0:T(8,128)(2,1)S(1)}, u32[]{:S(2)}, u32[]{:S(2)}) %collective-permute-start.3) | collective-permute-done | bytes 163872 | tf_op jit(solution)/shard_map/ppermute | solution.py:333
  89.6 0.9 shard_map.80
  90.5 0.0 copy-start.1
  90.5 0.0 copy-start.2
  90.5 0.0 all-to-all-done.1
  90.5 4.2 %all-to-all-start.2 = ((bf16[8,16,1280]{2,1,0:T(8,128)(2,1)}), bf16[8,16,1280]{2,1,0:T(8,128)(2,1)S(1)}, u32[]{:S(2)}, u32[]{:S(2)}) async-start(bf16[8,16,1280]{2,1,0:T(8,128)(2,1)} %shard_map.80), calls=%async_computation.2 | async-start | bytes 655360 | tf_op jit(solution)/shard_map/all_to_all | solution.py:361
  94.7 0.2 shard_map.82
  94.9 4.3 %collective-permute-start.4 = (bf16[2,16,1152]{2,1,0:T(8,128)(2,1)S(1)}, bf16[2,16,1152]{2,1,0:T(8,128)(2,1)S(1)}, u32[]{:S(2)}, u32[]{:S(2)}) collective-permute-start(bf16[2,16,1152]{2,1,0:T(8,128)(2,1)S(1)} %get-tuple-element.33), channel_id=1, source_target_pairs={{0,64},{64,0},{128,192},{192,128},{1,65},{65,1},{129,193},{193,129... | collective-permute-start | bytes 221192 | tf_op jit(solution)/shard_map/ppermute | solution.py:352
  99.1 2.9 %collective-permute-done.4.got_ref = bf16[2,16,1152]{2,1,0:T(8,128)(2,1)S(1)} collective-permute-done((bf16[2,16,1152]{2,1,0:T(8,128)(2,1)S(1)}, bf16[2,16,1152]{2,1,0:T(8,128)(2,1)S(1)}, u32[]{:S(2)}, u32[]{:S(2)}) %collective-permute-start.4) | collective-permute-done | bytes 73760 | tf_op jit(solution)/shard_map/ppermute | solution.py:352
  102.0 6.4 %collective-permute-start.5 = (bf16[16,1152]{1,0:T(8,128)(2,1)S(1)}, bf16[16,1152]{1,0:T(8,128)(2,1)S(1)}, u32[]{:S(2)}, u32[]{:S(2)}) collective-permute-start(bf16[16,1152]{1,0:T(8,128)(2,1)S(1)} %get-tuple-element.35), channel_id=1, source_target_pairs={{0,128},{64,192},{128,0},{192,64},{1,129},{65,193},{129,1},{193,65... | collective-permute-start | bytes 110600 | tf_op jit(solution)/shard_map/ppermute | solution.py:359
  108.4 3.4 %collective-permute-done.5.got_ref = bf16[16,1152]{1,0:T(8,128)(2,1)S(1)} collective-permute-done((bf16[16,1152]{1,0:T(8,128)(2,1)S(1)}, bf16[16,1152]{1,0:T(8,128)(2,1)S(1)}, u32[]{:S(2)}, u32[]{:S(2)}) %collective-permute-start.5) | collective-permute-done | bytes 36896 | tf_op jit(solution)/shard_map/ppermute | solution.py:359
  111.8 0.0 copy-done.1
  111.8 0.8 shard_map.84
  112.6 5.1 %all-to-all-done.2.terms_ref = bf16[8,16,1280]{2,1,0:T(8,128)(2,1)S(1)} async-done(((bf16[8,16,1280]{2,1,0:T(8,128)(2,1)}), bf16[8,16,1280]{2,1,0:T(8,128)(2,1)S(1)}, u32[]{:S(2)}, u32[]{:S(2)}) %all-to-all-start.2) | async-done | bytes 327712 | tf_op jit(solution)/shard_map/all_to_all | solution.py:361
  117.7 0.8 shard_map.81
  (2 shorter events, 0.0 us)
Async XLA Ops:
  2.7 59.4 %all-to-all-start = ((bf16[32,16,1280]{2,1,0:T(8,128)(2,1)}), bf16[32,16,1280]{2,1,0:T(8,128)(2,1)S(1)}, u32[]{:S(2)}, u32[]{:S(2)}) async-start(bf16[32,16,1280]{2,1,0:T(8,128)(2,1)} %get-tuple-element.21), calls=%async_computation | async-start | bytes 2621440 | tf_op jit(solution)/shard_map/all_to_all | solution.py:279
  58.9 5.6 %collective-permute-start = (bf16[256,1280]{1,0:T(8,128)(2,1)S(1)}, bf16[256,1280]{1,0:T(8,128)(2,1)S(1)}, u32[]{:S(2)}, u32[]{:S(2)}) collective-permute-start(bf16[256,1280]{1,0:T(8,128)(2,1)S(1)} %all_gather.3.mine.mine_ref), channel_id=1, source_target_pairs={{0,32},{32,0},{1,33},{33,1},{2,34},{34,2},{3,35},{35,3},{4,36},{36... | collective-permute-start | bytes 1966088 | tf_op jit(solution)/shard_map/ppermute | solution.py:256
  68.0 10.2 %copy-start = (f32[256,1280]{1,0:T(8,128)S(1)}, f32[256,1280]{1,0:T(8,128)}, u32[]{:S(2)}) copy-start(f32[256,1280]{1,0:T(8,128)} %get-tuple-element.22.keep_ref) | copy-start | bytes 3932164
  68.0 22.5 %all-to-all-start.1 = ((bf16[32,16,1152]{2,1,0:T(8,128)(2,1)}), bf16[32,16,1152]{2,1,0:T(8,128)(2,1)S(1)}, u32[]{:S(2)}, u32[]{:S(2)}) async-start(bf16[32,16,1152]{2,1,0:T(8,128)(2,1)} %get-tuple-element.28), calls=%async_computation.1 | async-start | bytes 2359296 | tf_op jit(solution)/shard_map/all_to_all | solution.py:321
  74.0 4.2 %collective-permute-start.1 = (bf16[256,1280]{1,0:T(8,128)(2,1)}, bf16[256,1280]{1,0:T(8,128)(2,1)S(1)}, u32[]{:S(2)}, u32[]{:S(2)}) collective-permute-start(bf16[256,1280]{1,0:T(8,128)(2,1)} %get-tuple-element.24), channel_id=1, source_target_pairs={{0,32},{32,0},{1,33},{33,1},{2,34},{34,2},{3,35},{35,3},{4,36},{36... | collective-permute-start | bytes 1966088 | tf_op jit(solution)/shard_map/ppermute | solution.py:256
  78.3 8.1 %collective-permute-start.2 = (bf16[128,640]{1,0:T(8,128)(2,1)S(1)}, bf16[128,640]{1,0:T(8,128)(2,1)S(1)}, u32[]{:S(2)}, u32[]{:S(2)}) collective-permute-start(bf16[128,640]{1,0:T(8,128)(2,1)S(1)} %get-tuple-element.26), channel_id=1, source_target_pairs={{0,1},{1,0},{2,3},{3,2},{4,5},{5,4},{6,7},{7,6},{8,9},{9,8},{10,11... | collective-permute-start | bytes 491528 | tf_op jit(solution)/shard_map/ppermute | solution.py:332
  80.3 9.3 %collective-permute-start.3 = (bf16[128,640]{1,0:T(8,128)(2,1)S(1)}, bf16[128,640]{1,0:T(8,128)(2,1)S(1)}, u32[]{:S(2)}, u32[]{:S(2)}) collective-permute-start(bf16[128,640]{1,0:T(8,128)(2,1)S(1)} %get-tuple-element.27), channel_id=1, source_target_pairs={{0,15},{1,2},{2,1},{3,4},{4,3},{5,6},{6,5},{7,8},{8,7},{9,10},{10,... | collective-permute-start | bytes 491528 | tf_op jit(solution)/shard_map/ppermute | solution.py:333
  90.5 21.3 %copy-start.1 = (bf16[16,1152]{1,0:T(8,128)(2,1)S(1)}, bf16[16,1152]{1,0:T(8,128)(2,1)}, u32[]{:S(2)}) copy-start(bf16[16,1152]{1,0:T(8,128)(2,1)} %embed_ref.3) | copy-start | bytes 110596
  90.5 27.2 %copy-start.2 = (bf16[16,1152]{1,0:T(8,128)(2,1)S(1)}, bf16[16,1152]{1,0:T(8,128)(2,1)}, u32[]{:S(2)}) copy-start(bf16[16,1152]{1,0:T(8,128)(2,1)} %embed_ref.2) | copy-start | bytes 110596
  90.5 27.2 %all-to-all-start.2 = ((bf16[8,16,1280]{2,1,0:T(8,128)(2,1)}), bf16[8,16,1280]{2,1,0:T(8,128)(2,1)S(1)}, u32[]{:S(2)}, u32[]{:S(2)}) async-start(bf16[8,16,1280]{2,1,0:T(8,128)(2,1)} %shard_map.80), calls=%async_computation.2 | async-start | bytes 655360 | tf_op jit(solution)/shard_map/all_to_all | solution.py:361
  94.9 7.1 %collective-permute-start.4 = (bf16[2,16,1152]{2,1,0:T(8,128)(2,1)S(1)}, bf16[2,16,1152]{2,1,0:T(8,128)(2,1)S(1)}, u32[]{:S(2)}, u32[]{:S(2)}) collective-permute-start(bf16[2,16,1152]{2,1,0:T(8,128)(2,1)S(1)} %get-tuple-element.33), channel_id=1, source_target_pairs={{0,64},{64,0},{128,192},{192,128},{1,65},{65,1},{129,193},{193,129... | collective-permute-start | bytes 221192 | tf_op jit(solution)/shard_map/ppermute | solution.py:352
  102.0 9.8 %collective-permute-start.5 = (bf16[16,1152]{1,0:T(8,128)(2,1)S(1)}, bf16[16,1152]{1,0:T(8,128)(2,1)S(1)}, u32[]{:S(2)}, u32[]{:S(2)}) collective-permute-start(bf16[16,1152]{1,0:T(8,128)(2,1)S(1)} %get-tuple-element.35), channel_id=1, source_target_pairs={{0,128},{64,192},{128,0},{192,64},{1,129},{65,193},{129,1},{193,65... | collective-permute-start | bytes 110600 | tf_op jit(solution)/shard_map/ppermute | solution.py:359

commit v8 on v7

--- a/solution.py
+++ b/solution.py
@@ -134,16 +134,15 @@
 
 
 def second_tile(
-    order, far, log_temp_ref, bias_ref, other_ref, text_ref, mine_ref, coeffs_ref, give_out, text_out,
-    other, text, mine, mine_coeffs, coeffs_now, give_now, text_now, in_sem, out_sem
+    order, far, log_temp_ref, bias_ref, other, text_ref, mine_ref, coeffs_ref, give_out, text_out,
+    text, mine, mine_coeffs, coeffs_now, give_now, text_now, in_sem, out_sem
 ):
-    other_copy, text_copy, mine_copy, coeffs_copy = start(
-        pltpu.make_async_copy(other_ref, other, in_sem.at[0]),
-        pltpu.make_async_copy(text_ref, text, in_sem.at[1]),
-        pltpu.make_async_copy(mine_ref, mine, in_sem.at[2]),
-        pltpu.make_async_copy(coeffs_ref, mine_coeffs, in_sem.at[3]),
-    )
-    wait(other_copy, text_copy)
+    text_copy, mine_copy, coeffs_copy = start(
+        pltpu.make_async_copy(text_ref, text, in_sem.at[0]),
+        pltpu.make_async_copy(mine_ref, mine, in_sem.at[1]),
+        pltpu.make_async_copy(coeffs_ref, mine_coeffs, in_sem.at[2]),
+    )
+    wait(text_copy)
     loss, coeffs = half_tile(log_temp_ref, bias_ref, other, text)
     coeffs_now[...] = coeffs
     give_now[:, :WIDTH] = dot(coeffs, text[:, :WIDTH], 1, 0).astype(BF16)
@@ -199,9 +198,11 @@
         out_ref[block, :, split:WIDTH] = terms[:, : WIDTH - split].astype(BF16)
         loss = jnp.sum(terms[:, WIDTH - split :], axis=1, keepdims=True)
         out_ref[block, :, WIDTH:] = loss_pair(loss)
-        copies += start(
-            pltpu.make_async_copy(out_ref.at[block], part_out.at[block], out_sem.at[block])
-        )
+        if block % 4 == 3:
+            run = pl.ds(block - 3, 4)
+            copies += start(
+                pltpu.make_async_copy(out_ref.at[run], part_out.at[run], out_sem.at[block // 4])
+            )
     wait(*copies)
 
 
@@ -302,16 +303,15 @@
     give, text_part = call(
         functools.partial(second_tile, order, far),
         [(HBM, shape((half, WIDE), BF16)), (HBM, shape((plane, ROWS, WIDTH), BF16))],
-        [SMEM, SMEM, HBM, HBM, HBM, HBM],
+        [SMEM, SMEM, VMEM, HBM, HBM, HBM],
         [
-            pltpu.VMEM((half, WIDE), BF16),
             pltpu.VMEM((texts, WIDE), BF16),
             pltpu.VMEM((half, WIDE), BF16),
             pltpu.VMEM((half, texts), BF16),
             pltpu.VMEM((half, texts), BF16),
             pltpu.VMEM((half, WIDE), BF16),
             pltpu.VMEM((plane, ROWS, WIDTH), BF16),
-            pltpu.SemaphoreType.DMA((4,)),
+            pltpu.SemaphoreType.DMA((3,)),
             pltpu.SemaphoreType.DMA((plane // far + 1,)),
         ],
         flops=8 * half * texts * WIDTH,
@@ -337,7 +337,7 @@
         last_fold,
         [(HBM, shape((blocks, ROWS, WIDE), BF16))],
         [VMEM, VMEM, VMEM],
-        [pltpu.VMEM((blocks, ROWS, WIDE), BF16), pltpu.SemaphoreType.DMA((blocks,))],
+        [pltpu.VMEM((blocks, ROWS, WIDE), BF16), pltpu.SemaphoreType.DMA((blocks // 4,))],
         bytes_accessed=8 * rows * WIDE,
     )(keep, left, right)
     image_terms, text_terms = lax.optimization_barrier((image_terms, text_terms))

time: 119 us -> 119 us (level)
  no operation moved by 1% of the time
where the time goes in v8:
time: 119 us; the launch traced here: 118 us
  starting transfers between devices  45.9 us (39%)
  blocking collectives  39.5 us (33%)
  waiting for transfers between devices  20.3 us (17%)
  Pallas kernels  10.5 us (9%)
  between operations  2.09 us (2%)
    all_gather x1, blocking collectives, on_device(): mine = lax.all_gather(image_wide, COLUMN, axis=0, tiled=True)  39.5 us
    all_to_all x1, starting transfers between devices, on_device(): lax.all_to_all(text_wide, PLANE, 0, 0, tiled=True).reshape(-1, WIDE)  16.7 us
    ppermute x1, starting transfers between devices, on_device(): text_got = lax.ppermute(text_give, 'y_hi', [(i, i ^ 2) for i in range(far)])  6.39 us
    all_to_all x1, starting transfers between devices, on_device(): text_terms = lax.all_to_all(text_part, ('y_lo', 'x'), 0, 0, tiled=True)  5.95 us
    all_to_all x1, waiting for transfers between devices, on_device(): image_terms = lax.all_to_all(image_terms, 'z_hi', 0, 0, tiled=True)  5.13 us
    ppermute x1, starting transfers between devices, on_device(): text_got = lax.ppermute(text_give, 'y_hi', [(i, i ^ 1) for i in range(far)])  4.26 us
    all_to_all x1, starting transfers between devices, on_device(): image_terms = lax.all_to_all(image_terms, 'z_hi', 0, 0, tiled=True)  4.17 us
    ppermute x2, starting transfers between devices, swap_cores(): return lax.ppermute(part, 'core', [(0, 1), (1, 0)])  3.82 us
  transfers between devices with their start and end apart: 9, of which 6 were waited for; matrix products, arithmetic and copies ran while one was open for 0% of the time, Pallas kernels for 4%

profile of v8, /device:TPU:8, one launch (start us, length us, event | category | flops | bytes accessed | tf_op | source)
XLA Modules:
  0.0 118.4 jit_solution(6221499306588287140)
XLA Ops:
  0.6 2.0 %shard_map.76 = (bf16[16,1280]{1,0:T(8,128)(2,1)S(1)}, bf16[32,16,1280]{2,1,0:T(8,128)(2,1)}) custom-call(s32[16]{0:T(128)} %labels_ref.1, bf16[16,1152]{1,0:T(8,128)(2,1)} %embed_ref.2, bf16[16,1152]{1,0:T(8,128)(2,1)} %embed_ref.3), custom_call_target="tpu_custom_call" | custom-call | bytes 1310720 | tf_op jit(solution)/shard_map/pallas_call | solution.py:265
  2.7 16.7 %all-to-all-start = ((bf16[32,16,1280]{2,1,0:T(8,128)(2,1)}), bf16[32,16,1280]{2,1,0:T(8,128)(2,1)S(1)}, u32[]{:S(2)}, u32[]{:S(2)}) async-start(bf16[32,16,1280]{2,1,0:T(8,128)(2,1)} %get-tuple-element.21), calls=%async_computation | async-start | bytes 2621440 | tf_op jit(solution)/shard_map/all_to_all | solution.py:280
  19.4 39.5 %all_gather.3.mine.mine_ref = bf16[256,1280]{1,0:T(8,128)(2,1)S(1)} all-gather(bf16[16,1280]{1,0:T(8,128)(2,1)S(1)} %get-tuple-element.20), channel_id=1, replica_groups=mesh['x'=4,'y_hi'=4,'core'=2,'y_lo'=2,'z_hi'=8,'z_lo'=2] {'z_hi','z_lo'}, dimensions={0}, use_global_device_ids=true | all-gather | bytes 696320 | tf_op jit(solution)/shard_map/all_gather | solution.py:281
  58.9 1.9 %collective-permute-start = (bf16[256,1280]{1,0:T(8,128)(2,1)S(1)}, bf16[256,1280]{1,0:T(8,128)(2,1)S(1)}, u32[]{:S(2)}, u32[]{:S(2)}) collective-permute-start(bf16[256,1280]{1,0:T(8,128)(2,1)S(1)} %all_gather.3.mine.mine_ref), channel_id=1, source_target_pairs={{0,32},{32,0},{1,33},{33,1},{2,34},{34,2},{3,35},{35,3},{4,36},{36... | collective-permute-start | bytes 1966088 | tf_op jit(solution)/shard_map/ppermute | solution.py:257
  62.1 0.0 all-to-all-done
  62.1 2.4 %shard_map.77 = (bf16[256,512]{1,0:T(8,128)(2,1)}, f32[256,1280]{1,0:T(8,128)}) custom-call(f32[1]{0:T(128)S(6)} %copy.8.log_temp_ref, f32[1]{0:T(128)S(6)} %copy.9.bias_ref, bf16[256,1280]{1,0:T(8,128)(2,1)S(1)} %all_gather.3.mine.mine_ref, bf16[512,1280]{1,0:T(8,128)(2,1)S(1)} %bitcast.7), custom_call_target="tpu_custom_call" | custom-call | flops 603979776 | bytes 2621440 | tf_op jit(solution)/shard_map/pallas_call | solution.py:286
  64.5 0.0 collective-permute-done.other
  64.5 3.3 %shard_map.78 = (bf16[256,1280]{1,0:T(8,128)(2,1)}, bf16[32,16,1152]{2,1,0:T(8,128)(2,1)}) custom-call(f32[1]{0:T(128)S(6)} %copy.8.log_temp_ref, f32[1]{0:T(128)S(6)} %copy.9.bias_ref, bf16[256,1280]{1,0:T(8,128)(2,1)S(1)} %collective-permute-done.other, bf16[512,1280]{1,0:T(8,128)(2,1)S(1)} %bitcast.8, bf16[256,1280]{1,0:T(8,128)(2,1)S(1)} %all_gather.3.mine.mine_ref, ...), custom_call_target="tpu_custom_call" | custom-call | flops 1207959552 | bytes 3932160 | tf_op jit(solution)/shard_map/pallas_call | solution.py:303
  67.8 0.0 copy-start
  67.8 6.0 %all-to-all-start.1 = ((bf16[32,16,1152]{2,1,0:T(8,128)(2,1)}), bf16[32,16,1152]{2,1,0:T(8,128)(2,1)S(1)}, u32[]{:S(2)}, u32[]{:S(2)}) async-start(bf16[32,16,1152]{2,1,0:T(8,128)(2,1)} %get-tuple-element.28), calls=%async_computation.1 | async-start | bytes 2359296 | tf_op jit(solution)/shard_map/all_to_all | solution.py:321
  73.7 1.9 %collective-permute-start.1 = (bf16[256,1280]{1,0:T(8,128)(2,1)}, bf16[256,1280]{1,0:T(8,128)(2,1)S(1)}, u32[]{:S(2)}, u32[]{:S(2)}) collective-permute-start(bf16[256,1280]{1,0:T(8,128)(2,1)} %get-tuple-element.24), channel_id=1, source_target_pairs={{0,32},{32,0},{1,33},{33,1},{2,34},{34,2},{3,35},{35,3},{4,36},{36... | collective-permute-start | bytes 1966088 | tf_op jit(solution)/shard_map/ppermute | solution.py:257
  75.7 2.3 %collective-permute-done.1.got_ref = bf16[256,1280]{1,0:T(8,128)(2,1)S(1)} collective-permute-done((bf16[256,1280]{1,0:T(8,128)(2,1)}, bf16[256,1280]{1,0:T(8,128)(2,1)S(1)}, u32[]{:S(2)}, u32[]{:S(2)}) %collective-permute-start.1) | collective-permute-done | bytes 655392 | tf_op jit(solution)/shard_map/ppermute | solution.py:257
  77.9 0.0 copy-done
  77.9 0.2 shard_map.79
  78.1 1.9 %collective-permute-start.2 = (bf16[128,640]{1,0:T(8,128)(2,1)S(1)}, bf16[128,640]{1,0:T(8,128)(2,1)S(1)}, u32[]{:S(2)}, u32[]{:S(2)}) collective-permute-start(bf16[128,640]{1,0:T(8,128)(2,1)S(1)} %get-tuple-element.26), channel_id=1, source_target_pairs={{0,1},{1,0},{2,3},{3,2},{4,5},{5,4},{6,7},{7,6},{8,9},{9,8},{10,11... | collective-permute-start | bytes 491528 | tf_op jit(solution)/shard_map/ppermute | solution.py:332
  80.0 2.7 %collective-permute-start.3 = (bf16[128,640]{1,0:T(8,128)(2,1)S(1)}, bf16[128,640]{1,0:T(8,128)(2,1)S(1)}, u32[]{:S(2)}, u32[]{:S(2)}) collective-permute-start(bf16[128,640]{1,0:T(8,128)(2,1)S(1)} %get-tuple-element.27), channel_id=1, source_target_pairs={{0,15},{1,2},{2,1},{3,4},{4,3},{5,6},{6,5},{7,8},{8,7},{9,10},{10,... | collective-permute-start | bytes 491528 | tf_op jit(solution)/shard_map/ppermute | solution.py:333
  82.8 3.5 %collective-permute-done.2.left_ref = bf16[128,640]{1,0:T(8,128)(2,1)S(1)} collective-permute-done((bf16[128,640]{1,0:T(8,128)(2,1)S(1)}, bf16[128,640]{1,0:T(8,128)(2,1)S(1)}, u32[]{:S(2)}, u32[]{:S(2)}) %collective-permute-start.2) | collective-permute-done | bytes 163872 | tf_op jit(solution)/shard_map/ppermute | solution.py:332
  86.3 3.1 %collective-permute-done.3.right_ref = bf16[128,640]{1,0:T(8,128)(2,1)S(1)} collective-permute-done((bf16[128,640]{1,0:T(8,128)(2,1)S(1)}, bf16[128,640]{1,0:T(8,128)(2,1)S(1)}, u32[]{:S(2)}, u32[]{:S(2)}) %collective-permute-start.3) | collective-permute-done | bytes 163872 | tf_op jit(solution)/shard_map/ppermute | solution.py:333
  89.4 0.8 shard_map.80
  90.2 0.0 copy-start.1
  90.3 0.0 copy-start.2
  90.3 0.0 all-to-all-done.1
  90.3 4.2 %all-to-all-start.2 = ((bf16[8,16,1280]{2,1,0:T(8,128)(2,1)}), bf16[8,16,1280]{2,1,0:T(8,128)(2,1)S(1)}, u32[]{:S(2)}, u32[]{:S(2)}) async-start(bf16[8,16,1280]{2,1,0:T(8,128)(2,1)} %shard_map.80), calls=%async_computation.2 | async-start | bytes 655360 | tf_op jit(solution)/shard_map/all_to_all | solution.py:361
  94.4 0.2 shard_map.82
  94.6 4.3 %collective-permute-start.4 = (bf16[2,16,1152]{2,1,0:T(8,128)(2,1)S(1)}, bf16[2,16,1152]{2,1,0:T(8,128)(2,1)S(1)}, u32[]{:S(2)}, u32[]{:S(2)}) collective-permute-start(bf16[2,16,1152]{2,1,0:T(8,128)(2,1)S(1)} %get-tuple-element.33), channel_id=1, source_target_pairs={{0,64},{64,0},{128,192},{192,128},{1,65},{65,1},{129,193},{193,129... | collective-permute-start | bytes 221192 | tf_op jit(solution)/shard_map/ppermute | solution.py:352
  98.9 2.9 %collective-permute-done.4.got_ref = bf16[2,16,1152]{2,1,0:T(8,128)(2,1)S(1)} collective-permute-done((bf16[2,16,1152]{2,1,0:T(8,128)(2,1)S(1)}, bf16[2,16,1152]{2,1,0:T(8,128)(2,1)S(1)}, u32[]{:S(2)}, u32[]{:S(2)}) %collective-permute-start.4) | collective-permute-done | bytes 73760 | tf_op jit(solution)/shard_map/ppermute | solution.py:352
  101.8 6.4 %collective-permute-start.5 = (bf16[16,1152]{1,0:T(8,128)(2,1)S(1)}, bf16[16,1152]{1,0:T(8,128)(2,1)S(1)}, u32[]{:S(2)}, u32[]{:S(2)}) collective-permute-start(bf16[16,1152]{1,0:T(8,128)(2,1)S(1)} %get-tuple-element.35), channel_id=1, source_target_pairs={{0,128},{64,192},{128,0},{192,64},{1,129},{65,193},{129,1},{193,65... | collective-permute-start | bytes 110600 | tf_op jit(solution)/shard_map/ppermute | solution.py:359
  108.2 3.4 %collective-permute-done.5.got_ref = bf16[16,1152]{1,0:T(8,128)(2,1)S(1)} collective-permute-done((bf16[16,1152]{1,0:T(8,128)(2,1)S(1)}, bf16[16,1152]{1,0:T(8,128)(2,1)S(1)}, u32[]{:S(2)}, u32[]{:S(2)}) %collective-permute-start.5) | collective-permute-done | bytes 36896 | tf_op jit(solution)/shard_map/ppermute | solution.py:359
  111.6 0.0 copy-done.1
  111.6 0.8 shard_map.84
  112.4 5.1 %all-to-all-done.2.terms_ref = bf16[8,16,1280]{2,1,0:T(8,128)(2,1)S(1)} async-done(((bf16[8,16,1280]{2,1,0:T(8,128)(2,1)}), bf16[8,16,1280]{2,1,0:T(8,128)(2,1)S(1)}, u32[]{:S(2)}, u32[]{:S(2)}) %all-to-all-start.2) | async-done | bytes 327712 | tf_op jit(solution)/shard_map/all_to_all | solution.py:361
  117.5 0.8 shard_map.81
  (2 shorter events, 0.0 us)
Async XLA Ops:
  2.7 59.4 %all-to-all-start = ((bf16[32,16,1280]{2,1,0:T(8,128)(2,1)}), bf16[32,16,1280]{2,1,0:T(8,128)(2,1)S(1)}, u32[]{:S(2)}, u32[]{:S(2)}) async-start(bf16[32,16,1280]{2,1,0:T(8,128)(2,1)} %get-tuple-element.21), calls=%async_computation | async-start | bytes 2621440 | tf_op jit(solution)/shard_map/all_to_all | solution.py:280
  58.9 5.6 %collective-permute-start = (bf16[256,1280]{1,0:T(8,128)(2,1)S(1)}, bf16[256,1280]{1,0:T(8,128)(2,1)S(1)}, u32[]{:S(2)}, u32[]{:S(2)}) collective-permute-start(bf16[256,1280]{1,0:T(8,128)(2,1)S(1)} %all_gather.3.mine.mine_ref), channel_id=1, source_target_pairs={{0,32},{32,0},{1,33},{33,1},{2,34},{34,2},{3,35},{35,3},{4,36},{36... | collective-permute-start | bytes 1966088 | tf_op jit(solution)/shard_map/ppermute | solution.py:257
  67.8 10.2 %copy-start = (f32[256,1280]{1,0:T(8,128)S(1)}, f32[256,1280]{1,0:T(8,128)}, u32[]{:S(2)}) copy-start(f32[256,1280]{1,0:T(8,128)} %get-tuple-element.22.keep_ref) | copy-start | bytes 3932164
  67.8 22.5 %all-to-all-start.1 = ((bf16[32,16,1152]{2,1,0:T(8,128)(2,1)}), bf16[32,16,1152]{2,1,0:T(8,128)(2,1)S(1)}, u32[]{:S(2)}, u32[]{:S(2)}) async-start(bf16[32,16,1152]{2,1,0:T(8,128)(2,1)} %get-tuple-element.28), calls=%async_computation.1 | async-start | bytes 2359296 | tf_op jit(solution)/shard_map/all_to_all | solution.py:321
  73.7 4.2 %collective-permute-start.1 = (bf16[256,1280]{1,0:T(8,128)(2,1)}, bf16[256,1280]{1,0:T(8,128)(2,1)S(1)}, u32[]{:S(2)}, u32[]{:S(2)}) collective-permute-start(bf16[256,1280]{1,0:T(8,128)(2,1)} %get-tuple-element.24), channel_id=1, source_target_pairs={{0,32},{32,0},{1,33},{33,1},{2,34},{34,2},{3,35},{35,3},{4,36},{36... | collective-permute-start | bytes 1966088 | tf_op jit(solution)/shard_map/ppermute | solution.py:257
  78.1 8.1 %collective-permute-start.2 = (bf16[128,640]{1,0:T(8,128)(2,1)S(1)}, bf16[128,640]{1,0:T(8,128)(2,1)S(1)}, u32[]{:S(2)}, u32[]{:S(2)}) collective-permute-start(bf16[128,640]{1,0:T(8,128)(2,1)S(1)} %get-tuple-element.26), channel_id=1, source_target_pairs={{0,1},{1,0},{2,3},{3,2},{4,5},{5,4},{6,7},{7,6},{8,9},{9,8},{10,11... | collective-permute-start | bytes 491528 | tf_op jit(solution)/shard_map/ppermute | solution.py:332
  80.0 9.3 %collective-permute-start.3 = (bf16[128,640]{1,0:T(8,128)(2,1)S(1)}, bf16[128,640]{1,0:T(8,128)(2,1)S(1)}, u32[]{:S(2)}, u32[]{:S(2)}) collective-permute-start(bf16[128,640]{1,0:T(8,128)(2,1)S(1)} %get-tuple-element.27), channel_id=1, source_target_pairs={{0,15},{1,2},{2,1},{3,4},{4,3},{5,6},{6,5},{7,8},{8,7},{9,10},{10,... | collective-permute-start | bytes 491528 | tf_op jit(solution)/shard_map/ppermute | solution.py:333
  90.2 21.3 %copy-start.1 = (bf16[16,1152]{1,0:T(8,128)(2,1)S(1)}, bf16[16,1152]{1,0:T(8,128)(2,1)}, u32[]{:S(2)}) copy-start(bf16[16,1152]{1,0:T(8,128)(2,1)} %embed_ref.3) | copy-start | bytes 110596
  90.3 27.3 %copy-start.2 = (bf16[16,1152]{1,0:T(8,128)(2,1)S(1)}, bf16[16,1152]{1,0:T(8,128)(2,1)}, u32[]{:S(2)}) copy-start(bf16[16,1152]{1,0:T(8,128)(2,1)} %embed_ref.2) | copy-start | bytes 110596
  90.3 27.3 %all-to-all-start.2 = ((bf16[8,16,1280]{2,1,0:T(8,128)(2,1)}), bf16[8,16,1280]{2,1,0:T(8,128)(2,1)S(1)}, u32[]{:S(2)}, u32[]{:S(2)}) async-start(bf16[8,16,1280]{2,1,0:T(8,128)(2,1)} %shard_map.80), calls=%async_computation.2 | async-start | bytes 655360 | tf_op jit(solution)/shard_map/all_to_all | solution.py:361
  94.6 7.1 %collective-permute-start.4 = (bf16[2,16,1152]{2,1,0:T(8,128)(2,1)S(1)}, bf16[2,16,1152]{2,1,0:T(8,128)(2,1)S(1)}, u32[]{:S(2)}, u32[]{:S(2)}) collective-permute-start(bf16[2,16,1152]{2,1,0:T(8,128)(2,1)S(1)} %get-tuple-element.33), channel_id=1, source_target_pairs={{0,64},{64,0},{128,192},{192,128},{1,65},{65,1},{129,193},{193,129... | collective-permute-start | bytes 221192 | tf_op jit(solution)/shard_map/ppermute | solution.py:352
  101.8 9.8 %collective-permute-start.5 = (bf16[16,1152]{1,0:T(8,128)(2,1)S(1)}, bf16[16,1152]{1,0:T(8,128)(2,1)S(1)}, u32[]{:S(2)}, u32[]{:S(2)}) collective-permute-start(bf16[16,1152]{1,0:T(8,128)(2,1)S(1)} %get-tuple-element.35), channel_id=1, source_target_pairs={{0,128},{64,192},{128,0},{192,64},{1,129},{65,193},{129,1},{193,65... | collective-permute-start | bytes 110600 | tf_op jit(solution)/shard_map/ppermute | solution.py:359

commit v9 on v7

--- a/solution.py
+++ b/solution.py
@@ -8,7 +8,7 @@
 from jax.sharding import Mesh, PartitionSpec as P
 
 AXES = ("x", "y_hi", "core", "y_lo", "z_hi", "z_lo")
-PLANE = ("x", "y_hi", "y_lo")
+PLANE = ("x", "y_lo", "y_hi")
 COLUMN = ("z_hi", "z_lo")
 WIDTH = 1152
 WIDE = WIDTH + 128
@@ -298,7 +298,7 @@
     far, low = lax.axis_size("y_hi"), lax.axis_size("y_lo")
     near = plane // far
     wide = plane // far // low
-    order = [((b % low) * wide + b // low // far) * far + (b // low) % far for b in range(plane)]
+    order = [(b // far % low * wide + b // far // low) * far + b % far for b in range(plane)]
     give, text_part = call(
         functools.partial(second_tile, order, far),
         [(HBM, shape((half, WIDE), BF16)), (HBM, shape((plane, ROWS, WIDTH), BF16))],

time: 119 us -> 119 us (level)
  the two profiles are of different devices: /device:TPU:8 before, /device:TPU:16 now
where the time goes in v9:
time: 119 us
  starting transfers between devices  41.6 us (35%)
  blocking collectives  39.5 us (33%)
  waiting for transfers between devices  24.5 us (21%)
  Pallas kernels  10.8 us (9%)
  between operations  2.08 us (2%)
    all_gather x1, blocking collectives, on_device(): mine = lax.all_gather(image_wide, COLUMN, axis=0, tiled=True)  39.5 us
    all_to_all x1, starting transfers between devices, on_device(): lax.all_to_all(text_wide, PLANE, 0, 0, tiled=True).reshape(-1, WIDE)  16.6 us
    ppermute x1, waiting for transfers between devices, on_device(): text_got = lax.ppermute(text_give, 'y_hi', [(i, i ^ 2) for i in range(far)])  5.49 us
    all_to_all x1, starting transfers between devices, on_device(): text_terms = lax.all_to_all(text_part, ('y_lo', 'x'), 0, 0, tiled=True)  5.31 us
    all_to_all x1, waiting for transfers between devices, on_device(): image_terms = lax.all_to_all(image_terms, 'z_hi', 0, 0, tiled=True)  5.24 us
    ppermute x1, waiting for transfers between devices, on_device(): text_got = lax.ppermute(text_give, 'y_hi', [(i, i ^ 1) for i in range(far)])  4.8 us
    ppermute x1, starting transfers between devices, on_device(): text_got = lax.ppermute(text_give, 'y_hi', [(i, i ^ 2) for i in range(far)])  4.65 us
    all_to_all x1, starting transfers between devices, on_device(): image_terms = lax.all_to_all(image_terms, 'z_hi', 0, 0, tiled=True)  4.06 us
  transfers between devices with their start and end apart: 9, of which 7 were waited for; matrix products, arithmetic and copies ran while one was open for 0% of the time, Pallas kernels for 4%

profile of v9, /device:TPU:16, one launch (start us, length us, event | category | flops | bytes accessed | tf_op | source)
XLA Modules:
  0.0 118.5 jit_solution(3913474965409988905)
XLA Ops:
  0.6 2.0 %shard_map.76 = (bf16[16,1280]{1,0:T(8,128)(2,1)S(1)}, bf16[32,16,1280]{2,1,0:T(8,128)(2,1)}) custom-call(s32[16]{0:T(128)} %labels_ref.1, bf16[16,1152]{1,0:T(8,128)(2,1)} %embed_ref.2, bf16[16,1152]{1,0:T(8,128)(2,1)} %embed_ref.3), custom_call_target="tpu_custom_call" | custom-call | bytes 1310720 | tf_op jit(solution)/shard_map/pallas_call | solution.py:264
  2.7 16.6 %all-to-all-start = ((bf16[32,16,1280]{2,1,0:T(8,128)(2,1)}), bf16[32,16,1280]{2,1,0:T(8,128)(2,1)S(1)}, u32[]{:S(2)}, u32[]{:S(2)}) async-start(bf16[32,16,1280]{2,1,0:T(8,128)(2,1)} %get-tuple-element.21), calls=%async_computation | async-start | bytes 2621440 | tf_op jit(solution)/shard_map/all_to_all | solution.py:279
  19.3 39.5 %all_gather.3.mine.mine_ref = bf16[256,1280]{1,0:T(8,128)(2,1)S(1)} all-gather(bf16[16,1280]{1,0:T(8,128)(2,1)S(1)} %get-tuple-element.20), channel_id=1, replica_groups=mesh['x'=4,'y_hi'=4,'core'=2,'y_lo'=2,'z_hi'=8,'z_lo'=2] {'z_hi','z_lo'}, dimensions={0}, use_global_device_ids=true | all-gather | bytes 696320 | tf_op jit(solution)/shard_map/all_gather | solution.py:280
  58.8 1.9 %collective-permute-start = (bf16[256,1280]{1,0:T(8,128)(2,1)S(1)}, bf16[256,1280]{1,0:T(8,128)(2,1)S(1)}, u32[]{:S(2)}, u32[]{:S(2)}) collective-permute-start(bf16[256,1280]{1,0:T(8,128)(2,1)S(1)} %all_gather.3.mine.mine_ref), channel_id=1, source_target_pairs={{0,32},{32,0},{1,33},{33,1},{2,34},{34,2},{3,35},{35,3},{4,36},{36... | collective-permute-start | bytes 1966088 | tf_op jit(solution)/shard_map/ppermute | solution.py:256
  62.0 0.0 all-to-all-done
  62.0 2.4 %shard_map.77 = (bf16[256,512]{1,0:T(8,128)(2,1)}, f32[256,1280]{1,0:T(8,128)}) custom-call(f32[1]{0:T(128)S(6)} %copy.8.log_temp_ref, f32[1]{0:T(128)S(6)} %copy.9.bias_ref, bf16[256,1280]{1,0:T(8,128)(2,1)S(1)} %all_gather.3.mine.mine_ref, bf16[512,1280]{1,0:T(8,128)(2,1)S(1)} %bitcast.7), custom_call_target="tpu_custom_call" | custom-call | flops 603979776 | bytes 2621440 | tf_op jit(solution)/shard_map/pallas_call | solution.py:285
  64.4 0.0 collective-permute-done.other_ref
  64.4 3.5 %shard_map.78 = (bf16[256,1280]{1,0:T(8,128)(2,1)}, bf16[32,16,1152]{2,1,0:T(8,128)(2,1)}) custom-call(f32[1]{0:T(128)S(6)} %copy.8.log_temp_ref, f32[1]{0:T(128)S(6)} %copy.9.bias_ref, bf16[256,1280]{1,0:T(8,128)(2,1)S(1)} %collective-permute-done.other_ref, bf16[512,1280]{1,0:T(8,128)(2,1)S(1)} %bitcast.8, bf16[256,1280]{1,0:T(8,128)(2,1)S(1)} %all_gather.3.mine.mine_ref, ...), custom_call_target="tpu_custom_call" | custom-call | flops 1207959552 | bytes 3932160 | tf_op jit(solution)/shard_map/pallas_call | solution.py:302
  67.9 0.0 copy-start
  67.9 5.3 %all-to-all-start.1 = ((bf16[32,16,1152]{2,1,0:T(8,128)(2,1)}), bf16[32,16,1152]{2,1,0:T(8,128)(2,1)S(1)}, u32[]{:S(2)}, u32[]{:S(2)}) async-start(bf16[32,16,1152]{2,1,0:T(8,128)(2,1)} %get-tuple-element.28), calls=%async_computation.1 | async-start | bytes 2359296 | tf_op jit(solution)/shard_map/all_to_all | solution.py:321
  73.2 2.1 %collective-permute-start.1 = (bf16[256,1280]{1,0:T(8,128)(2,1)}, bf16[256,1280]{1,0:T(8,128)(2,1)S(1)}, u32[]{:S(2)}, u32[]{:S(2)}) collective-permute-start(bf16[256,1280]{1,0:T(8,128)(2,1)} %get-tuple-element.24), channel_id=1, source_target_pairs={{0,32},{32,0},{1,33},{33,1},{2,34},{34,2},{3,35},{35,3},{4,36},{36... | collective-permute-start | bytes 1966088 | tf_op jit(solution)/shard_map/ppermute | solution.py:256
  75.3 2.1 %collective-permute-done.1.got_ref = bf16[256,1280]{1,0:T(8,128)(2,1)S(1)} collective-permute-done((bf16[256,1280]{1,0:T(8,128)(2,1)}, bf16[256,1280]{1,0:T(8,128)(2,1)S(1)}, u32[]{:S(2)}, u32[]{:S(2)}) %collective-permute-start.1) | collective-permute-done | bytes 655392 | tf_op jit(solution)/shard_map/ppermute | solution.py:256
  77.4 0.0 copy-done
  77.4 0.2 shard_map.79
  77.6 1.9 %collective-permute-start.2 = (bf16[128,640]{1,0:T(8,128)(2,1)S(1)}, bf16[128,640]{1,0:T(8,128)(2,1)S(1)}, u32[]{:S(2)}, u32[]{:S(2)}) collective-permute-start(bf16[128,640]{1,0:T(8,128)(2,1)S(1)} %get-tuple-element.26), channel_id=1, source_target_pairs={{0,1},{1,0},{2,3},{3,2},{4,5},{5,4},{6,7},{7,6},{8,9},{9,8},{10,11... | collective-permute-start | bytes 491528 | tf_op jit(solution)/shard_map/ppermute | solution.py:332
  79.5 2.7 %collective-permute-start.3 = (bf16[128,640]{1,0:T(8,128)(2,1)S(1)}, bf16[128,640]{1,0:T(8,128)(2,1)S(1)}, u32[]{:S(2)}, u32[]{:S(2)}) collective-permute-start(bf16[128,640]{1,0:T(8,128)(2,1)S(1)} %get-tuple-element.27), channel_id=1, source_target_pairs={{0,15},{1,2},{2,1},{3,4},{4,3},{5,6},{6,5},{7,8},{8,7},{9,10},{10,... | collective-permute-start | bytes 491528 | tf_op jit(solution)/shard_map/ppermute | solution.py:333
  82.2 3.6 %collective-permute-done.2.left_ref = bf16[128,640]{1,0:T(8,128)(2,1)S(1)} collective-permute-done((bf16[128,640]{1,0:T(8,128)(2,1)S(1)}, bf16[128,640]{1,0:T(8,128)(2,1)S(1)}, u32[]{:S(2)}, u32[]{:S(2)}) %collective-permute-start.2) | collective-permute-done | bytes 163872 | tf_op jit(solution)/shard_map/ppermute | solution.py:332
  85.8 3.1 %collective-permute-done.3.right_ref = bf16[128,640]{1,0:T(8,128)(2,1)S(1)} collective-permute-done((bf16[128,640]{1,0:T(8,128)(2,1)S(1)}, bf16[128,640]{1,0:T(8,128)(2,1)S(1)}, u32[]{:S(2)}, u32[]{:S(2)}) %collective-permute-start.3) | collective-permute-done | bytes 163872 | tf_op jit(solution)/shard_map/ppermute | solution.py:333
  88.9 0.9 shard_map.80
  89.8 0.0 copy-start.1
  89.8 0.0 copy-start.2
  89.9 0.2 all-to-all-done.1
  90.1 4.1 %all-to-all-start.2 = ((bf16[8,16,1280]{2,1,0:T(8,128)(2,1)}), bf16[8,16,1280]{2,1,0:T(8,128)(2,1)S(1)}, u32[]{:S(2)}, u32[]{:S(2)}) async-start(bf16[8,16,1280]{2,1,0:T(8,128)(2,1)} %shard_map.80), calls=%async_computation.2 | async-start | bytes 655360 | tf_op jit(solution)/shard_map/all_to_all | solution.py:361
  94.1 0.2 shard_map.82
  94.3 2.4 %collective-permute-start.4 = (bf16[2,16,1152]{2,1,0:T(8,128)(2,1)S(1)}, bf16[2,16,1152]{2,1,0:T(8,128)(2,1)S(1)}, u32[]{:S(2)}, u32[]{:S(2)}) collective-permute-start(bf16[2,16,1152]{2,1,0:T(8,128)(2,1)S(1)} %get-tuple-element.33), channel_id=1, source_target_pairs={{0,64},{64,0},{128,192},{192,128},{1,65},{65,1},{129,193},{193,129... | collective-permute-start | bytes 221192 | tf_op jit(solution)/shard_map/ppermute | solution.py:352
  96.7 4.8 %collective-permute-done.4.got_ref = bf16[2,16,1152]{2,1,0:T(8,128)(2,1)S(1)} collective-permute-done((bf16[2,16,1152]{2,1,0:T(8,128)(2,1)S(1)}, bf16[2,16,1152]{2,1,0:T(8,128)(2,1)S(1)}, u32[]{:S(2)}, u32[]{:S(2)}) %collective-permute-start.4) | collective-permute-done | bytes 73760 | tf_op jit(solution)/shard_map/ppermute | solution.py:352
  101.5 4.7 %collective-permute-start.5 = (bf16[16,1152]{1,0:T(8,128)(2,1)S(1)}, bf16[16,1152]{1,0:T(8,128)(2,1)S(1)}, u32[]{:S(2)}, u32[]{:S(2)}) collective-permute-start(bf16[16,1152]{1,0:T(8,128)(2,1)S(1)} %get-tuple-element.35), channel_id=1, source_target_pairs={{0,128},{64,192},{128,0},{192,64},{1,129},{65,193},{129,1},{193,65... | collective-permute-start | bytes 110600 | tf_op jit(solution)/shard_map/ppermute | solution.py:359
  106.1 5.5 %collective-permute-done.5.got_ref = bf16[16,1152]{1,0:T(8,128)(2,1)S(1)} collective-permute-done((bf16[16,1152]{1,0:T(8,128)(2,1)S(1)}, bf16[16,1152]{1,0:T(8,128)(2,1)S(1)}, u32[]{:S(2)}, u32[]{:S(2)}) %collective-permute-start.5) | collective-permute-done | bytes 36896 | tf_op jit(solution)/shard_map/ppermute | solution.py:359
  111.6 0.0 copy-done.1
  111.6 0.8 shard_map.84
  112.5 5.2 %all-to-all-done.2.terms_ref = bf16[8,16,1280]{2,1,0:T(8,128)(2,1)S(1)} async-done(((bf16[8,16,1280]{2,1,0:T(8,128)(2,1)}), bf16[8,16,1280]{2,1,0:T(8,128)(2,1)S(1)}, u32[]{:S(2)}, u32[]{:S(2)}) %all-to-all-start.2) | async-done | bytes 327712 | tf_op jit(solution)/shard_map/all_to_all | solution.py:361
  117.7 0.8 shard_map.81
  (2 shorter events, 0.0 us)
Async XLA Ops:
  2.7 59.3 %all-to-all-start = ((bf16[32,16,1280]{2,1,0:T(8,128)(2,1)}), bf16[32,16,1280]{2,1,0:T(8,128)(2,1)S(1)}, u32[]{:S(2)}, u32[]{:S(2)}) async-start(bf16[32,16,1280]{2,1,0:T(8,128)(2,1)} %get-tuple-element.21), calls=%async_computation | async-start | bytes 2621440 | tf_op jit(solution)/shard_map/all_to_all | solution.py:279
  58.8 5.6 %collective-permute-start = (bf16[256,1280]{1,0:T(8,128)(2,1)S(1)}, bf16[256,1280]{1,0:T(8,128)(2,1)S(1)}, u32[]{:S(2)}, u32[]{:S(2)}) collective-permute-start(bf16[256,1280]{1,0:T(8,128)(2,1)S(1)} %all_gather.3.mine.mine_ref), channel_id=1, source_target_pairs={{0,32},{32,0},{1,33},{33,1},{2,34},{34,2},{3,35},{35,3},{4,36},{36... | collective-permute-start | bytes 1966088 | tf_op jit(solution)/shard_map/ppermute | solution.py:256
  67.9 9.5 %copy-start = (f32[256,1280]{1,0:T(8,128)S(1)}, f32[256,1280]{1,0:T(8,128)}, u32[]{:S(2)}) copy-start(f32[256,1280]{1,0:T(8,128)} %get-tuple-element.22.keep_ref) | copy-start | bytes 3932164
  67.9 22.2 %all-to-all-start.1 = ((bf16[32,16,1152]{2,1,0:T(8,128)(2,1)}), bf16[32,16,1152]{2,1,0:T(8,128)(2,1)S(1)}, u32[]{:S(2)}, u32[]{:S(2)}) async-start(bf16[32,16,1152]{2,1,0:T(8,128)(2,1)} %get-tuple-element.28), calls=%async_computation.1 | async-start | bytes 2359296 | tf_op jit(solution)/shard_map/all_to_all | solution.py:321
  73.2 4.2 %collective-permute-start.1 = (bf16[256,1280]{1,0:T(8,128)(2,1)}, bf16[256,1280]{1,0:T(8,128)(2,1)S(1)}, u32[]{:S(2)}, u32[]{:S(2)}) collective-permute-start(bf16[256,1280]{1,0:T(8,128)(2,1)} %get-tuple-element.24), channel_id=1, source_target_pairs={{0,32},{32,0},{1,33},{33,1},{2,34},{34,2},{3,35},{35,3},{4,36},{36... | collective-permute-start | bytes 1966088 | tf_op jit(solution)/shard_map/ppermute | solution.py:256
  77.6 8.2 %collective-permute-start.2 = (bf16[128,640]{1,0:T(8,128)(2,1)S(1)}, bf16[128,640]{1,0:T(8,128)(2,1)S(1)}, u32[]{:S(2)}, u32[]{:S(2)}) collective-permute-start(bf16[128,640]{1,0:T(8,128)(2,1)S(1)} %get-tuple-element.26), channel_id=1, source_target_pairs={{0,1},{1,0},{2,3},{3,2},{4,5},{5,4},{6,7},{7,6},{8,9},{9,8},{10,11... | collective-permute-start | bytes 491528 | tf_op jit(solution)/shard_map/ppermute | solution.py:332
  79.5 9.4 %collective-permute-start.3 = (bf16[128,640]{1,0:T(8,128)(2,1)S(1)}, bf16[128,640]{1,0:T(8,128)(2,1)S(1)}, u32[]{:S(2)}, u32[]{:S(2)}) collective-permute-start(bf16[128,640]{1,0:T(8,128)(2,1)S(1)} %get-tuple-element.27), channel_id=1, source_target_pairs={{0,15},{1,2},{2,1},{3,4},{4,3},{5,6},{6,5},{7,8},{8,7},{9,10},{10,... | collective-permute-start | bytes 491528 | tf_op jit(solution)/shard_map/ppermute | solution.py:333
  89.8 21.8 %copy-start.1 = (bf16[16,1152]{1,0:T(8,128)(2,1)S(1)}, bf16[16,1152]{1,0:T(8,128)(2,1)}, u32[]{:S(2)}) copy-start(bf16[16,1152]{1,0:T(8,128)(2,1)} %embed_ref.3) | copy-start | bytes 110596
  89.8 27.9 %copy-start.2 = (bf16[16,1152]{1,0:T(8,128)(2,1)S(1)}, bf16[16,1152]{1,0:T(8,128)(2,1)}, u32[]{:S(2)}) copy-start(bf16[16,1152]{1,0:T(8,128)(2,1)} %embed_ref.2) | copy-start | bytes 110596
  90.1 27.6 %all-to-all-start.2 = ((bf16[8,16,1280]{2,1,0:T(8,128)(2,1)}), bf16[8,16,1280]{2,1,0:T(8,128)(2,1)S(1)}, u32[]{:S(2)}, u32[]{:S(2)}) async-start(bf16[8,16,1280]{2,1,0:T(8,128)(2,1)} %shard_map.80), calls=%async_computation.2 | async-start | bytes 655360 | tf_op jit(solution)/shard_map/all_to_all | solution.py:361
  94.3 7.2 %collective-permute-start.4 = (bf16[2,16,1152]{2,1,0:T(8,128)(2,1)S(1)}, bf16[2,16,1152]{2,1,0:T(8,128)(2,1)S(1)}, u32[]{:S(2)}, u32[]{:S(2)}) collective-permute-start(bf16[2,16,1152]{2,1,0:T(8,128)(2,1)S(1)} %get-tuple-element.33), channel_id=1, source_target_pairs={{0,64},{64,0},{128,192},{192,128},{1,65},{65,1},{129,193},{193,129... | collective-permute-start | bytes 221192 | tf_op jit(solution)/shard_map/ppermute | solution.py:352
  101.5 10.2 %collective-permute-start.5 = (bf16[16,1152]{1,0:T(8,128)(2,1)S(1)}, bf16[16,1152]{1,0:T(8,128)(2,1)S(1)}, u32[]{:S(2)}, u32[]{:S(2)}) collective-permute-start(bf16[16,1152]{1,0:T(8,128)(2,1)S(1)} %get-tuple-element.35), channel_id=1, source_target_pairs={{0,128},{64,192},{128,0},{192,64},{1,129},{65,193},{129,1},{193,65... | collective-permute-start | bytes 110600 | tf_op jit(solution)/shard_map/ppermute | solution.py:359
